TPU v7x, 32 devices: a whole 2x2x4 slice. The times are simulated.
32 devices in a mesh: row: 4 (over y, core), col: 8 (over z, x).
Axes of the slice: x: 2, y: 2, z: 4, core: 2. Of those that a mesh axis runs over, the one named last changes fastest.
Arguments:
- activations: float32 [4096, 2048], P('row', 'col'), may hold values from -6 to 6
- cotangent: float32 [4096, 2048], P('row', 'col'), may hold values from -6 to 6
- lengths: int32 [4], P('row'), may hold values from 256 to 1024, as said below
- first_gain: float32 [2, 2048], P(None, 'col'), may hold values from 0.5 to 1.5
- first_shift: float32 [2, 2048], P(None, 'col'), may hold values from -1.75 to 1.75
- joined_weight: float32 [2, 2048, 6144], P(None, 'row', 'col'), may hold values from -0.125 to 0.125
- query_bias: float32 [2, 2048], P(None, 'col'), may hold values from -1.75 to 1.75
- value_bias: float32 [2, 2048], P(None, 'col'), may hold values from -1.75 to 1.75
- output_weight: float32 [2, 2048, 2048], P(None, 'col', 'row'), may hold values from -0.5 to 0.5
- output_bias: float32 [2, 2048], P(None, 'col'), may hold values from -1.75 to 1.75
- second_gain: float32 [2, 2048], P(None, 'col'), may hold values from 0.5 to 1.5
- second_shift: float32 [2, 2048], P(None, 'col'), may hold values from -1.75 to 1.75
- up_weight: float32 [2, 2048, 8192], P(None, 'row', 'col'), may hold values from -0.125 to 0.125
- up_bias: float32 [2, 8192], P(None, 'col'), may hold values from -1.75 to 1.75
- down_weight: float32 [2, 8192, 2048], P(None, 'col', 'row'), may hold values from -0.0625 to 0.0625
- down_bias: float32 [2, 2048], P(None, 'col'), may hold values from -1.75 to 1.75
Outputs:
- result: float32 [4096, 2048], P('row', 'col')
- input_grad: float32 [4096, 2048], P('row', 'col')
- first_gain_grad: float32 [2, 2048], P(None, 'col')
- first_shift_grad: float32 [2, 2048], P(None, 'col')
- joined_weight_grad: float32 [2, 2048, 6144], P(None, 'row', 'col')
- query_bias_grad: float32 [2, 2048], P(None, 'col')
- value_bias_grad: float32 [2, 2048], P(None, 'col')
- output_weight_grad: float32 [2, 2048, 2048], P(None, 'col', 'row')
- output_bias_grad: float32 [2, 2048], P(None, 'col')
- second_gain_grad: float32 [2, 2048], P(None, 'col')
- second_shift_grad: float32 [2, 2048], P(None, 'col')
- up_weight_grad: float32 [2, 2048, 8192], P(None, 'row', 'col')
- up_bias_grad: float32 [2, 8192], P(None, 'col')
- down_weight_grad: float32 [2, 8192, 2048], P(None, 'col', 'row')
- down_bias_grad: float32 [2, 2048], P(None, 'col')
Inputs may be any that keep to these rules, and one draw needn't show every extreme that they name: `lengths`: each slot's length lies between 256 and 1024; in every draw some slot is exactly 1024 long and some exactly 256.
All inputs are finite; a program needn't handle non-finite values.
Results may differ from a plain program's by a relative error of at most 0.015.
Values may be sent and summed in bfloat16 or wider, within the bound.
No kernel may reach another device: no remote copies, remote signals or barrier semaphores. Data moves between devices by JAX's collectives and lax.ppermute only.
A program may use at most 256 MiB of HBM per device.

v0:
```python
import math

import jax
import jax.numpy as jnp
from jax import lax
from jax.sharding import PartitionSpec as P

HEADS = 16
HEAD_DIM = 128


norm_eps = 1e-05
masked_score = -1e30


def gelu_tanh(value):
    return jax.nn.gelu(value, approximate=True)


def norm_forward(value, gain, shift):
    width = value.shape[1] * lax.axis_size("col")
    total, squares = lax.psum((jnp.sum(value, axis=1), jnp.sum(value * value, axis=1)), "col")
    mean = total / width
    inverse = lax.rsqrt(squares / width - mean * mean + norm_eps)
    centred = (value - mean[:, None]) * inverse[:, None]
    return (centred, inverse, centred * gain + shift)


def norm_backward(gradient, centred, inverse, gain):
    width = gradient.shape[1] * lax.axis_size("col")
    scaled = gradient * gain
    first_sum, second_sum = lax.psum(
        (jnp.sum(scaled, axis=1), jnp.sum(scaled * centred, axis=1)), "col"
    )
    passed = inverse[:, None] * (
        scaled - first_sum[:, None] / width - centred * second_sum[:, None] / width
    )
    return (passed, jnp.sum(gradient * centred, axis=0), jnp.sum(gradient, axis=0))


def gather_features(value):
    return lax.all_gather(value, "col", axis=1, tiled=True)


def regather_features(value):
    return lax.all_gather(value, "col", axis=1, tiled=True)


def gather_gradient(value):
    return lax.all_gather(value, "col", axis=1, tiled=True)


def column_sum(partial_term):
    return lax.psum_scatter(partial_term, "col", scatter_dimension=1, tiled=True)


def column_sum_back(partial_term):
    return lax.psum_scatter(partial_term, "col", scatter_dimension=1, tiled=True)


def cast_weights(joined_weight, output_weight, up_weight, down_weight, layer):
    return (
        joined_weight[layer].astype(jnp.bfloat16),
        output_weight[layer].astype(jnp.bfloat16),
        up_weight[layer].astype(jnp.bfloat16),
        down_weight[layer].astype(jnp.bfloat16),
    )


def gather_weights(rounded):
    return (
        lax.all_gather(rounded[0], "row", axis=0, tiled=True),
        lax.all_gather(rounded[1], "row", axis=1, tiled=True),
        lax.all_gather(rounded[2], "row", axis=0, tiled=True),
        lax.all_gather(rounded[3], "row", axis=1, tiled=True),
    )


def regather_weights(rounded):
    return (
        lax.all_gather(rounded[0], "row", axis=0, tiled=True),
        lax.all_gather(rounded[1], "row", axis=1, tiled=True),
        lax.all_gather(rounded[2], "row", axis=0, tiled=True),
        lax.all_gather(rounded[3], "row", axis=1, tiled=True),
    )


def slot_scores(query, key, lengths, slopes):
    slot_count = lengths.shape[0]
    span = query.shape[0] // slot_count
    heads = query.shape[1]
    depth = query.shape[2]
    query_slots = query.reshape(slot_count, span, heads, depth)
    key_slots = key.reshape(slot_count, span, heads, depth)
    position = jnp.arange(span)
    distance = (position[:, None] - position[None, :]).astype(jnp.float32)
    allowed = (position[None, None, :] <= position[None, :, None]) & (
        position[None, None, :] < lengths[:, None, None]
    )
    scores = jnp.einsum(
        "sqhd,skhd->shqk", query_slots, key_slots, preferred_element_type=jnp.float32
    ) * (1.0 / math.sqrt(depth))
    scores = scores - slopes[None, :, None, None] * distance[None, None]
    return jnp.where(allowed[:, None], scores, masked_score)


def attention_forward(query, key, value, lengths, slopes):
    tokens, heads, depth = query.shape
    slot_count = lengths.shape[0]
    scores = slot_scores(query, key, lengths, slopes)
    highest_score = jnp.max(scores, axis=-1, keepdims=True)
    raised = jnp.exp(scores - highest_score)
    total = jnp.sum(raised, axis=-1, keepdims=True)
    chances = raised / total
    log_total = highest_score[..., 0] + jnp.log(total[..., 0])
    value_slots = value.reshape(slot_count, tokens // slot_count, heads, depth)
    context = jnp.einsum(
        "shqk,skhd->sqhd",
        chances.astype(jnp.bfloat16),
        value_slots,
        preferred_element_type=jnp.float32,
    )
    return (context.reshape(tokens, heads * depth), log_total)


def attention_backward(query, key, value, log_total, context_grad, lengths, slopes):
    tokens, heads, depth = query.shape
    slot_count = lengths.shape[0]
    span = tokens // slot_count
    scores = slot_scores(query, key, lengths, slopes)
    chances = jnp.exp(scores - log_total[..., None])
    output_slots = context_grad.reshape(slot_count, span, heads, depth)
    value_slots = value.reshape(slot_count, span, heads, depth)
    query_slots = query.reshape(slot_count, span, heads, depth)
    key_slots = key.reshape(slot_count, span, heads, depth)
    value_grad = jnp.einsum(
        "shqk,sqhd->skhd",
        chances.astype(jnp.bfloat16),
        output_slots,
        preferred_element_type=jnp.float32,
    )
    chance_grad = jnp.einsum(
        "sqhd,skhd->shqk", output_slots, value_slots, preferred_element_type=jnp.float32
    )
    row_dot = jnp.sum(chances * chance_grad, axis=-1, keepdims=True)
    score_grad = (chances * (chance_grad - row_dot)).astype(jnp.bfloat16)
    factor = 1.0 / math.sqrt(depth)
    query_grad = (
        jnp.einsum("shqk,skhd->sqhd", score_grad, key_slots, preferred_element_type=jnp.float32)
        * factor
    )
    key_grad = (
        jnp.einsum("shqk,sqhd->skhd", score_grad, query_slots, preferred_element_type=jnp.float32)
        * factor
    )
    return (
        query_grad.reshape(tokens, heads, depth).astype(jnp.bfloat16),
        key_grad.reshape(tokens, heads, depth).astype(jnp.bfloat16),
        value_grad.reshape(tokens, heads, depth).astype(jnp.bfloat16),
    )


def stack_layers(items, index):
    return jnp.stack([entry[index] for entry in items])


def on_device(
    activations,
    cotangent,
    lengths,
    first_gain,
    first_shift,
    joined_weight,
    query_bias,
    value_bias,
    output_weight,
    output_bias,
    second_gain,
    second_shift,
    up_weight,
    up_bias,
    down_weight,
    down_bias,
):
    tokens, local_width = activations.shape
    heads_local = local_width // HEAD_DIM
    layers = first_gain.shape[0]
    head_index = lax.axis_index("col") * heads_local + jnp.arange(heads_local)
    slopes = jnp.exp2(-8.0 * (head_index + 1).astype(jnp.float32) / HEADS)
    slot_count = lengths.shape[0]
    span = tokens // slot_count
    valid = (jnp.arange(span)[None, :] < lengths[:, None]).reshape(tokens, 1)
    residual = activations
    saved = []
    for layer in range(layers):
        weights = gather_weights(
            cast_weights(joined_weight, output_weight, up_weight, down_weight, layer)
        )
        centred_one, inverse_one, normed_one = norm_forward(
            residual, first_gain[layer], first_shift[layer]
        )
        gathered_one = gather_features(normed_one.astype(jnp.bfloat16))
        joined = jnp.dot(gathered_one, weights[0], preferred_element_type=jnp.float32).reshape(
            tokens, heads_local, 3, HEAD_DIM
        )
        query = (joined[:, :, 0] + query_bias[layer].reshape(heads_local, HEAD_DIM)).astype(
            jnp.bfloat16
        )
        key = joined[:, :, 1].astype(jnp.bfloat16)
        value = (joined[:, :, 2] + value_bias[layer].reshape(heads_local, HEAD_DIM)).astype(
            jnp.bfloat16
        )
        context, log_total = attention_forward(query, key, value, lengths, slopes)
        context = context.astype(jnp.bfloat16)
        middle = (
            residual
            + column_sum(jnp.dot(context, weights[1], preferred_element_type=jnp.float32))
            + output_bias[layer]
        )
        centred_two, inverse_two, normed_two = norm_forward(
            middle, second_gain[layer], second_shift[layer]
        )
        gathered_two = gather_features(normed_two.astype(jnp.bfloat16))
        upper = (
            jnp.dot(gathered_two, weights[2], preferred_element_type=jnp.float32) + up_bias[layer]
        )
        activated = gelu_tanh(upper).astype(jnp.bfloat16)
        residual = (
            middle
            + column_sum(jnp.dot(activated, weights[3], preferred_element_type=jnp.float32))
            + down_bias[layer]
        )
        kept = None
        saved.append(
            (
                centred_one,
                inverse_one,
                query,
                key,
                value,
                log_total,
                context,
                centred_two,
                inverse_two,
                upper,
                activated,
                kept,
            )
        )
    gradient = cotangent * valid
    weight_terms = [None] * layers
    small_terms = [None] * layers
    for layer in reversed(range(layers)):
        (
            centred_one,
            inverse_one,
            query,
            key,
            value,
            log_total,
            context,
            centred_two,
            inverse_two,
            upper,
            activated,
            kept,
        ) = saved[layer]
        weights = regather_weights(
            cast_weights(joined_weight, output_weight, up_weight, down_weight, layer)
        )
        gathered_one = regather_features(
            (centred_one * first_gain[layer] + first_shift[layer]).astype(jnp.bfloat16)
        )
        gathered_two = regather_features(
            (centred_two * second_gain[layer] + second_shift[layer]).astype(jnp.bfloat16)
        )
        down_bias_term = jnp.sum(gradient, axis=0)
        low_gradient = gather_gradient(gradient.astype(jnp.bfloat16))
        hidden_grad = jnp.einsum(
            "td,fd->tf", low_gradient, weights[3], preferred_element_type=jnp.float32
        )
        down_term = jnp.einsum(
            "tf,td->fd", activated, low_gradient, preferred_element_type=jnp.float32
        )
        upper_grad = jax.vjp(gelu_tanh, upper)[1](hidden_grad)[0].astype(jnp.bfloat16)
        up_bias_term = jnp.sum(upper_grad.astype(jnp.float32), axis=0)
        up_term = jnp.einsum(
            "td,tf->df", gathered_two, upper_grad, preferred_element_type=jnp.float32
        )
        normed_two_grad = column_sum_back(
            jnp.einsum("tf,df->td", upper_grad, weights[2], preferred_element_type=jnp.float32)
        )
        passed_two, gain_two_term, shift_two_term = norm_backward(
            normed_two_grad, centred_two, inverse_two, second_gain[layer]
        )
        middle_grad = gradient + passed_two
        output_bias_term = jnp.sum(middle_grad, axis=0)
        low_middle = gather_gradient(middle_grad.astype(jnp.bfloat16))
        context_grad = jnp.einsum(
            "td,cd->tc", low_middle, weights[1], preferred_element_type=jnp.float32
        ).astype(jnp.bfloat16)
        output_term = jnp.einsum(
            "tc,td->cd", context, low_middle, preferred_element_type=jnp.float32
        )
        query_grad, key_grad, value_grad = attention_backward(
            query, key, value, log_total, context_grad, lengths, slopes
        )
        joined_grad = jnp.stack((query_grad, key_grad, value_grad), axis=2).reshape(
            tokens, 3 * local_width
        )
        query_bias_term = jnp.sum(query_grad.astype(jnp.float32), axis=0).reshape(local_width)
        value_bias_term = jnp.sum(value_grad.astype(jnp.float32), axis=0).reshape(local_width)
        joined_term = jnp.einsum(
            "td,tc->dc", gathered_one, joined_grad, preferred_element_type=jnp.float32
        )
        normed_one_grad = column_sum_back(
            jnp.einsum("tc,dc->td", joined_grad, weights[0], preferred_element_type=jnp.float32)
        )
        passed_one, gain_one_term, shift_one_term = norm_backward(
            normed_one_grad, centred_one, inverse_one, first_gain[layer]
        )
        gradient = middle_grad + passed_one
        small_terms[layer] = (
            gain_one_term,
            shift_one_term,
            query_bias_term,
            value_bias_term,
            output_bias_term,
            gain_two_term,
            shift_two_term,
            up_bias_term,
            down_bias_term,
        )
        weight_terms[layer] = (
            lax.psum_scatter(
                joined_term.astype(jnp.bfloat16), "row", scatter_dimension=0, tiled=True
            ).astype(jnp.float32),
            lax.psum_scatter(
                output_term.astype(jnp.bfloat16), "row", scatter_dimension=1, tiled=True
            ).astype(jnp.float32),
            lax.psum_scatter(
                up_term.astype(jnp.bfloat16), "row", scatter_dimension=0, tiled=True
            ).astype(jnp.float32),
            lax.psum_scatter(
                down_term.astype(jnp.bfloat16), "row", scatter_dimension=1, tiled=True
            ).astype(jnp.float32),
        )
    joined_all = stack_layers(weight_terms, 0)
    output_all = stack_layers(weight_terms, 1)
    up_all = stack_layers(weight_terms, 2)
    down_all = stack_layers(weight_terms, 3)
    small_sums = lax.psum(
        (
            stack_layers(small_terms, 0),
            stack_layers(small_terms, 1),
            stack_layers(small_terms, 2),
            stack_layers(small_terms, 3),
            stack_layers(small_terms, 4),
            stack_layers(small_terms, 5),
            stack_layers(small_terms, 6),
            stack_layers(small_terms, 7),
            stack_layers(small_terms, 8),
        ),
        "row",
    )
    return (
        residual,
        gradient,
        small_sums[0],
        small_sums[1],
        joined_all,
        small_sums[2],
        small_sums[3],
        output_all,
        small_sums[4],
        small_sums[5],
        small_sums[6],
        up_all,
        small_sums[7],
        down_all,
        small_sums[8],
    )


def solution(mesh):
    return jax.shard_map(
        on_device,
        mesh=mesh,
        in_specs=(
            P("row", "col"),
            P("row", "col"),
            P("row"),
            P(None, "col"),
            P(None, "col"),
            P(None, "row", "col"),
            P(None, "col"),
            P(None, "col"),
            P(None, "col", "row"),
            P(None, "col"),
            P(None, "col"),
            P(None, "col"),
            P(None, "row", "col"),
            P(None, "col"),
            P(None, "col", "row"),
            P(None, "col"),
        ),
        out_specs=(
            P("row", "col"),
            P("row", "col"),
            P(None, "col"),
            P(None, "col"),
            P(None, "row", "col"),
            P(None, "col"),
            P(None, "col"),
            P(None, "col", "row"),
            P(None, "col"),
            P(None, "col"),
            P(None, "col"),
            P(None, "row", "col"),
            P(None, "col"),
            P(None, "col", "row"),
            P(None, "col"),
        ),
        check_vma=False,
    )
```

profile of v0, /device:TPU:1, one launch (start us, length us, event | category | flops | bytes accessed | tf_op | source)
XLA Modules:
  0.0 2566.9 jit_solution(14317949054706198857)
XLA Ops:
  11.1 19.0 all-reduce.7
  36.7 5.2 all-gather.41.cloned.1.call-done
  41.8 76.8 %all-gather.25.cloned.1.call-done = bf16[1024,2048]{1,0:T(8,128)(2,1)} async-done(((bf16[1024,256]{1,0:T(8,128)(2,1)}), bf16[1024,2048]{1,0:T(8,128)(2,1)}) %all-gather.25.cloned.1.call-update) | async-done | bytes 4194320 | tf_op jit(solution)/shard_map/all_gather | solution.py:42
  118.7 6.2 fusion.51
  130.6 4.8 fusion.122
  140.5 5.9 fusion.80
  150.8 144.0 %reduce-scatter.17.cloned.1.call-done = f32[1024,256]{1,0:T(8,128)} async-done(((f32[1024,2048]{1,0:T(8,128)}), f32[1024,256]{1,0:T(8,128)}) %reduce-scatter.17.cloned.1.call-update) | async-done | bytes 1048592 | tf_op jit(solution)/shard_map/reduce_scatter | solution.py:54
  296.4 16.2 all-reduce.6
  317.9 12.8 all-gather.45.cloned.1.call-done
  330.7 76.3 %all-gather.27.cloned.1.call-done = bf16[1024,2048]{1,0:T(8,128)(2,1)} async-done(((bf16[1024,256]{1,0:T(8,128)(2,1)}), bf16[1024,2048]{1,0:T(8,128)(2,1)}) %all-gather.27.cloned.1.call-update) | async-done | bytes 4194320 | tf_op jit(solution)/shard_map/all_gather | solution.py:42
  407.1 10.0 fusion.38
  417.0 25.8 %all-gather.47.cloned.1.call-done = bf16[1,1024,2048]{2,1,0:T(8,128)(2,1)} async-done(((bf16[1,1024,512]{2,1,0:T(8,128)(2,1)}), bf16[1,1024,2048]{2,1,0:T(8,128)(2,1)}) %all-gather.47.cloned.1.call-update) | async-done | bytes 4194320 | tf_op jit(solution)/shard_map/all_gather | solution.py:75
  442.8 11.6 fusion.34
  455.3 148.4 %reduce-scatter.19.cloned.1.call-done = f32[1024,256]{1,0:T(8,128)} async-done(((f32[1024,2048]{1,0:T(8,128)}), f32[1024,256]{1,0:T(8,128)}) %reduce-scatter.19.cloned.1.call-update) | async-done | bytes 1048592 | tf_op jit(solution)/shard_map/reduce_scatter | solution.py:54
  605.2 16.2 all-reduce.5
  623.6 9.6 all-gather.49.cloned.1.call-done
  633.2 76.7 %all-gather.29.cloned.1.call-done = bf16[1024,2048]{1,0:T(8,128)(2,1)} async-done(((bf16[1024,256]{1,0:T(8,128)(2,1)}), bf16[1024,2048]{1,0:T(8,128)(2,1)}) %all-gather.29.cloned.1.call-update) | async-done | bytes 4194320 | tf_op jit(solution)/shard_map/all_gather | solution.py:42
  709.8 6.2 fusion.47
  723.6 5.0 fusion.123
  733.6 5.9 fusion.76
  740.3 147.4 %reduce-scatter.21.cloned.1.call-done = f32[1024,256]{1,0:T(8,128)} async-done(((f32[1024,2048]{1,0:T(8,128)}), f32[1024,256]{1,0:T(8,128)}) %reduce-scatter.21.cloned.1.call-update) | async-done | bytes 1048592 | tf_op jit(solution)/shard_map/reduce_scatter | solution.py:54
  889.4 16.1 all-reduce.4
  910.1 13.2 all-gather.53.cloned.1.call-done
  923.3 76.9 %all-gather.31.cloned.1.call-done = bf16[1024,2048]{1,0:T(8,128)(2,1)} async-done(((bf16[1024,256]{1,0:T(8,128)(2,1)}), bf16[1024,2048]{1,0:T(8,128)(2,1)}) %all-gather.31.cloned.1.call-update) | async-done | bytes 4194320 | tf_op jit(solution)/shard_map/all_gather | solution.py:42
  1000.2 10.0 fusion.30
  1010.1 25.6 all-gather.55.cloned.1.call-done
  1035.8 76.3 %all-gather.33.cloned.1.call-done = bf16[1024,2048]{1,0:T(8,128)(2,1)} async-done(((bf16[1024,256]{1,0:T(8,128)(2,1)}), bf16[1024,2048]{1,0:T(8,128)(2,1)}) %all-gather.33.cloned.1.call-update) | async-done | bytes 4194320 | tf_op jit(solution)/shard_map/all_gather | solution.py:50
  1112.1 12.3 convert_reduce_fusion
  1125.7 6.8 fusion.28
  1132.7 11.7 fusion.26
  1144.4 136.3 %reduce-scatter.25.cloned.1.call-done = f32[1024,256]{1,0:T(8,128)} async-done(((f32[1024,2048]{1,0:T(8,128)}), f32[1024,256]{1,0:T(8,128)}) %reduce-scatter.25.cloned.1.call-update) | async-done | bytes 1048592 | tf_op jit(solution)/shard_map/reduce_scatter | solution.py:58
  1283.2 16.6 all-reduce.3
  1299.8 133.1 %reduce-scatter.23.cloned.1.call-done = f32[1024,256]{1,0:T(8,128)} async-done(((f32[1024,2048]{1,0:T(8,128)}), f32[1024,256]{1,0:T(8,128)}) %reduce-scatter.23.cloned.1.call-update) | async-done | bytes 1048592 | tf_op jit(solution)/shard_map/reduce_scatter | solution.py:54
  1437.9 73.6 %all-gather.35.cloned.1.call-done = bf16[1024,2048]{1,0:T(8,128)(2,1)} async-done(((bf16[1024,256]{1,0:T(8,128)(2,1)}), bf16[1024,2048]{1,0:T(8,128)(2,1)}) %all-gather.35.cloned.1.call-update) | async-done | bytes 4194320 | tf_op jit(solution)/shard_map/all_gather | solution.py:50
  1515.3 5.3 multiply_reduce_fusion.1
  1531.4 5.7 fusion.45
  1537.2 148.2 %reduce-scatter.27.cloned.1.call-done = f32[1024,256]{1,0:T(8,128)} async-done(((f32[1024,2048]{1,0:T(8,128)}), f32[1024,256]{1,0:T(8,128)}) %reduce-scatter.27.cloned.1.call-update) | async-done | bytes 1048592 | tf_op jit(solution)/shard_map/reduce_scatter | solution.py:58
  1687.2 16.1 all-reduce.2
  1707.4 75.2 %all-gather.37.cloned.1.call-done = bf16[1024,2048]{1,0:T(8,128)(2,1)} async-done(((bf16[1024,256]{1,0:T(8,128)(2,1)}), bf16[1024,2048]{1,0:T(8,128)(2,1)}) %all-gather.37.cloned.1.call-update) | async-done | bytes 4194320 | tf_op jit(solution)/shard_map/all_gather | solution.py:50
  1782.6 11.7 convert_reduce_fusion.1
  1794.4 6.7 fusion.36
  1801.2 148.2 %reduce-scatter.29.cloned.1.call-done = f32[1024,256]{1,0:T(8,128)} async-done(((f32[1024,2048]{1,0:T(8,128)}), f32[1024,256]{1,0:T(8,128)}) %reduce-scatter.29.cloned.1.call-update) | async-done | bytes 1048592 | tf_op jit(solution)/shard_map/reduce_scatter | solution.py:58
  1951.3 16.2 all-reduce.1
  1970.7 10.7 convolution_convert_fusion
  1981.5 10.7 convolution_convert_fusion.1
  1992.4 9.5 convolution_convert_fusion.2
  2002.0 9.4 convolution_convert_fusion.3
  2012.4 4.4 convolution_convert_fusion.6
  2016.9 28.8 %all-gather.39.cloned.1.call-done = bf16[1024,2048]{1,0:T(8,128)(2,1)} async-done(((bf16[1024,256]{1,0:T(8,128)(2,1)}), bf16[1024,2048]{1,0:T(8,128)(2,1)}) %all-gather.39.cloned.1.call-update) | async-done | bytes 4194320 | tf_op jit(solution)/shard_map/all_gather | solution.py:50
  2045.8 4.4 convolution_convert_fusion.7
  2050.5 8.4 convolution_convert_fusion.4
  2062.7 5.4 multiply_reduce_fusion
  2079.8 4.9 convolution_convert_fusion.5
  2085.0 9.2 fusion.49
  2094.9 44.2 %reduce-scatter.45.cloned.1.call-done = bf16[1024,512]{1,0:T(8,128)(2,1)} async-done(((bf16[1024,2048]{1,0:T(8,128)(2,1)}), bf16[1024,512]{1,0:T(8,128)(2,1)}) %reduce-scatter.45.cloned.1.call-update) | async-done | bytes 1048592 | tf_op jit(solution)/shard_map/reduce_scatter | solution.py:344
  2142.9 43.8 %reduce-scatter.43.cloned.1.call-done = bf16[512,1024]{1,0:T(8,128)(2,1)} async-done(((bf16[2048,1024]{1,0:T(8,128)(2,1)}), bf16[512,1024]{1,0:T(8,128)(2,1)}) %reduce-scatter.43.cloned.1.call-update) | async-done | bytes 1048592 | tf_op jit(solution)/shard_map/reduce_scatter | solution.py:341
  2186.8 46.9 %reduce-scatter.41.cloned.1.call-done = bf16[512,1024]{1,0:T(8,128)(2,1)} async-done(((bf16[2048,1024]{1,0:T(8,128)(2,1)}), bf16[512,1024]{1,0:T(8,128)(2,1)}) %reduce-scatter.41.cloned.1.call-update) | async-done | bytes 1048592 | tf_op jit(solution)/shard_map/reduce_scatter | solution.py:341
  2237.6 24.2 reduce-scatter.39.cloned.1.call-done
  2261.8 27.5 %reduce-scatter.37.cloned.1.call-done = bf16[256,512]{1,0:T(8,128)(2,1)} async-done(((bf16[256,2048]{1,0:T(8,128)(2,1)}), bf16[256,512]{1,0:T(8,128)(2,1)}) %reduce-scatter.37.cloned.1.call-update) | async-done | bytes 262160 | tf_op jit(solution)/shard_map/reduce_scatter | solution.py:338
  2291.4 38.5 %reduce-scatter.35.cloned.1.call-done = bf16[512,768]{1,0:T(8,128)(2,1)} async-done(((bf16[2048,768]{1,0:T(8,128)(2,1)}), bf16[512,768]{1,0:T(8,128)(2,1)}) %reduce-scatter.35.cloned.1.call-update) | async-done | bytes 786448 | tf_op jit(solution)/shard_map/reduce_scatter | solution.py:335
  2329.8 41.1 %reduce-scatter.33.cloned.1.call-done = bf16[512,768]{1,0:T(8,128)(2,1)} async-done(((bf16[2048,768]{1,0:T(8,128)(2,1)}), bf16[512,768]{1,0:T(8,128)(2,1)}) %reduce-scatter.33.cloned.1.call-update) | async-done | bytes 786448 | tf_op jit(solution)/shard_map/reduce_scatter | solution.py:335
  2374.2 150.4 %reduce-scatter.31.cloned.1.call-done = f32[1024,256]{1,0:T(8,128)} async-done(((f32[1024,2048]{1,0:T(8,128)}), f32[1024,256]{1,0:T(8,128)}) %reduce-scatter.31.cloned.1.call-update) | async-done | bytes 1048592 | tf_op jit(solution)/shard_map/reduce_scatter | solution.py:58
  2526.4 16.1 all-reduce
  2542.6 14.6 all-reduce.8
  (290 shorter events, 125.4 us)
Async XLA Ops:
  7.2 22.9 copy-start.49
  7.2 22.9 copy-start.50
  7.2 34.6 %all-gather.41.cloned.1.call-start = ((), (), s32[]{:S(2)}) async-start(), calls=%async_computation.40 | async-start | bytes 3932160 | tf_op jit(solution)/shard_map/all_gather | solution.py:72
  9.4 22.6 copy-start.20
  10.7 108.0 %all-gather.25.cloned.1.call-start = ((), (), s32[]{:S(2)}) async-start(), calls=%async_computation.16 | async-start | bytes 4718592 | tf_op jit(solution)/shard_map/all_gather | solution.py:42
  31.9 108.6 %all-gather.43.cloned.1.call-start = ((), (), s32[]{:S(2)}) async-start(), calls=%async_computation.41 | async-start | bytes 1310720 | tf_op jit(solution)/shard_map/all_gather | solution.py:73
  32.9 261.9 %reduce-scatter.17.cloned.1.call-start = ((), (), s32[]{:S(2)}) async-start(), calls=%async_computation.17 | async-start | bytes 9437184 | tf_op jit(solution)/shard_map/reduce_scatter | solution.py:54
  36.6 94.0 %copy-start.41 = (f32[1,256]{1,0:T(1,128)}, f32[1,256]{1,0:T(1,128)S(1)}, u32[]{:S(2)}) copy-start(f32[1,256]{1,0:T(1,128)S(1)} %get-tuple-element.102) | copy-start | bytes 3076
  36.7 100.0 %copy-start.43 = (f32[1,256]{1,0:T(1,128)}, f32[1,256]{1,0:T(1,128)S(1)}, u32[]{:S(2)}) copy-start(f32[1,256]{1,0:T(1,128)S(1)} %get-tuple-element.100) | copy-start | bytes 3076
  127.9 7.5 copy-start.8
  140.4 5.9 copy-start.21
  146.4 184.3 %all-gather.45.cloned.1.call-start = ((), (), s32[]{:S(2)}) async-start(), calls=%async_computation.42 | async-start | bytes 5242880 | tf_op jit(solution)/shard_map/all_gather | solution.py:74
  150.5 256.5 %all-gather.27.cloned.1.call-start = ((), (), s32[]{:S(2)}) async-start(), calls=%async_computation.18 | async-start | bytes 4718592 | tf_op jit(solution)/shard_map/all_gather | solution.py:42
  150.8 165.5 %copy-start.39 = (f32[1,256]{1,0:T(1,128)}, f32[1,256]{1,0:T(1,128)S(1)}, u32[]{:S(2)}) copy-start(f32[1,256]{1,0:T(1,128)S(1)} %get-tuple-element.96) | copy-start | bytes 3076
  313.8 129.0 %all-gather.47.cloned.1.call-start = ((), (), s32[]{:S(2)}) async-start(), calls=%async_computation.43 | async-start | bytes 5242880 | tf_op jit(solution)/shard_map/all_gather | solution.py:75
  317.9 285.8 %reduce-scatter.19.cloned.1.call-start = ((), (), s32[]{:S(2)}) async-start(), calls=%async_computation.19 | async-start | bytes 9437184 | tf_op jit(solution)/shard_map/reduce_scatter | solution.py:54
  454.5 178.7 %all-gather.49.cloned.1.call-start = ((), (), s32[]{:S(2)}) async-start(), calls=%async_computation.44 | async-start | bytes 3932160 | tf_op jit(solution)/shard_map/all_gather | solution.py:72
  455.2 254.6 %all-gather.29.cloned.1.call-start = ((), (), s32[]{:S(2)}) async-start(), calls=%async_computation.20 | async-start | bytes 4718592 | tf_op jit(solution)/shard_map/all_gather | solution.py:42
  622.6 110.9 %all-gather.51.cloned.1.call-start = ((), (), s32[]{:S(2)}) async-start(), calls=%async_computation.45 | async-start | bytes 1310720 | tf_op jit(solution)/shard_map/all_gather | solution.py:73
  623.3 264.4 %reduce-scatter.21.cloned.1.call-start = ((), (), s32[]{:S(2)}) async-start(), calls=%async_computation.21 | async-start | bytes 9437184 | tf_op jit(solution)/shard_map/reduce_scatter | solution.py:54
  733.5 6.0 copy-start.23
  739.5 183.7 %all-gather.53.cloned.1.call-start = ((), (), s32[]{:S(2)}) async-start(), calls=%async_computation.46 | async-start | bytes 5242880 | tf_op jit(solution)/shard_map/all_gather | solution.py:74
  740.3 259.9 %all-gather.31.cloned.1.call-start = ((), (), s32[]{:S(2)}) async-start(), calls=%async_computation.22 | async-start | bytes 4718592 | tf_op jit(solution)/shard_map/all_gather | solution.py:42
  906.7 129.1 %all-gather.55.cloned.1.call-start = ((), (), s32[]{:S(2)}) async-start(), calls=%async_computation.47 | async-start | bytes 5242880 | tf_op jit(solution)/shard_map/all_gather | solution.py:75
  907.3 204.8 %all-gather.33.cloned.1.call-start = ((), (), s32[]{:S(2)}) async-start(), calls=%async_computation.24 | async-start | bytes 4718592 | tf_op jit(solution)/shard_map/all_gather | solution.py:50
  909.6 371.1 %reduce-scatter.25.cloned.1.call-start = ((), (), s32[]{:S(2)}) async-start(), calls=%async_computation.25 | async-start | bytes 9437184 | tf_op jit(solution)/shard_map/reduce_scatter | solution.py:58
  1112.1 13.6 copy-start.59
  1132.5 300.5 %reduce-scatter.23.cloned.1.call-start = ((), (), s32[]{:S(2)}) async-start(), calls=%async_computation.23 | async-start | bytes 9437184 | tf_op jit(solution)/shard_map/reduce_scatter | solution.py:54
  1144.4 367.1 %all-gather.35.cloned.1.call-start = ((), (), s32[]{:S(2)}) async-start(), calls=%async_computation.26 | async-start | bytes 4718592 | tf_op jit(solution)/shard_map/all_gather | solution.py:50
  1437.8 77.5 %copy-start.16 = (f32[1024,2,1,128]{3,0,1,2:T(8,128)S(1)}, f32[1024,2,1,128]{3,0,1,2:T(8,128)}, u32[]{:S(2)}) copy-start(f32[1024,2,1,128]{3,0,1,2:T(8,128)} %copy.97) | copy-start | bytes 3145732
  1437.8 247.5 %reduce-scatter.27.cloned.1.call-start = ((), (), s32[]{:S(2)}) async-start(), calls=%async_computation.27 | async-start | bytes 9437184 | tf_op jit(solution)/shard_map/reduce_scatter | solution.py:58
  1515.3 5.3 slice-start.2
  1515.3 5.8 slice-start.3
  1537.1 166.3 %copy-start.5 = (f32[1024,256]{1,0:T(8,128)S(1)}, f32[1024,256]{1,0:T(8,128)}, u32[]{:S(2)}) copy-start(f32[1024,256]{1,0:T(8,128)} %copy-done.4) | copy-start | bytes 3145732
  1537.1 245.5 %all-gather.37.cloned.1.call-start = ((), (), s32[]{:S(2)}) async-start(), calls=%async_computation.28 | async-start | bytes 4718592 | tf_op jit(solution)/shard_map/all_gather | solution.py:50
  1707.2 242.3 %reduce-scatter.29.cloned.1.call-start = ((), (), s32[]{:S(2)}) async-start(), calls=%async_computation.29 | async-start | bytes 9437184 | tf_op jit(solution)/shard_map/reduce_scatter | solution.py:58
  1782.6 11.7 copy-start.58
  1794.4 6.8 copy-start.62
  1801.1 148.3 %copy-start.32 = (f32[1024]{0:T(1024)S(1)}, f32[1024]{0:T(1024)}, u32[]{:S(2)}) copy-start(f32[1024]{0:T(1024)} %copy-done.31) | copy-start | bytes 12292
  1801.1 148.3 %copy-start.34 = (f32[1024]{0:T(1024)S(1)}, f32[1024]{0:T(1024)}, u32[]{:S(2)}) copy-start(f32[1024]{0:T(1024)} %copy-done.33) | copy-start | bytes 12292
  1801.1 148.3 %copy-start.40 = (f32[1,256]{1,0:T(1,128)S(1)}, f32[1,256]{1,0:T(1,128)}, u32[]{:S(2)}) copy-start(f32[1,256]{1,0:T(1,128)} %copy-done.39) | copy-start | bytes 3076
  1801.1 166.3 %copy-start.7 = (f32[1024,256]{1,0:T(8,128)S(1)}, f32[1024,256]{1,0:T(8,128)}, u32[]{:S(2)}) copy-start(f32[1024,256]{1,0:T(8,128)} %copy-done.6) | copy-start | bytes 3145732
  1801.2 244.6 %all-gather.39.cloned.1.call-start = ((), (), s32[]{:S(2)}) async-start(), calls=%async_computation.30 | async-start | bytes 4718592 | tf_op jit(solution)/shard_map/all_gather | solution.py:50
  1970.3 124.6 %reduce-scatter.47.cloned.1.call-start = ((), (), s32[]{:S(2)}) async-start(), calls=%async_computation.39 | async-start | bytes 5242880 | tf_op jit(solution)/shard_map/reduce_scatter | solution.py:344
  1981.4 157.7 %reduce-scatter.45.cloned.1.call-start = ((), (), s32[]{:S(2)}) async-start(), calls=%async_computation.38 | async-start | bytes 5242880 | tf_op jit(solution)/shard_map/reduce_scatter | solution.py:344
  1992.2 194.5 %reduce-scatter.43.cloned.1.call-start = ((), (), s32[]{:S(2)}) async-start(), calls=%async_computation.37 | async-start | bytes 5242880 | tf_op jit(solution)/shard_map/reduce_scatter | solution.py:341
  2001.9 231.8 %reduce-scatter.41.cloned.1.call-start = ((), (), s32[]{:S(2)}) async-start(), calls=%async_computation.36 | async-start | bytes 5242880 | tf_op jit(solution)/shard_map/reduce_scatter | solution.py:341
  2011.4 34.3 %copy-start.22 = (bf16[2,128,1024]{2,1,0:T(8,128)(2,1)S(1)}, bf16[2,128,1024]{2,1,0:T(8,128)(2,1)}, u32[]{:S(2)}) copy-start(bf16[2,128,1024]{2,1,0:T(8,128)(2,1)} %copy-done.21) | copy-start | bytes 1572868
  2011.4 250.4 %reduce-scatter.39.cloned.1.call-start = ((), (), s32[]{:S(2)}) async-start(), calls=%async_computation.35 | async-start | bytes 1310720 | tf_op jit(solution)/shard_map/reduce_scatter | solution.py:338
  2016.9 272.4 %reduce-scatter.37.cloned.1.call-start = ((), (), s32[]{:S(2)}) async-start(), calls=%async_computation.34 | async-start | bytes 1310720 | tf_op jit(solution)/shard_map/reduce_scatter | solution.py:338
  2050.2 8.8 copy-start.26
  2050.2 8.8 copy-start.36
  2050.2 8.9 copy-start.19
  2050.2 279.6 %reduce-scatter.35.cloned.1.call-start = ((), (), s32[]{:S(2)}) async-start(), calls=%async_computation.33 | async-start | bytes 3932160 | tf_op jit(solution)/shard_map/reduce_scatter | solution.py:335
  2059.0 312.0 %reduce-scatter.33.cloned.1.call-start = ((), (), s32[]{:S(2)}) async-start(), calls=%async_computation.32 | async-start | bytes 3932160 | tf_op jit(solution)/shard_map/reduce_scatter | solution.py:335
  2062.6 5.5 slice-start
  2062.6 6.5 slice-start.1
  2084.7 439.8 %reduce-scatter.31.cloned.1.call-start = ((), (), s32[]{:S(2)}) async-start(), calls=%async_computation.31 | async-start | bytes 9437184 | tf_op jit(solution)/shard_map/reduce_scatter | solution.py:58
  2142.9 94.6 %copy-start.47 = (f32[256]{0:T(256)S(1)}, f32[256]{0:T(256)}, u32[]{:S(2)}) copy-start(f32[256]{0:T(256)} %get-tuple-element.28) | copy-start | bytes 3076
  2142.9 94.6 %copy-start.46 = (f32[256]{0:T(256)S(1)}, f32[256]{0:T(256)}, u32[]{:S(2)}) copy-start(f32[256]{0:T(256)} %get-tuple-element.17) | copy-start | bytes 3076
  2237.5 287.0 %copy-start.3 = (f32[1024,256]{1,0:T(8,128)S(1)}, f32[1024,256]{1,0:T(8,128)}, u32[]{:S(2)}) copy-start(f32[1024,256]{1,0:T(8,128)} %param.16) | copy-start | bytes 3145732
  2237.5 287.0 %copy-start.28 = (f32[1024]{0:T(1024)S(1)}, f32[1024]{0:T(1024)}, u32[]{:S(2)}) copy-start(f32[1024]{0:T(1024)} %copy-done.27) | copy-start | bytes 12292
  2237.5 287.0 %copy-start.30 = (f32[1024]{0:T(1024)S(1)}, f32[1024]{0:T(1024)}, u32[]{:S(2)}) copy-start(f32[1024]{0:T(1024)} %copy-done.29) | copy-start | bytes 12292
  2237.5 287.0 %copy-start.38 = (f32[1,256]{1,0:T(1,128)S(1)}, f32[1,256]{1,0:T(1,128)}, u32[]{:S(2)}) copy-start(f32[1,256]{1,0:T(1,128)} %copy-done.37) | copy-start | bytes 3076
  (35 other events, 79.6 us)
Sparse Core Ops, SparseCore 0:
  10.8 31.0 all-gather.40
  44.5 74.1 all-gather.24
  120.8 15.7 all-gather.42
  146.5 148.2 reduce-scatter.16
  296.9 33.8 all-gather.44
  332.8 74.1 all-gather.26
  409.3 33.4 all-gather.46
  454.6 149.0 reduce-scatter.18
  605.2 27.8 all-gather.48
  635.6 74.1 all-gather.28
  711.4 15.7 all-gather.50
  739.6 148.0 reduce-scatter.20
  889.4 33.8 all-gather.52
  925.9 74.1 all-gather.30
  1002.2 33.4 all-gather.54
  1037.8 74.1 all-gather.32
  1132.6 148.0 reduce-scatter.24
  1284.2 148.6 reduce-scatter.22
  1437.9 73.5 all-gather.34
  1537.2 148.0 reduce-scatter.26
  1707.3 75.3 all-gather.36
  1801.3 148.0 reduce-scatter.28
  1970.4 75.3 all-gather.38
  2048.3 43.1 reduce-scatter.46
  2094.5 44.5 reduce-scatter.44
  2142.2 44.4 reduce-scatter.42
  2189.1 44.5 reduce-scatter.40
  2237.0 24.8 reduce-scatter.38
  2264.4 24.8 reduce-scatter.36
  2291.8 37.9 reduce-scatter.34
  2332.9 37.9 reduce-scatter.32
  2375.0 149.5 reduce-scatter.30
where the time goes:
time: 2580 us; the launch traced here: 2570 us
  waiting for transfers between devices  2080 us (81%)
  matrix products  224 us (9%)
  blocking collectives  147 us (6%)
  other arithmetic  62.9 us (2%)
  local copies, waits for them, and re-layouts  34.6 us (1%)
    reduce_scatter x4, waiting for transfers between devices, column_sum_back(): lax.psum_scatter(partial_term, 'col', scatter_dimension=1, tiled=True)  583 us
    reduce_scatter x4, waiting for transfers between devices, column_sum(): lax.psum_scatter(partial_term, 'col', scatter_dimension=1, tiled=True)  573 us
    all_gather x4, waiting for transfers between devices, gather_features(): return lax.all_gather(value, 'col', axis=1, tiled=True)  307 us
    all_gather x4, waiting for transfers between devices, gather_gradient(): return lax.all_gather(value, 'col', axis=1, tiled=True)  254 us
    reduce_scatter x2, waiting for transfers between devices, on_device(): lax.psum_scatter(up_term.astype(jnp.bfloat16), 'row', scatter_dimension=0...  90.8 us
    reduce_scatter x2, waiting for transfers between devices, on_device(): lax.psum_scatter(joined_term.astype(jnp.bfloat16), 'row', scatter_dimensi...  79.6 us
    psum x4, blocking collectives, norm_forward(): lax.psum((jnp.sum(value, axis=1), jnp.sum(value * value, axis=1)), 'col')  67.5 us
    psum x4, blocking collectives, norm_backward(): lax.psum((jnp.sum(scaled, axis=1), jnp.sum(scaled * centred, axis=1)), 'c...  65.1 us
  transfers between devices with their start and end apart: 32, of which 29 were waited for; matrix products, arithmetic and copies ran while one was open for 8% of the time, Pallas kernels for 0%

commit v1 on v0

v1 whole, which is shorter than its diff:
```python
import functools
import math

import jax
import jax.numpy as jnp
from jax import lax
from jax.experimental import pallas as pl
from jax.experimental.pallas import tpu as pltpu
from jax.sharding import Mesh
from jax.sharding import PartitionSpec as P

HEADS = 16
HEAD_DIM = 128
PAD = 16
LANES = 128

norm_eps = 1e-05
masked_score = -1e30

F32 = jnp.float32
BF16 = jnp.bfloat16


def gelu_tanh(value):
    return jax.nn.gelu(value, approximate=True)


def ring_size():
    return lax.axis_size("t")


def ring(value, k):
    if k == 0:
        return value
    return lax.ppermute(value, "t", [(i, i ^ k) for i in range(ring_size())])


def partner(value):
    return lax.ppermute(value, "c", [(0, 1), (1, 0)])


def far(value):
    return lax.ppermute(value, "zh", [(0, 1), (1, 0)])


def swap_roles(value):
    return lax.ppermute(value, ("c", "zh"), [(0, 0), (1, 2), (2, 1), (3, 3)])


def block_index():
    return lax.axis_index("c") * ring_size() + lax.axis_index("t")


def slot_blocks():
    return (jnp.arange(2 * ring_size(), dtype=jnp.int32) ^ block_index()).astype(jnp.int32)


def gather_slots(value):
    mine = [ring(value, k) for k in range(ring_size())]
    return mine + [partner(v) for v in mine]


def scatter_slots(mine, other):
    got = partner(other)
    pair = mine.astype(F32) + got.astype(F32)
    total = pair[0]
    for k in range(1, ring_size()):
        total = total + ring(pair[k].astype(BF16), k).astype(F32)
    return total


def rows_of(column):
    return column.reshape(-1, LANES)


def packed(value, rows, width):
    extra = jnp.zeros((PAD, width), value.dtype)
    extra = lax.dynamic_update_slice(extra, rows.astype(value.dtype), (0, 0))
    return jnp.concatenate([value, extra], axis=0)


def assemble_norm_kernel(slots, width, blocks_ref, *refs):
    shards = refs[:slots]
    means_ref, spread_ref, gain_ref, shift_ref, own_ref = refs[slots : slots + 5]
    out_ref, centred_ref, inverse_ref = refs[slots + 5 :]
    f = shards[0].shape[1]
    offsets = lax.dot_general(
        means_ref[0].astype(BF16),
        spread_ref[...],
        (((0,), (0,)), ((), ())),
        preferred_element_type=F32,
    )
    values = [shards[s][...].astype(F32) + offsets[:, s * f : (s + 1) * f] for s in range(slots)]
    total = values[0]
    for v in values[1:]:
        total = total + v
    mean = jnp.sum(total, axis=1, keepdims=True) / width
    values = [v - mean for v in values]
    squares = values[0] * values[0]
    for v in values[1:]:
        squares = squares + v * v
    inverse = lax.rsqrt(jnp.sum(squares, axis=1, keepdims=True) / width + norm_eps)
    for s in range(slots):
        block = blocks_ref[s]
        normed = values[s] * inverse * gain_ref[block] + shift_ref[block]
        out_ref[:, pl.ds(pl.multiple_of(block * f, f), f)] = normed.astype(BF16)
    centred_ref[...] = (own_ref[...] - mean) * inverse
    inverse_ref[...] = jnp.broadcast_to(inverse, inverse_ref.shape)


def assemble_norm(shards, own, gain, shift):
    slots = len(shards)
    tokens, f = own.shape
    width = slots * f
    groups = tokens // LANES
    means = jnp.stack([s[tokens : tokens + groups, :LANES] for s in shards], axis=1).astype(F32)
    spread = jnp.repeat(jnp.eye(slots, dtype=BF16), f, axis=1)
    tile = LANES
    whole = lambda shape: pl.BlockSpec(shape, lambda g, b: (0,) * len(shape))
    return pl.pallas_call(
        functools.partial(assemble_norm_kernel, slots, width),
        grid_spec=pltpu.PrefetchScalarGridSpec(
            num_scalar_prefetch=1,
            grid=(tokens // tile,),
            in_specs=[pl.BlockSpec((tile, f), lambda g, b: (g, 0))] * slots
            + [
                pl.BlockSpec((1, slots, LANES), lambda g, b: (g, 0, 0)),
                whole((slots, width)),
                whole((slots, 1, f)),
                whole((slots, 1, f)),
                pl.BlockSpec((tile, f), lambda g, b: (g, 0)),
            ],
            out_specs=[
                pl.BlockSpec((tile, width), lambda g, b: (g, 0)),
                pl.BlockSpec((tile, f), lambda g, b: (g, 0)),
                pl.BlockSpec((tile, LANES), lambda g, b: (g, 0)),
            ],
        ),
        out_shape=[
            jax.ShapeDtypeStruct((tokens, width), BF16),
            jax.ShapeDtypeStruct((tokens, f), F32),
            jax.ShapeDtypeStruct((tokens, LANES), F32),
        ],
        compiler_params=pltpu.CompilerParams(vmem_limit_bytes=24 * 2**20),
        cost_estimate=pl.CostEstimate(
            flops=12 * tokens * width, bytes_accessed=6 * tokens * width, transcendentals=tokens
        ),
        name="assemble_norm",
    )(
        slot_blocks(),
        *shards,
        means,
        spread,
        gain.reshape(slots, 1, f),
        shift.reshape(slots, 1, f),
        own,
    )


def assemble_kernel(slots, blocks_ref, *refs):
    out_ref = refs[slots]
    f = refs[0].shape[1]
    for s in range(slots):
        out_ref[:, pl.ds(pl.multiple_of(blocks_ref[s] * f, f), f)] = refs[s][...]


def assemble(shards):
    slots = len(shards)
    tokens, f = shards[0].shape
    tile = min(tokens, 256)
    return pl.pallas_call(
        functools.partial(assemble_kernel, slots),
        grid_spec=pltpu.PrefetchScalarGridSpec(
            num_scalar_prefetch=1,
            grid=(tokens // tile,),
            in_specs=[pl.BlockSpec((tile, f), lambda g, b: (g, 0))] * slots,
            out_specs=pl.BlockSpec((tile, slots * f), lambda g, b: (g, 0)),
        ),
        out_shape=jax.ShapeDtypeStruct((tokens, slots * f), shards[0].dtype),
        compiler_params=pltpu.CompilerParams(vmem_limit_bytes=24 * 2**20),
        cost_estimate=pl.CostEstimate(
            flops=0, bytes_accessed=4 * tokens * slots * f, transcendentals=0
        ),
        name="assemble",
    )(slot_blocks(), *shards)


def slot_matmul_kernel(transposed, tile, blocks_ref, x_ref, w_ref, extra_ref, out_ref):
    tokens = x_ref.shape[0]
    w = w_ref[...].reshape(w_ref.shape[-2:])
    dims = (((1,), (1 if transposed else 0,)), ((), ()))

    @pl.loop(0, tokens // tile)
    def _(g):
        at = pl.ds(pl.multiple_of(g * tile, tile), tile)
        out_ref[0, at, :] = lax.dot_general(
            x_ref[at, :], w, dims, preferred_element_type=F32
        ).astype(BF16)

    out_ref[0, tokens:, :] = extra_ref[...]


def slot_matmul(x, w, extra, other, transposed):
    tokens, depth = x.shape
    n = ring_size()
    f = extra.shape[1]
    blocks = slot_blocks()
    blocks = blocks[n:] if other else blocks[:n]
    if transposed:
        w_spec = pl.BlockSpec((f, depth), lambda k, b: (b[k], 0))
    else:
        per = w.shape[2] // f
        w_spec = pl.BlockSpec((1, depth, f), lambda k, b: (b[k] // per, 0, b[k] % per))
    tile = min(tokens, 256)
    return pl.pallas_call(
        functools.partial(slot_matmul_kernel, transposed, tile),
        grid_spec=pltpu.PrefetchScalarGridSpec(
            num_scalar_prefetch=1,
            grid=(n,),
            in_specs=[
                pl.BlockSpec((tokens, depth), lambda k, b: (0, 0)),
                w_spec,
                pl.BlockSpec((PAD, f), lambda k, b: (0, 0)),
            ],
            out_specs=pl.BlockSpec((1, tokens + PAD, f), lambda k, b: (k, 0, 0)),
        ),
        out_shape=jax.ShapeDtypeStruct((n, tokens + PAD, f), BF16),
        compiler_params=pltpu.CompilerParams(vmem_limit_bytes=24 * 2**20),
        cost_estimate=pl.CostEstimate(
            flops=2 * tokens * depth * n * f,
            bytes_accessed=2 * (tokens * depth + n * f * (depth + tokens)),
            transcendentals=0,
        ),
        name="slot_matmul",
    )(blocks, x, w, extra)


def column_sum(x, w, extra, transposed):
    other = slot_matmul(x, w, extra, True, transposed)
    mine = slot_matmul(x, w, extra, False, transposed)
    return scatter_slots(mine, other)


def gather_weight(weight):
    same = lax.axis_index("c") == lax.axis_index("zh")
    first = lax.axis_index("c") == 0
    own = weight.astype(BF16)
    received = far(own)
    keep = jnp.where(same, own, received)
    got = partner(jnp.where(same, received, own))
    pair = jnp.stack([jnp.where(first, keep, got), jnp.where(first, got, keep)])
    return lax.all_gather(pair, "rh", axis=0, tiled=True)


def scatter_weight(term):
    same = lax.axis_index("c") == lax.axis_index("zh")
    first = lax.axis_index("c") == 0
    pair = lax.psum_scatter(term.astype(BF16), "rh", scatter_dimension=0, tiled=True)
    mine = jnp.where(first, pair[0], pair[1])
    got = partner(jnp.where(first, pair[1], pair[0]))
    keep = jnp.where(same, mine, got)
    received = far(jnp.where(same, got, mine))
    return keep.astype(F32) + received.astype(F32)


def slot_scores(query, key, lengths, slopes):
    slot_count = lengths.shape[0]
    span = query.shape[0] // slot_count
    heads = query.shape[1]
    depth = query.shape[2]
    query_slots = query.reshape(slot_count, span, heads, depth)
    key_slots = key.reshape(slot_count, span, heads, depth)
    position = jnp.arange(span)
    distance = (position[:, None] - position[None, :]).astype(F32)
    allowed = (position[None, None, :] <= position[None, :, None]) & (
        position[None, None, :] < lengths[:, None, None]
    )
    scores = jnp.einsum(
        "sqhd,skhd->shqk", query_slots, key_slots, preferred_element_type=F32
    ) * (1.0 / math.sqrt(depth))
    scores = scores - slopes[None, :, None, None] * distance[None, None]
    return jnp.where(allowed[:, None], scores, masked_score)


def attention_forward(query, key, value, lengths, slopes):
    tokens, heads, depth = query.shape
    slot_count = lengths.shape[0]
    scores = slot_scores(query, key, lengths, slopes)
    highest_score = jnp.max(scores, axis=-1, keepdims=True)
    raised = jnp.exp(scores - highest_score)
    total = jnp.sum(raised, axis=-1, keepdims=True)
    chances = raised / total
    log_total = highest_score[..., 0] + jnp.log(total[..., 0])
    value_slots = value.reshape(slot_count, tokens // slot_count, heads, depth)
    context = jnp.einsum(
        "shqk,skhd->sqhd", chances.astype(BF16), value_slots, preferred_element_type=F32
    )
    return (context.reshape(tokens, heads * depth), log_total)


def attention_backward(query, key, value, log_total, context_grad, lengths, slopes):
    tokens, heads, depth = query.shape
    slot_count = lengths.shape[0]
    span = tokens // slot_count
    scores = slot_scores(query, key, lengths, slopes)
    chances = jnp.exp(scores - log_total[..., None])
    output_slots = context_grad.reshape(slot_count, span, heads, depth)
    value_slots = value.reshape(slot_count, span, heads, depth)
    query_slots = query.reshape(slot_count, span, heads, depth)
    key_slots = key.reshape(slot_count, span, heads, depth)
    value_grad = jnp.einsum(
        "shqk,sqhd->skhd", chances.astype(BF16), output_slots, preferred_element_type=F32
    )
    chance_grad = jnp.einsum(
        "sqhd,skhd->shqk", output_slots, value_slots, preferred_element_type=F32
    )
    row_dot = jnp.sum(chances * chance_grad, axis=-1, keepdims=True)
    score_grad = (chances * (chance_grad - row_dot)).astype(BF16)
    factor = 1.0 / math.sqrt(depth)
    query_grad = (
        jnp.einsum("shqk,skhd->sqhd", score_grad, key_slots, preferred_element_type=F32) * factor
    )
    key_grad = (
        jnp.einsum("shqk,sqhd->skhd", score_grad, query_slots, preferred_element_type=F32) * factor
    )
    return (
        query_grad.reshape(tokens, heads, depth).astype(BF16),
        key_grad.reshape(tokens, heads, depth).astype(BF16),
        value_grad.reshape(tokens, heads, depth).astype(BF16),
    )


def shard_of(value):
    mean = lax.reduce_precision(jnp.mean(value, axis=1, keepdims=True), 8, 7)
    return packed((value - mean).astype(BF16), rows_of(mean), value.shape[1])


def weight_products(gain, shift, weight):
    def parts(v):
        high = lax.reduce_precision(v, 8, 7)
        return [high.astype(BF16), (v - high).astype(BF16)]

    rows = jnp.stack(parts(gain) + parts(shift))
    out = jnp.dot(rows, weight, preferred_element_type=F32)
    return out[0] + out[1], out[2] + out[3]


def sums_rows(first, second, width):
    extra = jnp.concatenate([rows_of(first), rows_of(second)], axis=0).astype(BF16)
    return jnp.pad(extra, ((0, PAD - extra.shape[0]), (0, width - extra.shape[1])))


def norm_backward(summed, centred, inverse, gain, width):
    tokens = centred.shape[0]
    groups = tokens // LANES
    gradient = summed[:tokens]
    first_sum = summed[tokens : tokens + groups, :LANES].reshape(tokens, 1)
    second_sum = summed[tokens + groups : tokens + 2 * groups, :LANES].reshape(tokens, 1)
    passed = inverse[:, :1] * (gradient * gain - first_sum / width - centred * (second_sum / width))
    return (passed, jnp.sum(gradient * centred, axis=0), jnp.sum(gradient, axis=0))


def on_device(
    activations,
    cotangent,
    lengths,
    first_gain,
    first_shift,
    joined_weight,
    query_bias,
    value_bias,
    output_weight,
    output_bias,
    second_gain,
    second_shift,
    up_weight,
    up_bias,
    down_weight,
    down_bias,
):
    tokens, f = activations.shape
    layers = first_gain.shape[0]
    blocks = 2 * ring_size()
    width = blocks * f
    heads_local = f // HEAD_DIM
    mine = block_index()

    smalls = (
        first_gain,
        first_shift,
        query_bias,
        value_bias,
        output_bias,
        second_gain,
        second_shift,
        down_bias,
    )
    table = jnp.concatenate([s.reshape(layers, 1, f) for s in smalls] + [up_bias.reshape(layers, -1, f)], axis=1)
    table = lax.all_gather(table, ("zh", "t"), axis=0)
    own_table = lax.dynamic_index_in_dim(table, mine, 0, keepdims=False)
    own_up = own_table[:, len(smalls) :].reshape(layers, -1)

    all_lengths = lax.all_gather(lengths, "c", axis=0)
    lengths = lax.dynamic_index_in_dim(all_lengths, lax.axis_index("zh"), 0, keepdims=False)

    head_index = mine * heads_local + jnp.arange(heads_local)
    slopes = jnp.exp2(-8.0 * (head_index + 1).astype(F32) / HEADS)
    slot_count = lengths.shape[0]
    span = tokens // slot_count
    valid = (jnp.arange(span)[None, :] < lengths[:, None]).reshape(tokens, 1)

    shard = swap_roles(shard_of(activations))
    residual = swap_roles(activations)
    no_rows = jnp.zeros((PAD, f), BF16)
    saved = []
    for layer in range(layers):
        joined_w = gather_weight(joined_weight[layer])
        output_w = gather_weight(output_weight[layer])
        up_w = gather_weight(up_weight[layer])
        down_w = gather_weight(down_weight[layer])
        joined_w = joined_w.reshape(width, -1)
        up_w = up_w.reshape(width, -1)
        gains = [table[:, layer, k] for k in range(len(smalls))]

        if layer > 0:
            shard = shard_of(residual)
        normed_one, centred_one, inverse_one = assemble_norm(
            gather_slots(shard), residual, gains[0], gains[1]
        )
        joined = jnp.dot(normed_one, joined_w, preferred_element_type=F32).reshape(
            tokens, heads_local, 3, HEAD_DIM
        )
        query_shift = own_table[layer, 2].reshape(heads_local, HEAD_DIM)
        value_shift = own_table[layer, 3].reshape(heads_local, HEAD_DIM)
        query = (joined[:, :, 0] + query_shift).astype(BF16)
        key = joined[:, :, 1].astype(BF16)
        value = (joined[:, :, 2] + value_shift).astype(BF16)
        context, log_total = attention_forward(query, key, value, lengths, slopes)
        context = context.astype(BF16)
        middle = (
            residual
            + column_sum(context, output_w, no_rows, False)[:tokens]
            + own_table[layer, 4]
        )
        normed_two, centred_two, inverse_two = assemble_norm(
            gather_slots(shard_of(middle)), middle, gains[5], gains[6]
        )
        upper = jnp.dot(normed_two, up_w, preferred_element_type=F32) + own_up[layer]
        activated = gelu_tanh(upper).astype(BF16)
        residual = (
            middle
            + column_sum(activated, down_w, no_rows, False)[:tokens]
            + own_table[layer, 7]
        )
        saved.append(
            (
                normed_one,
                centred_one,
                inverse_one,
                query,
                key,
                value,
                log_total,
                context,
                normed_two,
                centred_two,
                inverse_two,
                upper,
                activated,
                joined_w,
                output_w,
                up_w,
                down_w,
            )
        )
    result = swap_roles(residual)
    gradient = swap_roles(cotangent) * valid
    weight_terms = [None] * layers
    small_terms = [None] * layers
    passed_one = None
    for layer in reversed(range(layers)):
        (
            normed_one,
            centred_one,
            inverse_one,
            query,
            key,
            value,
            log_total,
            context,
            normed_two,
            centred_two,
            inverse_two,
            upper,
            activated,
            joined_w,
            output_w,
            up_w,
            down_w,
        ) = saved[layer]
        own = own_table[layer]
        gains = [table[:, layer, k].reshape(width) for k in range(len(smalls))]
        column_blocks = down_w.shape[0]

        down_bias_term = jnp.sum(gradient, axis=0)
        low_gradient = assemble(gather_slots(gradient.astype(BF16)))
        down_full = down_w.transpose(1, 0, 2).reshape(-1, width)
        hidden_grad = jnp.einsum("td,fd->tf", low_gradient, down_full, preferred_element_type=F32)
        upper_grad = jax.vjp(gelu_tanh, upper)[1](hidden_grad)[0].astype(BF16)
        wide_grad = upper_grad.astype(F32)
        gain_product, shift_product = weight_products(gains[5], gains[6], up_w)
        first_sum = jnp.sum(wide_grad * gain_product, axis=1)
        second_sum = jnp.sum(wide_grad * (upper - (own_up[layer] + shift_product)), axis=1)
        normed_two_grad = column_sum(upper_grad, up_w, sums_rows(first_sum, second_sum, f), True)
        up_bias_term = jnp.sum(wide_grad, axis=0)
        down_term = jnp.einsum("tf,td->fd", activated, low_gradient, preferred_element_type=F32)
        up_term = jnp.einsum("td,tf->df", normed_two, upper_grad, preferred_element_type=F32)
        passed_two, gain_two_term, shift_two_term = norm_backward(
            normed_two_grad, centred_two, inverse_two, own[5], width
        )
        middle_grad = gradient + passed_two
        output_bias_term = jnp.sum(middle_grad, axis=0)
        low_middle = assemble(gather_slots(middle_grad.astype(BF16)))
        output_full = output_w.transpose(1, 0, 2).reshape(-1, width)
        context_grad = jnp.einsum(
            "td,cd->tc", low_middle, output_full, preferred_element_type=F32
        ).astype(BF16)
        output_term = jnp.einsum("tc,td->cd", context, low_middle, preferred_element_type=F32)
        query_grad, key_grad, value_grad = attention_backward(
            query, key, value, log_total, context_grad, lengths, slopes
        )
        joined_grad = jnp.stack((query_grad, key_grad, value_grad), axis=2).reshape(tokens, 3 * f)
        query_shift = own[2].reshape(heads_local, HEAD_DIM)
        value_shift = own[3].reshape(heads_local, HEAD_DIM)
        joined_shift = jnp.stack(
            (query_shift, jnp.zeros_like(query_shift), value_shift), axis=1
        ).reshape(3 * f)
        joined = jnp.stack((query, key, value), axis=2).reshape(tokens, 3 * f)
        wide_grad = joined_grad.astype(F32)
        gain_product, shift_product = weight_products(gains[0], gains[1], joined_w)
        first_sum = jnp.sum(wide_grad * gain_product, axis=1)
        second_sum = jnp.sum(
            wide_grad * (joined.astype(F32) - (joined_shift + shift_product)), axis=1
        )
        normed_one_grad = column_sum(joined_grad, joined_w, sums_rows(first_sum, second_sum, f), True)
        query_bias_term = jnp.sum(query_grad.astype(F32), axis=0).reshape(f)
        value_bias_term = jnp.sum(value_grad.astype(F32), axis=0).reshape(f)
        joined_term = jnp.einsum("td,tc->dc", normed_one, joined_grad, preferred_element_type=F32)
        passed_one, gain_one_term, shift_one_term = norm_backward(
            normed_one_grad, centred_one, inverse_one, own[0], width
        )
        gradient = middle_grad + passed_one
        small_terms[layer] = jnp.concatenate(
            [
                t.reshape(-1, f)
                for t in (
                    gain_one_term,
                    shift_one_term,
                    query_bias_term,
                    value_bias_term,
                    output_bias_term,
                    gain_two_term,
                    shift_two_term,
                    down_bias_term,
                    up_bias_term,
                )
            ],
            axis=0,
        )

        def by_columns(term):
            return term.reshape(term.shape[0], column_blocks, -1).transpose(1, 0, 2)

        def by_rows(term):
            return term.reshape(column_blocks, -1, term.shape[1])

        weight_terms[layer] = (
            scatter_weight(by_rows(joined_term)),
            scatter_weight(by_columns(output_term)),
            scatter_weight(by_rows(up_term)),
            scatter_weight(by_columns(down_term)),
        )
    input_grad = swap_roles(middle_grad) + swap_roles(passed_one.astype(BF16)).astype(F32)
    small = lax.psum(jnp.stack(small_terms), ("rh", "zh"))
    same = lax.axis_index("c") == lax.axis_index("zh")
    small = jnp.where(same, small, partner(small))

    def weight_out(k):
        return jnp.stack([entry[k] for entry in weight_terms])

    return (
        result,
        input_grad,
        small[:, 0],
        small[:, 1],
        weight_out(0),
        small[:, 2],
        small[:, 3],
        weight_out(1),
        small[:, 4],
        small[:, 5],
        small[:, 6],
        weight_out(2),
        small[:, 8:].reshape(layers, -1),
        weight_out(3),
        small[:, 7],
    )


def solution(mesh):
    rows, columns = mesh.devices.shape
    inner = Mesh(mesh.devices.reshape(rows // 2, 2, 2, columns // 2), ("rh", "c", "zh", "t"))
    row, col = ("rh", "c"), ("zh", "t")
    return jax.shard_map(
        on_device,
        mesh=inner,
        in_specs=(
            P(row, col),
            P(row, col),
            P(row),
            P(None, col),
            P(None, col),
            P(None, row, col),
            P(None, col),
            P(None, col),
            P(None, col, row),
            P(None, col),
            P(None, col),
            P(None, col),
            P(None, row, col),
            P(None, col),
            P(None, col, row),
            P(None, col),
        ),
        out_specs=(
            P(row, col),
            P(row, col),
            P(None, col),
            P(None, col),
            P(None, row, col),
            P(None, col),
            P(None, col),
            P(None, col, row),
            P(None, col),
            P(None, col),
            P(None, col),
            P(None, row, col),
            P(None, col),
            P(None, col, row),
            P(None, col),
        ),
        check_vma=False,
    )
```

time: 2580 us -> 1560 us (0.60)
  waiting for transfers between devices: 2080 us -> 646 us
  starting transfers between devices: 3.54 us -> 169 us
  local copies, waits for them, and re-layouts: 34.6 us -> 171 us
  Pallas kernels: 0 us -> 133 us
  matrix products: 224 us -> 137 us
  other arithmetic: 62.9 us -> 149 us
  blocking collectives: 147 us -> 116 us
    reduce_scatter x16 -> x8, waiting for transfers between devices: 1420 us -> 0.05 us  [scatter_weight(): lax.psum_scatter(term.astype(BF16), 'rh', scatter_dimension=0, tiled=True)]
    all_gather x16 -> x8, waiting for transfers between devices: 653 us -> 0.09 us  [gather_weight(): return lax.all_gather(pair, 'rh', axis=0, tiled=True)]
    ppermute x0 -> x127, waiting for transfers between devices: none -> 646 us  [the longest x48 316 us: ring(): return lax.ppermute(value, 't', [(i, i ^ k) for i in range(ring_size())])]
    ppermute x0 -> x127, starting transfers between devices: none -> 167 us  [the longest x57 87.5 us: partner(): return lax.ppermute(value, 'c', [(0, 1), (1, 0)])]
    psum x9 -> x1, blocking collectives: 147 us -> 12.8 us  [on_device(): small = lax.psum(jnp.stack(small_terms), ('rh', 'zh'))]
    pallas_call x0 -> x24, Pallas kernels: none -> 133 us  [the longest x16 93.4 us: slot_matmul(): pl.pallas_call(functools.partial(slot_matmul_kernel, transposed, tile), g...]
    all_gather x0 -> x1, blocking collectives: none -> 100 us  [on_device(): table = lax.all_gather(table, ('zh', 't'), axis=0)]
    dot_general x28 -> x24, matrix products: 196 us -> 116 us  [the longest x2 19.9 us: on_device(): jnp.dot(normed_two, up_w, preferred_element_type=F32) + own_up[layer]]
  transfers between devices with their start and end apart: 32 -> 143, of which waited for: 29 -> 59; matrix products, arithmetic and copies ran while one was open for 8% -> 24% of each run, Pallas kernels for 0% -> 8%
where the time goes in v1:
time: 1560 us; the launch traced here: 1540 us
  waiting for transfers between devices  646 us (41%)
  local copies, waits for them, and re-layouts  171 us (11%)
  starting transfers between devices  169 us (11%)
  other arithmetic  149 us (10%)
  matrix products  137 us (9%)
  Pallas kernels  133 us (9%)
  blocking collectives  116 us (7%)
  between operations  17.8 us (1%)
    ppermute x48, waiting for transfers between devices, ring(): return lax.ppermute(value, 't', [(i, i ^ k) for i in range(ring_size())])  316 us
    ppermute x16, waiting for transfers between devices, far(): return lax.ppermute(value, 'zh', [(0, 1), (1, 0)])  201 us
    ppermute x6, waiting for transfers between devices, swap_roles(): return lax.ppermute(value, ('c', 'zh'), [(0, 0), (1, 2), (2, 1), (3, 3)])  117 us
    all_gather x1, blocking collectives, on_device(): table = lax.all_gather(table, ('zh', 't'), axis=0)  100 us
    pallas_call x16, Pallas kernels, slot_matmul(): pl.pallas_call(functools.partial(slot_matmul_kernel, transposed, tile), g...  93.4 us
    ppermute x57, starting transfers between devices, partner(): return lax.ppermute(value, 'c', [(0, 1), (1, 0)])  87.5 us
    unnamed x373, local copies, waits for them, and re-layouts  71.6 us
    ppermute x48, starting transfers between devices, ring(): return lax.ppermute(value, 't', [(i, i ^ k) for i in range(ring_size())])  46.1 us
  transfers between devices with their start and end apart: 143, of which 59 were waited for; matrix products, arithmetic and copies ran while one was open for 24% of the time, Pallas kernels for 8%

profile of v1, /device:TPU:1, one launch (start us, length us, event | category | flops | bytes accessed | tf_op | source)
XLA Modules:
  0.0 1537.9 jit_solution(6627093153140656536)
XLA Ops:
  13.6 50.9 %collective-permute-done.39 = bf16[512,768]{1,0:T(8,128)(2,1)S(1)} collective-permute-done((bf16[512,768]{1,0:T(8,128)(2,1)S(1)}, bf16[512,768]{1,0:T(8,128)(2,1)S(1)}, u32[]{:S(2)}, u32[]{:S(2)}) %collective-permute-start.39) | collective-permute-done | bytes 786464 | tf_op jit(solution)/shard_map/ppermute | solution.py:43
  73.5 19.1 %collective-permute-done.9 = bf16[512,768]{1,0:T(8,128)(2,1)} collective-permute-done((bf16[512,768]{1,0:T(8,128)(2,1)}, bf16[512,768]{1,0:T(8,128)(2,1)}, u32[]{:S(2)}, u32[]{:S(2)}) %collective-permute-start.9) | collective-permute-done | bytes 786464 | tf_op jit(solution)/shard_map/ppermute | solution.py:43
  123.0 100.3 %all-gather = f32[16,12,256]{2,1,0:T(8,128)S(1)} all-gather(f32[2,12,256]{2,1,0:T(8,128)S(1)} %concatenate.38), channel_id=2, replica_groups=mesh['rh'=2,'c'=2,'zh'=2,'t'=4] {'zh','t'}, dimensions={0}, use_global_device_ids=true | all-gather | bytes 221184 | tf_op jit(solution)/shard_map/all_gather | solution.py:399
  246.7 21.3 %collective-permute-done.4.refs_3_ = bf16[1040,256]{1,0:T(8,128)(2,1)S(1)} collective-permute-done((bf16[1040,256]{1,0:T(8,128)(2,1)S(1)}, bf16[1040,256]{1,0:T(8,128)(2,1)S(1)}, u32[]{:S(2)}, u32[]{:S(2)}) %collective-permute-start.4) | collective-permute-done | bytes 532512 | tf_op jit(solution)/shard_map/ppermute | solution.py:35
  271.3 15.4 %collective-permute-done.3.refs_2_ = bf16[1040,256]{1,0:T(8,128)(2,1)S(1)} collective-permute-done((bf16[1040,256]{1,0:T(8,128)(2,1)S(1)}, bf16[1040,256]{1,0:T(8,128)(2,1)S(1)}, u32[]{:S(2)}, u32[]{:S(2)}) %collective-permute-start.3) | collective-permute-done | bytes 532512 | tf_op jit(solution)/shard_map/ppermute | solution.py:35
  297.5 50.7 %collective-permute-done.refs_12_ = f32[1024,256]{1,0:T(8,128)S(1)} collective-permute-done((f32[1024,256]{1,0:T(8,128)}, f32[1024,256]{1,0:T(8,128)S(1)}, u32[]{:S(2)}, u32[]{:S(2)}) %collective-permute-start) | collective-permute-done | bytes 1048608 | tf_op jit(solution)/shard_map/ppermute | solution.py:47
  354.5 6.5 assemble_norm.4
  375.3 7.1 fusion.28
  412.8 22.4 %collective-permute-done.14 = bf16[1040,256]{1,0:T(8,128)(2,1)S(1)} collective-permute-done((bf16[1040,256]{1,0:T(8,128)(2,1)S(1)}, bf16[1040,256]{1,0:T(8,128)(2,1)S(1)}, u32[]{:S(2)}, u32[]{:S(2)}) %collective-permute-start.14) | collective-permute-done | bytes 532512 | tf_op jit(solution)/shard_map/ppermute | solution.py:35
  443.7 6.6 collective-permute-done.19.refs_3_
  453.9 7.1 collective-permute-done.18.refs_2_
  465.6 7.7 assemble_norm.5
  477.0 10.6 multiply_convert_fusion.3
  490.6 6.8 slot_matmul.19
  520.3 17.6 %collective-permute-done.31 = bf16[1040,256]{1,0:T(8,128)(2,1)S(1)} collective-permute-done((bf16[1040,256]{1,0:T(8,128)(2,1)S(1)}, bf16[1040,256]{1,0:T(8,128)(2,1)S(1)}, u32[]{:S(2)}, u32[]{:S(2)}) %collective-permute-start.31) | collective-permute-done | bytes 532512 | tf_op jit(solution)/shard_map/ppermute | solution.py:35
  537.9 11.3 collective-permute-done.30
  566.2 8.4 collective-permute-done.32.refs_1_
  576.5 11.8 collective-permute-done.33.refs_2_
  591.5 8.2 collective-permute-done.34.refs_3_
  603.6 7.9 assemble_norm.6
  643.6 6.4 copy.712
  650.0 10.0 fusion.216
  668.9 22.0 %collective-permute-done.44 = bf16[1040,256]{1,0:T(8,128)(2,1)S(1)} collective-permute-done((bf16[1040,256]{1,0:T(8,128)(2,1)S(1)}, bf16[1040,256]{1,0:T(8,128)(2,1)S(1)}, u32[]{:S(2)}, u32[]{:S(2)}) %collective-permute-start.44) | collective-permute-done | bytes 532512 | tf_op jit(solution)/shard_map/ppermute | solution.py:35
  710.1 7.0 collective-permute-done.48.refs_2_
  722.0 7.7 assemble_norm.7
  729.7 9.3 convert_reduce_fusion.1
  745.7 6.4 slot_matmul.24
  756.2 21.5 %collective-permute-done.72 = bf16[1040,256]{1,0:T(8,128)(2,1)S(1)} collective-permute-done((bf16[1040,256]{1,0:T(8,128)(2,1)S(1)}, bf16[1040,256]{1,0:T(8,128)(2,1)S(1)}, u32[]{:S(2)}, u32[]{:S(2)}) %collective-permute-start.72) | collective-permute-done | bytes 532512 | tf_op jit(solution)/shard_map/ppermute | solution.py:35
  785.8 8.3 collective-permute-done.77.refs_3_
  798.1 6.5 collective-permute-done.76.refs_2_
  812.2 6.4 copy.786
  823.2 8.3 convolution_convert_fusion
  831.6 6.4 copy.747
  867.3 6.5 slot_matmul.27
  874.1 6.3 convolution_convert_fusion.2
  893.3 22.2 %collective-permute-done.83 = bf16[1040,256]{1,0:T(8,128)(2,1)S(1)} collective-permute-done((bf16[1040,256]{1,0:T(8,128)(2,1)S(1)}, bf16[1040,256]{1,0:T(8,128)(2,1)S(1)}, u32[]{:S(2)}, u32[]{:S(2)}) %collective-permute-start.83) | collective-permute-done | bytes 532512 | tf_op jit(solution)/shard_map/ppermute | solution.py:35
  935.4 7.6 collective-permute-done.87.refs_2_
  947.8 6.4 copy.784
  958.2 8.0 convert_reduce_fusion
  966.3 7.0 slot_matmul.29
  980.8 6.3 slot_matmul.28
  992.5 22.4 %collective-permute-done.94 = bf16[1040,256]{1,0:T(8,128)(2,1)S(1)} collective-permute-done((bf16[1040,256]{1,0:T(8,128)(2,1)S(1)}, bf16[1040,256]{1,0:T(8,128)(2,1)S(1)}, u32[]{:S(2)}, u32[]{:S(2)}) %collective-permute-start.94) | collective-permute-done | bytes 532512 | tf_op jit(solution)/shard_map/ppermute | solution.py:35
  1021.2 8.8 collective-permute-done.100.refs_3_
  1033.5 6.8 collective-permute-done.99.refs_2_
  1047.9 6.4 copy.785
  1059.0 8.3 convolution_convert_fusion.1
  1067.4 6.4 copy.746
  1077.6 6.8 slot_matmul.23
  1084.8 6.6 copy.783
  1125.0 21.3 %collective-permute-done.59 = bf16[1040,256]{1,0:T(8,128)(2,1)S(1)} collective-permute-done((bf16[1040,256]{1,0:T(8,128)(2,1)S(1)}, bf16[1040,256]{1,0:T(8,128)(2,1)S(1)}, u32[]{:S(2)}, u32[]{:S(2)}) %collective-permute-start.59) | collective-permute-done | bytes 532512 | tf_op jit(solution)/shard_map/ppermute | solution.py:35
  1152.3 8.5 collective-permute-start.117
  1169.8 14.9 collective-permute-done.62
  1225.1 6.5 slot_matmul.31
  1231.6 6.7 collective-permute-start.105
  1243.1 28.7 %collective-permute-done.126 = bf16[1024,512]{0,1:T(8,128)(2,1)} collective-permute-done((bf16[1024,512]{0,1:T(8,128)(2,1)}, bf16[1024,512]{0,1:T(8,128)(2,1)}, u32[]{:S(2)}, u32[]{:S(2)}) %collective-permute-start.126) | collective-permute-done | bytes 1048608 | tf_op jit(solution)/shard_map/ppermute | solution.py:43
  1276.1 18.1 %collective-permute-done.122 = bf16[512,1024]{1,0:T(8,128)(2,1)} collective-permute-done((bf16[512,1024]{1,0:T(8,128)(2,1)}, bf16[512,1024]{1,0:T(8,128)(2,1)}, u32[]{:S(2)}, u32[]{:S(2)}) %collective-permute-start.122) | collective-permute-done | bytes 1048608 | tf_op jit(solution)/shard_map/ppermute | solution.py:43
  1314.6 22.2 %collective-permute-done.114 = bf16[512,768]{1,0:T(8,128)(2,1)} collective-permute-done((bf16[512,768]{1,0:T(8,128)(2,1)}, bf16[512,768]{1,0:T(8,128)(2,1)}, u32[]{:S(2)}, u32[]{:S(2)}) %collective-permute-start.114) | collective-permute-done | bytes 786464 | tf_op jit(solution)/shard_map/ppermute | solution.py:43
  1339.7 9.7 collective-permute-done.116
  1350.4 12.7 collective-permute-done.107
  1368.5 12.8 psum.7
  1403.8 50.8 %collective-permute-done.109 = bf16[1024,256]{1,0:T(8,128)(2,1)} collective-permute-done((bf16[1024,256]{1,0:T(8,128)(2,1)}, bf16[1024,256]{1,0:T(8,128)(2,1)}, u32[]{:S(2)}, u32[]{:S(2)}) %collective-permute-start.109) | collective-permute-done | bytes 524320 | tf_op jit(solution)/shard_map/ppermute | solution.py:47
  1457.1 13.3 collective-permute-done.124
  1482.4 27.3 %collective-permute-done.120 = bf16[512,1024]{1,0:T(8,128)(2,1)} collective-permute-done((bf16[512,1024]{1,0:T(8,128)(2,1)}, bf16[512,1024]{1,0:T(8,128)(2,1)}, u32[]{:S(2)}, u32[]{:S(2)}) %collective-permute-start.120) | collective-permute-done | bytes 1048608 | tf_op jit(solution)/shard_map/ppermute | solution.py:43
  1514.4 12.0 collective-permute-done.112
  (900 shorter events, 588.0 us)
Async XLA Ops:
  7.2 363.5 %all-gather.11.cloned.1.call-start = ((), (), s32[]{:S(2)}) async-start(), calls=%async_computation.8 | async-start | bytes 4718592 | tf_op jit(solution)/shard_map/all_gather | solution.py:252
  10.4 54.1 %collective-permute-start.39 = (bf16[512,768]{1,0:T(8,128)(2,1)S(1)}, bf16[512,768]{1,0:T(8,128)(2,1)S(1)}, u32[]{:S(2)}, u32[]{:S(2)}) collective-permute-start(bf16[512,768]{1,0:T(8,128)(2,1)S(1)} %get-tuple-element.163), channel_id=1, source_target_pairs={{0,4},{4,0},{1,5},{5,1},{2,6},{6,2},{3,7},{7,3},{8,12},{12,8},{9,1... | collective-permute-start | bytes 2359304 | tf_op jit(solution)/shard_map/ppermute | solution.py:43
  13.5 79.2 %collective-permute-start.9 = (bf16[512,768]{1,0:T(8,128)(2,1)}, bf16[512,768]{1,0:T(8,128)(2,1)}, u32[]{:S(2)}, u32[]{:S(2)}) collective-permute-start(bf16[512,768]{1,0:T(8,128)(2,1)} %get-tuple-element.164), channel_id=1, source_target_pairs={{0,4},{4,0},{1,5},{5,1},{2,6},{6,2},{3,7},{7,3},{8,12},{12,8},{9,1... | collective-permute-start | bytes 2359304 | tf_op jit(solution)/shard_map/ppermute | solution.py:43
  65.5 27.2 %collective-permute-start.40 = (bf16[512,768]{1,0:T(8,128)(2,1)}, bf16[512,768]{1,0:T(8,128)(2,1)}, u32[]{:S(2)}, u32[]{:S(2)}) collective-permute-start(bf16[512,768]{1,0:T(8,128)(2,1)} %broadcast_select_fusion.14), channel_id=1, source_target_pairs={{0,8},{8,0},{1,9},{9,1},{2,10},{10,2},{3,11},{11,3},{4,12},{12,4},... | collective-permute-start | bytes 2359304 | tf_op jit(solution)/shard_map/ppermute | solution.py:39
  69.7 157.5 %collective-permute-start.41 = (bf16[256,512]{1,0:T(8,128)(2,1)}, bf16[256,512]{1,0:T(8,128)(2,1)}, u32[]{:S(2)}, u32[]{:S(2)}) collective-permute-start(bf16[256,512]{1,0:T(8,128)(2,1)} %get-tuple-element.179), channel_id=1, source_target_pairs={{0,4},{4,0},{1,5},{5,1},{2,6},{6,2},{3,7},{7,3},{8,12},{12,8},{9,1... | collective-permute-start | bytes 786440 | tf_op jit(solution)/shard_map/ppermute | solution.py:43
  69.7 163.9 %collective-permute-start.11 = (bf16[256,512]{1,0:T(8,128)(2,1)}, bf16[256,512]{1,0:T(8,128)(2,1)S(1)}, u32[]{:S(2)}, u32[]{:S(2)}) collective-permute-start(bf16[256,512]{1,0:T(8,128)(2,1)} %get-tuple-element.180), channel_id=1, source_target_pairs={{0,4},{4,0},{1,5},{5,1},{2,6},{6,2},{3,7},{7,3},{8,12},{12,8},{9,1... | collective-permute-start | bytes 786440 | tf_op jit(solution)/shard_map/ppermute | solution.py:43
  100.0 136.7 %collective-permute-start.1 = (bf16[1040,256]{1,0:T(8,128)(2,1)}, bf16[1040,256]{1,0:T(8,128)(2,1)S(1)}, u32[]{:S(2)}, u32[]{:S(2)}) collective-permute-start(bf16[1040,256]{1,0:T(8,128)(2,1)} %fusion.94), channel_id=1, source_target_pairs={{0,0},{4,8},{8,4},{12,12},{1,1},{5,9},{9,5},{13,13},{2,2},{6,10},{... | collective-permute-start | bytes 1597448 | tf_op jit(solution)/shard_map/ppermute | solution.py:47
  107.0 137.9 %collective-permute-start.56 = (bf16[1024,512]{0,1:T(8,128)(2,1)}, bf16[1024,512]{0,1:T(8,128)(2,1)}, u32[]{:S(2)}, u32[]{:S(2)}) collective-permute-start(bf16[1024,512]{0,1:T(8,128)(2,1)} %get-tuple-element.157), channel_id=1, source_target_pairs={{0,4},{4,0},{1,5},{5,1},{2,6},{6,2},{3,7},{7,3},{8,12},{12,8},{9,1... | collective-permute-start | bytes 3145736 | tf_op jit(solution)/shard_map/ppermute | solution.py:43
  116.1 274.3 %all-gather.13.cloned.1.call-start = ((), (), s32[]{:S(2)}) async-start(), calls=%async_computation.9 | async-start | bytes 1572864 | tf_op jit(solution)/shard_map/all_gather | solution.py:252
  118.3 124.7 %collective-permute-start.54 = (bf16[512,1024]{1,0:T(8,128)(2,1)}, bf16[512,1024]{1,0:T(8,128)(2,1)S(1)}, u32[]{:S(2)}, u32[]{:S(2)}) collective-permute-start(bf16[512,1024]{1,0:T(8,128)(2,1)} %get-tuple-element.160), channel_id=1, source_target_pairs={{0,4},{4,0},{1,5},{5,1},{2,6},{6,2},{3,7},{7,3},{8,12},{12,8},{9,1... | collective-permute-start | bytes 3145736 | tf_op jit(solution)/shard_map/ppermute | solution.py:43
  233.7 56.0 %collective-permute-start.24 = (bf16[512,1024]{1,0:T(8,128)(2,1)}, bf16[512,1024]{1,0:T(8,128)(2,1)}, u32[]{:S(2)}, u32[]{:S(2)}) collective-permute-start(bf16[512,1024]{1,0:T(8,128)(2,1)} %get-tuple-element.161), channel_id=1, source_target_pairs={{0,4},{4,0},{1,5},{5,1},{2,6},{6,2},{3,7},{7,3},{8,12},{12,8},{9,1... | collective-permute-start | bytes 3145736 | tf_op jit(solution)/shard_map/ppermute | solution.py:43
  236.7 33.3 %collective-permute-start.5 = (bf16[1040,256]{1,0:T(8,128)(2,1)S(1)}, bf16[1040,256]{1,0:T(8,128)(2,1)S(1)}, u32[]{:S(2)}, u32[]{:S(2)}) collective-permute-start(bf16[1040,256]{1,0:T(8,128)(2,1)S(1)} %collective-permute-done.1.refs_0_), channel_id=1, source_target_pairs={{0,8},{8,0},{1,9},{9,1},{2,10},{10,2},{3,11},{11,3},{4,12},{12,4},... | collective-permute-start | bytes 1597448 | tf_op jit(solution)/shard_map/ppermute | solution.py:39
  237.6 30.4 %collective-permute-start.4 = (bf16[1040,256]{1,0:T(8,128)(2,1)S(1)}, bf16[1040,256]{1,0:T(8,128)(2,1)S(1)}, u32[]{:S(2)}, u32[]{:S(2)}) collective-permute-start(bf16[1040,256]{1,0:T(8,128)(2,1)S(1)} %collective-permute-done.1.refs_0_), channel_id=1, source_target_pairs={{0,3},{1,2},{2,1},{3,0},{4,7},{5,6},{6,5},{7,4},{8,11},{9,10},{10,... | collective-permute-start | bytes 1597448 | tf_op jit(solution)/shard_map/ppermute | solution.py:35
  243.0 234.0 %all-gather.15.cloned.1.call-start = ((), (), s32[]{:S(2)}) async-start(), calls=%async_computation.10 | async-start | bytes 6291456 | tf_op jit(solution)/shard_map/all_gather | solution.py:252
  243.1 43.7 %collective-permute-start.3 = (bf16[1040,256]{1,0:T(8,128)(2,1)S(1)}, bf16[1040,256]{1,0:T(8,128)(2,1)S(1)}, u32[]{:S(2)}, u32[]{:S(2)}) collective-permute-start(bf16[1040,256]{1,0:T(8,128)(2,1)S(1)} %collective-permute-done.1.refs_0_), channel_id=1, source_target_pairs={{0,2},{1,3},{2,0},{3,1},{4,6},{5,7},{6,4},{7,5},{8,10},{9,11},{10,... | collective-permute-start | bytes 1597448 | tf_op jit(solution)/shard_map/ppermute | solution.py:35
  245.0 47.0 %collective-permute-start.55 = (bf16[512,1024]{1,0:T(8,128)(2,1)S(1)}, bf16[512,1024]{1,0:T(8,128)(2,1)S(1)}, u32[]{:S(2)}, u32[]{:S(2)}) collective-permute-start(bf16[512,1024]{1,0:T(8,128)(2,1)S(1)} %broadcast_select_fusion.8), channel_id=1, source_target_pairs={{0,8},{8,0},{1,9},{9,1},{2,10},{10,2},{3,11},{11,3},{4,12},{12,4},... | collective-permute-start | bytes 3145736 | tf_op jit(solution)/shard_map/ppermute | solution.py:39
  286.7 61.5 %collective-permute-start = (f32[1024,256]{1,0:T(8,128)}, f32[1024,256]{1,0:T(8,128)S(1)}, u32[]{:S(2)}, u32[]{:S(2)}) collective-permute-start(f32[1024,256]{1,0:T(8,128)} %param.16), channel_id=1, source_target_pairs={{0,0},{4,8},{8,4},{12,12},{1,1},{5,9},{9,5},{13,13},{2,2},{6,10},{... | collective-permute-start | bytes 3145736 | tf_op jit(solution)/shard_map/ppermute | solution.py:47
  289.7 73.4 %collective-permute-start.26 = (bf16[1024,512]{0,1:T(8,128)(2,1)}, bf16[1024,512]{0,1:T(8,128)(2,1)}, u32[]{:S(2)}, u32[]{:S(2)}) collective-permute-start(bf16[1024,512]{0,1:T(8,128)(2,1)} %get-tuple-element.158), channel_id=1, source_target_pairs={{0,4},{4,0},{1,5},{5,1},{2,6},{6,2},{3,7},{7,3},{8,12},{12,8},{9,1... | collective-permute-start | bytes 3145736 | tf_op jit(solution)/shard_map/ppermute | solution.py:43
  291.6 71.5 %collective-permute-start.57 = (bf16[1024,512]{0,1:T(8,128)(2,1)}, bf16[1024,512]{0,1:T(8,128)(2,1)}, u32[]{:S(2)}, u32[]{:S(2)}) collective-permute-start(bf16[1024,512]{0,1:T(8,128)(2,1)} %broadcast_select_fusion.4), channel_id=1, source_target_pairs={{0,8},{8,0},{1,9},{9,1},{2,10},{10,2},{3,11},{11,3},{4,12},{12,4},... | collective-permute-start | bytes 3145736 | tf_op jit(solution)/shard_map/ppermute | solution.py:39
  295.4 71.5 %collective-permute-start.25 = (bf16[512,1024]{1,0:T(8,128)(2,1)}, bf16[512,1024]{1,0:T(8,128)(2,1)}, u32[]{:S(2)}, u32[]{:S(2)}) collective-permute-start(bf16[512,1024]{1,0:T(8,128)(2,1)} %get-tuple-element.159), channel_id=1, source_target_pairs={{0,8},{8,0},{1,9},{9,1},{2,10},{10,2},{3,11},{11,3},{4,12},{12,4},... | collective-permute-start | bytes 3145736 | tf_op jit(solution)/shard_map/ppermute | solution.py:39
  366.8 29.6 %collective-permute-start.27 = (bf16[1024,512]{0,1:T(8,128)(2,1)S(1)}, bf16[1024,512]{0,1:T(8,128)(2,1)}, u32[]{:S(2)}, u32[]{:S(2)}) collective-permute-start(bf16[1024,512]{0,1:T(8,128)(2,1)S(1)} %get-tuple-element.156), channel_id=1, source_target_pairs={{0,8},{8,0},{1,9},{9,1},{2,10},{10,2},{3,11},{11,3},{4,12},{12,4},... | collective-permute-start | bytes 3145736 | tf_op jit(solution)/shard_map/ppermute | solution.py:39
  370.1 117.5 %all-gather.17.cloned.1.call-start = ((), (), s32[]{:S(2)}) async-start(), calls=%async_computation.11 | async-start | bytes 6291456 | tf_op jit(solution)/shard_map/all_gather | solution.py:252
  403.7 156.2 %all-gather.19.cloned.1.call-start = ((), (), s32[]{:S(2)}) async-start(), calls=%async_computation.12 | async-start | bytes 4718592 | tf_op jit(solution)/shard_map/all_gather | solution.py:252
  410.5 25.6 %collective-permute-start.15 = (bf16[1040,256]{1,0:T(8,128)(2,1)S(1)}, bf16[1040,256]{1,0:T(8,128)(2,1)S(1)}, u32[]{:S(2)}, u32[]{:S(2)}) collective-permute-start(bf16[1040,256]{1,0:T(8,128)(2,1)S(1)} %get-tuple-element.148), channel_id=1, source_target_pairs={{0,2},{1,3},{2,0},{3,1},{4,6},{5,7},{6,4},{7,5},{8,10},{9,11},{10,... | collective-permute-start | bytes 1597448 | tf_op jit(solution)/shard_map/ppermute | solution.py:35
  441.4 183.1 %all-gather.21.cloned.1.call-start = ((), (), s32[]{:S(2)}) async-start(), calls=%async_computation.13 | async-start | bytes 1572864 | tf_op jit(solution)/shard_map/all_gather | solution.py:252
  497.7 52.7 %collective-permute-start.63 = (f32[1024,256]{1,0:T(8,128)}, f32[1024,256]{1,0:T(8,128)}, u32[]{:S(2)}, u32[]{:S(2)}) collective-permute-start(f32[1024,256]{1,0:T(8,128)} %param.17), channel_id=1, source_target_pairs={{0,0},{4,8},{8,4},{12,12},{1,1},{5,9},{9,5},{13,13},{2,2},{6,10},{... | collective-permute-start | bytes 3145736 | tf_op jit(solution)/shard_map/ppermute | solution.py:47
  501.1 142.5 %all-gather.25.cloned.1.call-start = ((), (), s32[]{:S(2)}) async-start(), calls=%async_computation.15 | async-start | bytes 6291456 | tf_op jit(solution)/shard_map/all_gather | solution.py:252
  513.7 35.5 %collective-permute-start.30 = (bf16[1040,256]{1,0:T(8,128)(2,1)S(1)}, bf16[1040,256]{1,0:T(8,128)(2,1)S(1)}, u32[]{:S(2)}, u32[]{:S(2)}) collective-permute-start(bf16[1040,256]{1,0:T(8,128)(2,1)S(1)} %get-tuple-element.145), channel_id=1, source_target_pairs={{0,2},{1,3},{2,0},{3,1},{4,6},{5,7},{6,4},{7,5},{8,10},{9,11},{10,... | collective-permute-start | bytes 1597448 | tf_op jit(solution)/shard_map/ppermute | solution.py:35
  551.9 79.0 %collective-permute-start.66 = (bf16[1024,256]{1,0:T(8,128)(2,1)S(1)}, bf16[1024,256]{1,0:T(8,128)(2,1)S(1)}, u32[]{:S(2)}, u32[]{:S(2)}) collective-permute-start(bf16[1024,256]{1,0:T(8,128)(2,1)S(1)} %multiply_convert_fusion.5.refs_0_), channel_id=1, source_target_pairs={{0,3},{1,2},{2,1},{3,0},{4,7},{5,6},{6,5},{7,4},{8,11},{9,10},{10,... | collective-permute-start | bytes 1572872 | tf_op jit(solution)/shard_map/ppermute | solution.py:35
  552.0 79.3 %collective-permute-start.65 = (bf16[1024,256]{1,0:T(8,128)(2,1)S(1)}, bf16[1024,256]{1,0:T(8,128)(2,1)}, u32[]{:S(2)}, u32[]{:S(2)}) collective-permute-start(bf16[1024,256]{1,0:T(8,128)(2,1)S(1)} %multiply_convert_fusion.5.refs_0_), channel_id=1, source_target_pairs={{0,2},{1,3},{2,0},{3,1},{4,6},{5,7},{6,4},{7,5},{8,10},{9,11},{10,... | collective-permute-start | bytes 1572872 | tf_op jit(solution)/shard_map/ppermute | solution.py:35
  554.1 34.2 %collective-permute-start.33 = (bf16[1040,256]{1,0:T(8,128)(2,1)S(1)}, bf16[1040,256]{1,0:T(8,128)(2,1)}, u32[]{:S(2)}, u32[]{:S(2)}) collective-permute-start(bf16[1040,256]{1,0:T(8,128)(2,1)S(1)} %fusion.96.refs_0_), channel_id=1, source_target_pairs={{0,2},{1,3},{2,0},{3,1},{4,6},{5,7},{6,4},{7,5},{8,10},{9,11},{10,... | collective-permute-start | bytes 1597448 | tf_op jit(solution)/shard_map/ppermute | solution.py:35
  559.6 135.7 %all-gather.23.cloned.1.call-start = ((), (), s32[]{:S(2)}) async-start(), calls=%async_computation.14 | async-start | bytes 6291456 | tf_op jit(solution)/shard_map/all_gather | solution.py:252
  564.5 35.2 %collective-permute-start.34 = (bf16[1040,256]{1,0:T(8,128)(2,1)S(1)}, bf16[1040,256]{1,0:T(8,128)(2,1)S(1)}, u32[]{:S(2)}, u32[]{:S(2)}) collective-permute-start(bf16[1040,256]{1,0:T(8,128)(2,1)S(1)} %fusion.96.refs_0_), channel_id=1, source_target_pairs={{0,3},{1,2},{2,1},{3,0},{4,7},{5,6},{6,5},{7,4},{8,11},{9,10},{10,... | collective-permute-start | bytes 1597448 | tf_op jit(solution)/shard_map/ppermute | solution.py:35
  574.6 26.7 %collective-permute-start.35 = (bf16[1040,256]{1,0:T(8,128)(2,1)S(1)}, bf16[1040,256]{1,0:T(8,128)(2,1)S(1)}, u32[]{:S(2)}, u32[]{:S(2)}) collective-permute-start(bf16[1040,256]{1,0:T(8,128)(2,1)S(1)} %fusion.96.refs_0_), channel_id=1, source_target_pairs={{0,8},{8,0},{1,9},{9,1},{2,10},{10,2},{3,11},{11,3},{4,12},{12,4},... | collective-permute-start | bytes 1597448 | tf_op jit(solution)/shard_map/ppermute | solution.py:39
  601.4 30.1 %collective-permute-start.64 = (bf16[1024,256]{1,0:T(8,128)(2,1)S(1)}, bf16[1024,256]{1,0:T(8,128)(2,1)}, u32[]{:S(2)}, u32[]{:S(2)}) collective-permute-start(bf16[1024,256]{1,0:T(8,128)(2,1)S(1)} %multiply_convert_fusion.5.refs_0_), channel_id=1, source_target_pairs={{0,1},{1,0},{2,3},{3,2},{4,5},{5,4},{6,7},{7,6},{8,9},{9,8},{10,11... | collective-permute-start | bytes 1572872 | tf_op jit(solution)/shard_map/ppermute | solution.py:35
  630.4 33.4 %collective-permute-start.43 = (bf16[4,1040,256]{2,1,0:T(8,128)(2,1)}, bf16[4,1040,256]{2,1,0:T(8,128)(2,1)}, u32[]{:S(2)}, u32[]{:S(2)}) collective-permute-start(bf16[4,1040,256]{2,1,0:T(8,128)(2,1)} %slot_matmul.21), channel_id=1, source_target_pairs={{0,8},{8,0},{1,9},{9,1},{2,10},{10,2},{3,11},{11,3},{4,12},{12,4},... | collective-permute-start | bytes 6389768 | tf_op jit(solution)/shard_map/ppermute | solution.py:39
  633.4 517.1 %reduce-scatter.15.cloned.1.call-start = ((), (), s32[]{:S(2)}) async-start(), calls=%async_computation.19 | async-start | bytes 1572864 | tf_op jit(solution)/shard_map/reduce_scatter | solution.py:258
  753.3 25.4 %collective-permute-start.73 = (bf16[1040,256]{1,0:T(8,128)(2,1)S(1)}, bf16[1040,256]{1,0:T(8,128)(2,1)S(1)}, u32[]{:S(2)}, u32[]{:S(2)}) collective-permute-start(bf16[1040,256]{1,0:T(8,128)(2,1)S(1)} %get-tuple-element.136), channel_id=1, source_target_pairs={{0,2},{1,3},{2,0},{3,1},{4,6},{5,7},{6,4},{7,5},{8,10},{9,11},{10,... | collective-permute-start | bytes 1597448 | tf_op jit(solution)/shard_map/ppermute | solution.py:35
  823.2 337.6 %reduce-scatter.23.cloned.1.call-start = ((), (), s32[]{:S(2)}) async-start(), calls=%async_computation.23 | async-start | bytes 6291456 | tf_op jit(solution)/shard_map/reduce_scatter | solution.py:258
  838.0 325.5 %reduce-scatter.19.cloned.1.call-start = ((), (), s32[]{:S(2)}) async-start(), calls=%async_computation.21 | async-start | bytes 6291456 | tf_op jit(solution)/shard_map/reduce_scatter | solution.py:258
  880.4 314.2 %reduce-scatter.11.cloned.1.call-start = ((), (), s32[]{:S(2)}) async-start(), calls=%async_computation.17 | async-start | bytes 4718592 | tf_op jit(solution)/shard_map/reduce_scatter | solution.py:258
  927.3 26.8 %collective-permute-start.89 = (bf16[1024,256]{1,0:T(8,128)(2,1)S(1)}, bf16[1024,256]{1,0:T(8,128)(2,1)S(1)}, u32[]{:S(2)}, u32[]{:S(2)}) collective-permute-start(bf16[1024,256]{1,0:T(8,128)(2,1)S(1)} %convert_element_type.1066.refs_0_), channel_id=1, source_target_pairs={{0,8},{8,0},{1,9},{9,1},{2,10},{10,2},{3,11},{11,3},{4,12},{12,4},... | collective-permute-start | bytes 1572872 | tf_op jit(solution)/shard_map/ppermute | solution.py:39
  978.6 328.4 %reduce-scatter.13.cloned.1.call-start = ((), (), s32[]{:S(2)}) async-start(), calls=%async_computation.18 | async-start | bytes 1572864 | tf_op jit(solution)/shard_map/reduce_scatter | solution.py:258
  1059.0 304.4 %reduce-scatter.21.cloned.1.call-start = ((), (), s32[]{:S(2)}) async-start(), calls=%async_computation.22 | async-start | bytes 6291456 | tf_op jit(solution)/shard_map/reduce_scatter | solution.py:258
  1073.8 311.3 %reduce-scatter.17.cloned.1.call-start = ((), (), s32[]{:S(2)}) async-start(), calls=%async_computation.20 | async-start | bytes 6291456 | tf_op jit(solution)/shard_map/reduce_scatter | solution.py:258
  1119.1 279.2 %reduce-scatter.9.cloned.1.call-start = ((), (), s32[]{:S(2)}) async-start(), calls=%async_computation.16 | async-start | bytes 4718592 | tf_op jit(solution)/shard_map/reduce_scatter | solution.py:258
  1121.0 25.3 %collective-permute-start.59 = (bf16[1040,256]{1,0:T(8,128)(2,1)S(1)}, bf16[1040,256]{1,0:T(8,128)(2,1)S(1)}, u32[]{:S(2)}, u32[]{:S(2)}) collective-permute-start(bf16[1040,256]{1,0:T(8,128)(2,1)S(1)} %get-tuple-element.137), channel_id=1, source_target_pairs={{0,1},{1,0},{2,3},{3,2},{4,5},{5,4},{6,7},{7,6},{8,9},{9,8},{10,11... | collective-permute-start | bytes 1597448 | tf_op jit(solution)/shard_map/ppermute | solution.py:35
  1121.6 25.5 %collective-permute-start.60 = (bf16[1040,256]{1,0:T(8,128)(2,1)S(1)}, bf16[1040,256]{1,0:T(8,128)(2,1)S(1)}, u32[]{:S(2)}, u32[]{:S(2)}) collective-permute-start(bf16[1040,256]{1,0:T(8,128)(2,1)S(1)} %get-tuple-element.139), channel_id=1, source_target_pairs={{0,2},{1,3},{2,0},{3,1},{4,6},{5,7},{6,4},{7,5},{8,10},{9,11},{10,... | collective-permute-start | bytes 1597448 | tf_op jit(solution)/shard_map/ppermute | solution.py:35
  1148.5 36.2 %collective-permute-start.62 = (f32[1024,256]{1,0:T(8,128)}, f32[1024,256]{1,0:T(8,128)}, u32[]{:S(2)}, u32[]{:S(2)}) collective-permute-start(f32[1024,256]{1,0:T(8,128)} %fusion.77), channel_id=1, source_target_pairs={{0,0},{4,8},{8,4},{12,12},{1,1},{5,9},{9,5},{13,13},{2,2},{6,10},{... | collective-permute-start | bytes 3145736 | tf_op jit(solution)/shard_map/ppermute | solution.py:47
  1189.7 82.1 %collective-permute-start.126 = (bf16[1024,512]{0,1:T(8,128)(2,1)}, bf16[1024,512]{0,1:T(8,128)(2,1)}, u32[]{:S(2)}, u32[]{:S(2)}) collective-permute-start(bf16[1024,512]{0,1:T(8,128)(2,1)} %bitcast_select_fusion), channel_id=1, source_target_pairs={{0,4},{4,0},{1,5},{5,1},{2,6},{6,2},{3,7},{7,3},{8,12},{12,8},{9,1... | collective-permute-start | bytes 3145736 | tf_op jit(solution)/shard_map/ppermute | solution.py:43
  1190.9 103.3 %collective-permute-start.122 = (bf16[512,1024]{1,0:T(8,128)(2,1)}, bf16[512,1024]{1,0:T(8,128)(2,1)}, u32[]{:S(2)}, u32[]{:S(2)}) collective-permute-start(bf16[512,1024]{1,0:T(8,128)(2,1)} %bitcast_select_fusion.4), channel_id=1, source_target_pairs={{0,4},{4,0},{1,5},{5,1},{2,6},{6,2},{3,7},{7,3},{8,12},{12,8},{9,1... | collective-permute-start | bytes 3145736 | tf_op jit(solution)/shard_map/ppermute | solution.py:43
  1196.9 101.1 %collective-permute-start.113 = (bf16[512,768]{1,0:T(8,128)(2,1)}, bf16[512,768]{1,0:T(8,128)(2,1)}, u32[]{:S(2)}, u32[]{:S(2)}) collective-permute-start(bf16[512,768]{1,0:T(8,128)(2,1)} %select_bitcast_fusion.12), channel_id=1, source_target_pairs={{0,8},{8,0},{1,9},{9,1},{2,10},{10,2},{3,11},{11,3},{4,12},{12,4},... | collective-permute-start | bytes 2359304 | tf_op jit(solution)/shard_map/ppermute | solution.py:39
  1200.1 203.8 %collective-permute-start.97 = (f32[1024,256]{1,0:T(8,128)}, f32[1024,256]{1,0:T(8,128)}, u32[]{:S(2)}, u32[]{:S(2)}) collective-permute-start(f32[1024,256]{1,0:T(8,128)} %copy-done.110), channel_id=1, source_target_pairs={{0,0},{4,8},{8,4},{12,12},{1,1},{5,9},{9,5},{13,13},{2,2},{6,10},{... | collective-permute-start | bytes 3145736 | tf_op jit(solution)/shard_map/ppermute | solution.py:47
  1231.6 77.4 %collective-permute-start.105 = (bf16[4,1040,256]{2,1,0:T(8,128)(2,1)}, bf16[4,1040,256]{2,1,0:T(8,128)(2,1)}, u32[]{:S(2)}, u32[]{:S(2)}) collective-permute-start(bf16[4,1040,256]{2,1,0:T(8,128)(2,1)} %slot_matmul.31), channel_id=1, source_target_pairs={{0,8},{8,0},{1,9},{9,1},{2,10},{10,2},{3,11},{11,3},{4,12},{12,4},... | collective-permute-start | bytes 6389768 | tf_op jit(solution)/shard_map/ppermute | solution.py:39
  1299.1 37.7 %collective-permute-start.114 = (bf16[512,768]{1,0:T(8,128)(2,1)}, bf16[512,768]{1,0:T(8,128)(2,1)}, u32[]{:S(2)}, u32[]{:S(2)}) collective-permute-start(bf16[512,768]{1,0:T(8,128)(2,1)} %bitcast_select_fusion.8), channel_id=1, source_target_pairs={{0,4},{4,0},{1,5},{5,1},{2,6},{6,2},{3,7},{7,3},{8,12},{12,8},{9,1... | collective-permute-start | bytes 2359304 | tf_op jit(solution)/shard_map/ppermute | solution.py:43
  1311.9 38.5 %collective-permute-start.106 = (bf16[1040,256]{1,0:T(8,128)(2,1)S(1)}, bf16[1040,256]{1,0:T(8,128)(2,1)S(1)}, u32[]{:S(2)}, u32[]{:S(2)}) collective-permute-start(bf16[1040,256]{1,0:T(8,128)(2,1)S(1)} %get-tuple-element.125), channel_id=1, source_target_pairs={{0,1},{1,0},{2,3},{3,2},{4,5},{5,4},{6,7},{7,6},{8,9},{9,8},{10,11... | collective-permute-start | bytes 1597448 | tf_op jit(solution)/shard_map/ppermute | solution.py:35
  1312.5 37.9 %collective-permute-start.108 = (bf16[1040,256]{1,0:T(8,128)(2,1)S(1)}, bf16[1040,256]{1,0:T(8,128)(2,1)S(1)}, u32[]{:S(2)}, u32[]{:S(2)}) collective-permute-start(bf16[1040,256]{1,0:T(8,128)(2,1)S(1)} %get-tuple-element.126), channel_id=1, source_target_pairs={{0,3},{1,2},{2,1},{3,0},{4,7},{5,6},{6,5},{7,4},{8,11},{9,10},{10,... | collective-permute-start | bytes 1597448 | tf_op jit(solution)/shard_map/ppermute | solution.py:35
  1314.2 48.9 %collective-permute-start.107 = (bf16[1040,256]{1,0:T(8,128)(2,1)S(1)}, bf16[1040,256]{1,0:T(8,128)(2,1)S(1)}, u32[]{:S(2)}, u32[]{:S(2)}) collective-permute-start(bf16[1040,256]{1,0:T(8,128)(2,1)S(1)} %get-tuple-element.127), channel_id=1, source_target_pairs={{0,2},{1,3},{2,0},{3,1},{4,6},{5,7},{6,4},{7,5},{8,10},{9,11},{10,... | collective-permute-start | bytes 1597448 | tf_op jit(solution)/shard_map/ppermute | solution.py:35
  1366.0 27.5 %collective-permute-start.123 = (bf16[1024,512]{0,1:T(8,128)(2,1)}, bf16[1024,512]{0,1:T(8,128)(2,1)S(1)}, u32[]{:S(2)}, u32[]{:S(2)}) collective-permute-start(bf16[1024,512]{0,1:T(8,128)(2,1)} %select_bitcast_fusion.1), channel_id=1, source_target_pairs={{0,8},{8,0},{1,9},{9,1},{2,10},{10,2},{3,11},{11,3},{4,12},{12,4},... | collective-permute-start | bytes 3145736 | tf_op jit(solution)/shard_map/ppermute | solution.py:39
  1388.9 65.8 %collective-permute-start.109 = (bf16[1024,256]{1,0:T(8,128)(2,1)}, bf16[1024,256]{1,0:T(8,128)(2,1)}, u32[]{:S(2)}, u32[]{:S(2)}) collective-permute-start(bf16[1024,256]{1,0:T(8,128)(2,1)} %get-tuple-element.151), channel_id=1, source_target_pairs={{0,0},{4,8},{8,4},{12,12},{1,1},{5,9},{9,5},{13,13},{2,2},{6,10},{... | collective-permute-start | bytes 1572872 | tf_op jit(solution)/shard_map/ppermute | solution.py:47
  1394.6 75.8 %collective-permute-start.124 = (bf16[1024,512]{0,1:T(8,128)(2,1)}, bf16[1024,512]{0,1:T(8,128)(2,1)}, u32[]{:S(2)}, u32[]{:S(2)}) collective-permute-start(bf16[1024,512]{0,1:T(8,128)(2,1)} %bitcast_select_fusion.2), channel_id=1, source_target_pairs={{0,4},{4,0},{1,5},{5,1},{2,6},{6,2},{3,7},{7,3},{8,12},{12,8},{9,1... | collective-permute-start | bytes 3145736 | tf_op jit(solution)/shard_map/ppermute | solution.py:43
  1399.9 72.6 %collective-permute-start.111 = (bf16[512,768]{1,0:T(8,128)(2,1)S(1)}, bf16[512,768]{1,0:T(8,128)(2,1)S(1)}, u32[]{:S(2)}, u32[]{:S(2)}) collective-permute-start(bf16[512,768]{1,0:T(8,128)(2,1)S(1)} %select_bitcast_fusion.13), channel_id=1, source_target_pairs={{0,8},{8,0},{1,9},{9,1},{2,10},{10,2},{3,11},{11,3},{4,12},{12,4},... | collective-permute-start | bytes 2359304 | tf_op jit(solution)/shard_map/ppermute | solution.py:39
  1401.6 108.1 %collective-permute-start.120 = (bf16[512,1024]{1,0:T(8,128)(2,1)}, bf16[512,1024]{1,0:T(8,128)(2,1)}, u32[]{:S(2)}, u32[]{:S(2)}) collective-permute-start(bf16[512,1024]{1,0:T(8,128)(2,1)} %bitcast_select_fusion.6), channel_id=1, source_target_pairs={{0,4},{4,0},{1,5},{5,1},{2,6},{6,2},{3,7},{7,3},{8,12},{12,8},{9,1... | collective-permute-start | bytes 3145736 | tf_op jit(solution)/shard_map/ppermute | solution.py:43
  1473.6 52.8 %collective-permute-start.112 = (bf16[512,768]{1,0:T(8,128)(2,1)}, bf16[512,768]{1,0:T(8,128)(2,1)S(1)}, u32[]{:S(2)}, u32[]{:S(2)}) collective-permute-start(bf16[512,768]{1,0:T(8,128)(2,1)} %bitcast_select_fusion.10), channel_id=1, source_target_pairs={{0,4},{4,0},{1,5},{5,1},{2,6},{6,2},{3,7},{7,3},{8,12},{12,8},{9,1... | collective-permute-start | bytes 2359304 | tf_op jit(solution)/shard_map/ppermute | solution.py:43
  (252 other events, 3262.7 us)
Sparse Core Ops, SparseCore 0:
  116.2 46.7 all-gather.10
  243.1 19.4 all-gather.12
  370.2 54.9 all-gather.14
  426.7 56.7 all-gather.16
  484.8 44.9 all-gather.18
  531.2 21.3 all-gather.20
  559.7 56.2 all-gather.24
  633.5 54.2 all-gather.22
  823.3 17.9 reduce-scatter.14
  843.6 54.3 reduce-scatter.22
  900.2 54.3 reduce-scatter.18
  978.7 40.6 reduce-scatter.10
  1059.1 17.6 reduce-scatter.12
  1079.0 54.2 reduce-scatter.20
  1136.1 54.3 reduce-scatter.16
  1243.2 41.5 reduce-scatter.8

commit v2 on v1

v2 whole, which is shorter than its diff:
```python
import functools
import math

import jax
import jax.numpy as jnp
from jax import lax
from jax.experimental import pallas as pl
from jax.experimental.pallas import tpu as pltpu
from jax.sharding import Mesh
from jax.sharding import PartitionSpec as P

HEADS = 16
HEAD_DIM = 128
PAD = 16
LANES = 128
CHUNKS = 1
MIB = 2**20

norm_eps = 1e-05
masked_score = -1e30

F32 = jnp.float32
BF16 = jnp.bfloat16


def gelu_tanh(value):
    return jax.nn.gelu(value, approximate=True)


def after(value, *earlier):
    return lax.optimization_barrier((value, earlier))[0]


def ring_size():
    return lax.axis_size("t")


def ring(value, k):
    return lax.ppermute(value, "t", [(i, i ^ k) for i in range(ring_size())])


def partner(value):
    return lax.ppermute(value, "c", [(0, 1), (1, 0)])


def swap_roles(value):
    same = lax.axis_index("c") == lax.axis_index("x")
    return jnp.where(same, value, lax.ppermute(value, ("c", "x"), [(1, 2), (2, 1)]))


def block_index():
    return lax.axis_index("t") * 2 + lax.axis_index("c")


def slot_blocks():
    return (jnp.arange(2 * ring_size(), dtype=jnp.int32) ^ block_index()).astype(jnp.int32)


def gather_slots(value):
    if ring_size() == 4:
        far = ring(value, 2)
        mine = [value, ring(value, 1), far, ring(far, 1)]
    else:
        mine = [value] + [ring(value, k) for k in range(1, ring_size())]
    return [v for m in mine for v in (m, partner(m))]


def pair_blocks(mine, other):
    got = partner(other)
    pair = mine.astype(F32) + got.astype(F32)
    return [pair[0]] + [pair[k].astype(BF16) for k in range(1, ring_size())]


def ring_sum(pair):
    if ring_size() == 4:
        far = pair[2].astype(F32) + ring(pair[3], 1).astype(F32)
        got = [ring(pair[1], 1), ring(far.astype(BF16), 2)]
    else:
        got = [ring(pair[k], k) for k in range(1, ring_size())]
    return added([pair[0]] + [g.astype(F32) for g in got])


def whole(shape):
    return pl.BlockSpec(shape, lambda *_: (0,) * len(shape))


def assemble_norm_kernel(slots, width, blocks_ref, *refs):
    shards = refs[:slots]
    means_ref, spread_ref, gain_ref, shift_ref, own_ref = refs[slots : slots + 5]
    out_ref, centred_ref, inverse_ref = refs[slots + 5 :]
    f = shards[0].shape[1]
    offsets = lax.dot_general(
        means_ref[0].astype(BF16),
        spread_ref[...],
        (((0,), (0,)), ((), ())),
        preferred_element_type=F32,
    )
    values = [shards[s][...].astype(F32) + offsets[:, s * f : (s + 1) * f] for s in range(slots)]
    total = values[0]
    for v in values[1:]:
        total = total + v
    mean = jnp.sum(total, axis=1, keepdims=True) / width
    values = [v - mean for v in values]
    squares = values[0] * values[0]
    for v in values[1:]:
        squares = squares + v * v
    inverse = lax.rsqrt(jnp.sum(squares, axis=1, keepdims=True) / width + norm_eps)
    for s in range(slots):
        block = blocks_ref[s]
        normed = values[s] * inverse * gain_ref[s] + shift_ref[s]
        out_ref[:, pl.ds(pl.multiple_of(block * f, f), f)] = normed.astype(BF16)
    centred_ref[...] = (own_ref[...] - mean) * inverse
    inverse_ref[...] = jnp.broadcast_to(inverse, inverse_ref.shape)


def assemble_norm(shards, own, gain, shift):
    slots = len(shards)
    tokens, f = own.shape
    width = slots * f
    groups = tokens // LANES
    means = jnp.stack([s[tokens : tokens + groups, :LANES] for s in shards], axis=1).astype(F32)
    spread = jnp.repeat(jnp.eye(slots, dtype=BF16), f, axis=1)
    tile = LANES
    return pl.pallas_call(
        functools.partial(assemble_norm_kernel, slots, width),
        grid_spec=pltpu.PrefetchScalarGridSpec(
            num_scalar_prefetch=1,
            grid=(tokens // tile,),
            in_specs=[pl.BlockSpec((tile, f), lambda g, b: (g, 0))] * slots
            + [
                pl.BlockSpec((1, slots, LANES), lambda g, b: (g, 0, 0)),
                whole((slots, width)),
                whole((slots, 1, f)),
                whole((slots, 1, f)),
                pl.BlockSpec((tile, f), lambda g, b: (g, 0)),
            ],
            out_specs=[
                pl.BlockSpec((tile, width), lambda g, b: (g, 0)),
                pl.BlockSpec((tile, f), lambda g, b: (g, 0)),
                pl.BlockSpec((tile, LANES), lambda g, b: (g, 0)),
            ],
        ),
        out_shape=[
            jax.ShapeDtypeStruct((tokens, width), BF16),
            jax.ShapeDtypeStruct((tokens, f), F32),
            jax.ShapeDtypeStruct((tokens, LANES), F32),
        ],
        compiler_params=pltpu.CompilerParams(vmem_limit_bytes=24 * MIB),
        cost_estimate=pl.CostEstimate(
            flops=12 * tokens * width, bytes_accessed=6 * tokens * width, transcendentals=tokens
        ),
        name="assemble_norm",
    )(
        slot_blocks(),
        *shards,
        means,
        spread,
        gain.reshape(slots, 1, f),
        shift.reshape(slots, 1, f),
        own,
    )


def assemble_kernel(slots, blocks_ref, *refs):
    out_ref = refs[slots]
    f = refs[0].shape[1]
    for s in range(slots):
        out_ref[:, pl.ds(pl.multiple_of(blocks_ref[s] * f, f), f)] = refs[s][...]


def assemble(shards):
    slots = len(shards)
    tokens, f = shards[0].shape
    tile = min(tokens, 256)
    return pl.pallas_call(
        functools.partial(assemble_kernel, slots),
        grid_spec=pltpu.PrefetchScalarGridSpec(
            num_scalar_prefetch=1,
            grid=(tokens // tile,),
            in_specs=[pl.BlockSpec((tile, f), lambda g, b: (g, 0))] * slots,
            out_specs=pl.BlockSpec((tile, slots * f), lambda g, b: (g, 0)),
        ),
        out_shape=jax.ShapeDtypeStruct((tokens, slots * f), BF16),
        compiler_params=pltpu.CompilerParams(vmem_limit_bytes=24 * MIB),
        cost_estimate=pl.CostEstimate(
            flops=0, bytes_accessed=4 * tokens * slots * f, transcendentals=0
        ),
        name="assemble",
    )(slot_blocks(), *shards)


def pack_kernel(turned, *refs):
    out_ref = refs[-1]
    at = 0
    for turn, ref in zip(turned, refs):
        value = ref[0].T if turn else ref[0]
        out_ref[:, at : at + value.shape[1]] = value.astype(BF16)
        at += value.shape[1]


def pack(blocks, turned, layer):
    tile = LANES
    rows = blocks[0].shape[2 if turned[0] else 1]
    counts = [b.shape[1 if t else 2] for b, t in zip(blocks, turned)]
    return pl.pallas_call(
        functools.partial(pack_kernel, turned),
        grid=(rows // tile,),
        in_specs=[
            pl.BlockSpec((1, n, tile), lambda g: (layer, 0, g))
            if t
            else pl.BlockSpec((1, tile, n), lambda g: (layer, g, 0))
            for n, t in zip(counts, turned)
        ],
        out_specs=pl.BlockSpec((tile, sum(counts)), lambda g: (g, 0)),
        out_shape=jax.ShapeDtypeStruct((rows, sum(counts)), BF16),
        compiler_params=pltpu.CompilerParams(vmem_limit_bytes=24 * MIB),
        cost_estimate=pl.CostEstimate(
            flops=0, bytes_accessed=6 * rows * sum(counts), transcendentals=0
        ),
        name="pack",
    )(*blocks)


def unpack_kernel(layers, turned, counts, same_ref, *refs):
    outs = refs[2 * layers :]
    for layer in range(layers):

        @pl.when(pl.program_id(0) == layer)
        def _():
            own, received = refs[2 * layer][...].astype(F32), refs[2 * layer + 1][...].astype(F32)
            value = jnp.where(same_ref[0] == 1, own, received)
            at = 0
            for turn, count, out in zip(turned, counts, outs):
                piece = value[:, at : at + count]
                out[0] = piece.T if turn else piece
                at += count


def unpack(pairs, turned, counts):
    layers = len(pairs)
    rows, columns = pairs[0][0].shape
    tile = LANES
    same = (lax.axis_index("c") == lax.axis_index("x")).astype(jnp.int32).reshape(1)
    return pl.pallas_call(
        functools.partial(unpack_kernel, layers, turned, counts),
        grid_spec=pltpu.PrefetchScalarGridSpec(
            num_scalar_prefetch=1,
            grid=(layers, rows // tile),
            in_specs=[
                pl.BlockSpec((tile, columns), lambda n, g, _, layer=layer: (jnp.where(n == layer, g, 0), 0))
                for layer in range(layers)
                for _ in range(2)
            ],
            out_specs=[
                pl.BlockSpec((1, n, tile), lambda n, g, _: (n, 0, g))
                if t
                else pl.BlockSpec((1, tile, n), lambda n, g, _: (n, g, 0))
                for n, t in zip(counts, turned)
            ],
        ),
        out_shape=[
            jax.ShapeDtypeStruct((layers, n, rows) if t else (layers, rows, n), F32)
            for n, t in zip(counts, turned)
        ],
        compiler_params=pltpu.CompilerParams(vmem_limit_bytes=24 * MIB),
        cost_estimate=pl.CostEstimate(
            flops=0, bytes_accessed=8 * layers * rows * columns, transcendentals=0
        ),
        name="unpack",
    )(same, *[v for pair in pairs for v in pair])


def slot_matmul_kernel(tile, blocks_ref, x_ref, w_ref, extra_ref, out_ref):
    tokens = x_ref.shape[0]
    for g in range(tokens // tile):
        at = pl.ds(g * tile, tile)
        out_ref[0, at, :] = lax.dot_general(
            x_ref[at, :], w_ref[...], (((1,), (1,)), ((), ())), preferred_element_type=F32
        ).astype(BF16)
    out_ref[0, tokens:, :] = extra_ref[...]


def slot_matmul(x, w, extra, other):
    tokens, depth = x.shape
    n = ring_size()
    f = extra.shape[1]
    blocks = slot_blocks()[1 if other else 0 :: 2]
    tile = min(tokens, 512)
    return pl.pallas_call(
        functools.partial(slot_matmul_kernel, tile),
        grid_spec=pltpu.PrefetchScalarGridSpec(
            num_scalar_prefetch=1,
            grid=(n,),
            in_specs=[
                whole((tokens, depth)),
                pl.BlockSpec((f, depth), lambda k, b: (b[k], 0)),
                whole((PAD, f)),
            ],
            out_specs=pl.BlockSpec((1, tokens + PAD, f), lambda k, b: (k, 0, 0)),
        ),
        out_shape=jax.ShapeDtypeStruct((n, tokens + PAD, f), BF16),
        compiler_params=pltpu.CompilerParams(vmem_limit_bytes=24 * MIB),
        cost_estimate=pl.CostEstimate(
            flops=2 * tokens * depth * n * f,
            bytes_accessed=2 * (tokens * depth + n * f * (depth + tokens)),
            transcendentals=0,
        ),
        name="slot_matmul",
    )(blocks, x, w, extra)


def column_sum(x, w, extra):
    other = slot_matmul(x, w, extra, True)
    mine = slot_matmul(x, w, extra, False)
    return pair_blocks(mine, other)


def block_scores(query, key, row0, column0, length, slope):
    rows, columns = query.shape[0], key.shape[0]
    scores = lax.dot_general(
        query, key, (((1,), (1,)), ((), ())), preferred_element_type=F32
    ) * (1.0 / math.sqrt(HEAD_DIM))
    row = lax.broadcasted_iota(jnp.int32, (rows, columns), 0) + row0
    column = lax.broadcasted_iota(jnp.int32, (rows, columns), 1) + column0
    scores = scores - slope * (row - column).astype(F32)
    return jnp.where((column <= row) & (column < length), scores, masked_score)


def attend_kernel(chunk, tile, length_ref, slope_ref, q_ref, *refs):
    keys, values = refs[: chunk + 1], refs[chunk + 1 : 2 * chunk + 2]
    context_ref, log_ref = refs[2 * chunk + 2 :]
    h, g = pl.program_id(0), pl.program_id(1)
    span = keys[0].shape[0]
    query = q_ref[...]
    scores = [
        block_scores(query, keys[m][...], chunk * span + g * tile, m * span, length_ref[0], slope_ref[h])
        for m in range(chunk + 1)
    ]
    highest = functools.reduce(jnp.maximum, [jnp.max(s, axis=1, keepdims=True) for s in scores])
    raised = [jnp.exp(s - highest) for s in scores]
    total = sum(jnp.sum(r, axis=1, keepdims=True) for r in raised)
    context = sum(
        jnp.dot((r / total).astype(BF16), v[...], preferred_element_type=F32)
        for r, v in zip(raised, values)
    )
    context_ref[...] = context.astype(BF16)
    log_ref[...] = jnp.broadcast_to(highest + jnp.log(total), log_ref.shape)


def attend(chunk, joined, length, slopes):
    span, columns = joined[0].shape
    heads = columns // (3 * HEAD_DIM)
    tile = min(span, 256)
    own = joined[chunk]
    return pl.pallas_call(
        functools.partial(attend_kernel, chunk, tile),
        grid_spec=pltpu.PrefetchScalarGridSpec(
            num_scalar_prefetch=2,
            grid=(heads, span // tile),
            in_specs=[pl.BlockSpec((tile, HEAD_DIM), lambda h, g, *_: (g, 3 * h))]
            + [pl.BlockSpec((span, HEAD_DIM), lambda h, g, *_: (0, 3 * h + 1))] * (chunk + 1)
            + [pl.BlockSpec((span, HEAD_DIM), lambda h, g, *_: (0, 3 * h + 2))] * (chunk + 1),
            out_specs=[pl.BlockSpec((tile, HEAD_DIM), lambda h, g, *_: (g, h))] * 2,
        ),
        out_shape=[
            jax.ShapeDtypeStruct((span, heads * HEAD_DIM), BF16),
            jax.ShapeDtypeStruct((span, heads * HEAD_DIM), F32),
        ],
        compiler_params=pltpu.CompilerParams(vmem_limit_bytes=32 * MIB),
        cost_estimate=pl.CostEstimate(
            flops=4 * span * span * (chunk + 1) * heads * HEAD_DIM,
            bytes_accessed=8 * span * columns * (chunk + 1),
            transcendentals=span * span * (chunk + 1) * heads,
        ),
        name="attend",
    )(length, slopes, own, *joined[: chunk + 1], *joined[: chunk + 1])


def attend_back_kernel(chunk, last, tile, length_ref, slope_ref, q_ref, *refs):
    n = chunk + 1
    keys, values, refs = refs[:n], refs[n : 2 * n], refs[2 * n :]
    given = []
    if not last:
        given, refs = refs[:n], refs[n:]
    grad_ref, log_ref, refs = refs[0], refs[1], refs[2:]
    out_ref, sums, refs = refs[0], refs[1:n], refs[n:]
    key_sums, value_sums = refs[:n], refs[n:]
    h, g = pl.program_id(0), pl.program_id(1)
    span = keys[0].shape[0]
    d = HEAD_DIM

    @pl.when(g == 0)
    def _():
        for m in range(n):
            if last:
                key_sums[m][...] = jnp.zeros((span, d), F32)
                value_sums[m][...] = jnp.zeros((span, d), F32)
            else:
                key_sums[m][...] = given[m][:, :d]
                value_sums[m][...] = given[m][:, d:]

    query, grad = q_ref[...], grad_ref[...]
    log_total = log_ref[:, :1]
    by_rows = (((0,), (0,)), ((), ()))
    chances, chance_grads = [], []
    for m in range(n):
        scores = block_scores(
            query, keys[m][...], chunk * span + g * tile, m * span, length_ref[0], slope_ref[h]
        )
        chances.append(jnp.exp(scores - log_total))
        chance_grads.append(
            lax.dot_general(grad, values[m][...], (((1,), (1,)), ((), ())), preferred_element_type=F32)
        )
    row_dot = sum(
        jnp.sum(p * c, axis=1, keepdims=True) for p, c in zip(chances, chance_grads)
    )
    query_grad = jnp.zeros((tile, d), F32)
    for m in range(n):
        value_sums[m][...] += lax.dot_general(
            chances[m].astype(BF16), grad, by_rows, preferred_element_type=F32
        )
        score_grad = (chances[m] * (chance_grads[m] - row_dot)).astype(BF16)
        query_grad += jnp.dot(score_grad, keys[m][...], preferred_element_type=F32)
        key_sums[m][...] += lax.dot_general(
            score_grad, query, by_rows, preferred_element_type=F32
        )
    factor = 1.0 / math.sqrt(d)
    out_ref[pl.ds(pl.multiple_of(g * tile, tile), tile), :d] = (query_grad * factor).astype(BF16)

    @pl.when(g == pl.num_programs(1) - 1)
    def _():
        out_ref[:, d : 2 * d] = (key_sums[chunk][...] * factor).astype(BF16)
        out_ref[:, 2 * d :] = value_sums[chunk][...].astype(BF16)
        for m in range(chunk):
            sums[m][:, :d] = key_sums[m][...]
            sums[m][:, d:] = value_sums[m][...]


def attend_back(chunk, joined, given, context_grad, log_total, length, slopes):
    span, columns = joined[0].shape
    heads = columns // (3 * HEAD_DIM)
    tile = min(span, 256)
    n = chunk + 1
    last = given is None
    wide = pl.BlockSpec((span, 2 * HEAD_DIM), lambda h, g, *_: (0, h))
    tall = pl.BlockSpec((tile, HEAD_DIM), lambda h, g, *_: (g, h))
    outs = pl.pallas_call(
        functools.partial(attend_back_kernel, chunk, last, tile),
        grid_spec=pltpu.PrefetchScalarGridSpec(
            num_scalar_prefetch=2,
            grid=(heads, span // tile),
            in_specs=[pl.BlockSpec((tile, HEAD_DIM), lambda h, g, *_: (g, 3 * h))]
            + [pl.BlockSpec((span, HEAD_DIM), lambda h, g, *_: (0, 3 * h + 1))] * n
            + [pl.BlockSpec((span, HEAD_DIM), lambda h, g, *_: (0, 3 * h + 2))] * n
            + [wide] * (0 if last else n)
            + [tall, tall],
            out_specs=[pl.BlockSpec((span, 3 * HEAD_DIM), lambda h, g, *_: (0, h))] + [wide] * chunk,
            scratch_shapes=[pltpu.VMEM((span, HEAD_DIM), F32)] * (2 * n),
        ),
        out_shape=[jax.ShapeDtypeStruct((span, columns), BF16)]
        + [jax.ShapeDtypeStruct((span, heads * 2 * HEAD_DIM), F32)] * chunk,
        compiler_params=pltpu.CompilerParams(vmem_limit_bytes=40 * MIB),
        cost_estimate=pl.CostEstimate(
            flops=10 * span * span * n * heads * HEAD_DIM,
            bytes_accessed=12 * span * columns * n,
            transcendentals=span * span * n * heads,
        ),
        name="attend_back",
    )(
        length,
        slopes,
        joined[chunk],
        *joined[:n],
        *joined[:n],
        *([] if last else given),
        context_grad,
        log_total,
    )
    return outs[0], list(outs[1:])


def rows_of(column):
    return column.reshape(-1, LANES)


def packed(value, rows, width):
    extra = jnp.pad(rows.astype(value.dtype), ((0, PAD - rows.shape[0]), (0, width - rows.shape[1])))
    return jnp.concatenate([value, extra], axis=0)


def shard_of(value):
    mean = lax.reduce_precision(jnp.mean(value, axis=1, keepdims=True), 8, 7)
    return packed((value - mean).astype(BF16), rows_of(mean), value.shape[1])


def weight_products(gain, shift, weight):
    def parts(v):
        high = lax.reduce_precision(v, 8, 7)
        return [high.astype(BF16), (v - high).astype(BF16)]

    rows = jnp.stack(parts(gain) + parts(shift))
    out = jnp.dot(rows, weight, preferred_element_type=F32)
    return out[0] + out[1], out[2] + out[3]


def sums_rows(first, second, width):
    extra = jnp.concatenate([rows_of(first), rows_of(second)], axis=0).astype(BF16)
    return jnp.pad(extra, ((0, PAD - extra.shape[0]), (0, width - extra.shape[1])))


def norm_backward(summed, centred, inverse, gain, width):
    tokens = centred.shape[0]
    groups = tokens // LANES
    gradient = summed[:tokens]
    first_sum = summed[tokens : tokens + groups, :LANES].reshape(tokens, 1)
    second_sum = summed[tokens + groups : tokens + 2 * groups, :LANES].reshape(tokens, 1)
    passed = inverse[:, :1] * (gradient * gain - first_sum / width - centred * (second_sum / width))
    return (passed, jnp.sum(gradient * centred, axis=0), jnp.sum(gradient, axis=0))


def added(items):
    return functools.reduce(jnp.add, items)


def three_parts(value):
    terms = []
    for _ in range(3):
        high = lax.reduce_precision(value, 8, 7)
        terms.append(high.astype(BF16))
        value = value - high
    return terms


def gather_weight(block):
    return lax.all_gather(block, ("rh", "c", "x"), axis=0, tiled=True)


def own_columns(blocks, rows):
    n = blocks.shape[1]
    blocks = blocks.reshape(-1, 2, rows, n)
    return lax.dynamic_index_in_dim(blocks, lax.axis_index("c"), 1, keepdims=False).reshape(-1, n)


def scatter_weight(term):
    return lax.psum_scatter(term, ("rh", "x"), scatter_dimension=0, tiled=True)


def swapped(value):
    return value, lax.ppermute(value, ("c", "x"), [(1, 2), (2, 1)])


def on_device(
    activations,
    cotangent,
    lengths,
    first_gain,
    first_shift,
    joined_weight,
    query_bias,
    value_bias,
    output_weight,
    output_bias,
    second_gain,
    second_shift,
    up_weight,
    up_bias,
    down_weight,
    down_bias,
):
    tokens, f = activations.shape
    layers = first_gain.shape[0]
    width = 2 * ring_size() * f
    heads_local = f // HEAD_DIM
    span = tokens // CHUNKS
    chunks = range(CHUNKS)

    def cut(value):
        return [value[k * span : (k + 1) * span] for k in chunks]

    lengths = swap_roles(lengths)
    head_index = block_index() * heads_local + jnp.arange(heads_local)
    slopes = jnp.exp2(-8.0 * (head_index + 1).astype(F32) / HEADS)
    valid = (jnp.arange(tokens) < lengths[0]).reshape(tokens, 1)

    smalls = (
        first_gain,
        first_shift,
        query_bias,
        value_bias,
        output_bias,
        second_gain,
        second_shift,
        down_bias,
    )
    table = jnp.concatenate(
        [s.reshape(layers, 1, f) for s in smalls] + [up_bias.reshape(layers, -1, f)], axis=1
    )
    table_rows = table.shape[1]
    count = layers * table_rows
    table = jnp.concatenate(three_parts(table.reshape(count, f)), axis=0)
    table = jnp.pad(table, ((0, -table.shape[0] % PAD), (0, 0)))
    shards = [shard_of(v) for v in cut(activations)]
    shards[0] = jnp.concatenate([shards[0], table], axis=0)
    shards = [swap_roles(s) for s in shards]
    residual = [swap_roles(after(v, *shards)) for v in cut(activations)]

    packs = []
    for layer in range(layers):
        blocks = (
            pack((joined_weight, output_weight), (False, True), layer),
            pack((up_weight,), (False,), layer),
            pack((down_weight,), (True,), layer),
        )
        if layer == 0:
            blocks, _ = lax.optimization_barrier((blocks, shards))
        packs.append([gather_weight(b) for b in blocks])
        if layer == 0:
            gradient = [swap_roles(after(v, packs[0][0])) * m for v, m in zip(cut(cotangent), cut(valid))]
    rows = joined_weight.shape[1]
    weights = []

    slots = [gather_slots(s) for s in shards]
    held = jnp.stack([s[span + PAD :][: 3 * count] for s in slots[0]]).astype(F32)
    table = (held[:, :count] + held[:, count : 2 * count] + held[:, 2 * count :]).reshape(
        len(slots[0]), layers, table_rows, f
    )
    own_up = table[0, :, len(smalls) :].reshape(layers, -1)

    no_rows = jnp.zeros((PAD, f), BF16)
    saved = []
    first_slots = [None] * CHUNKS
    turn = ()
    for layer in range(layers):
        last = layer + 1 == layers
        first_w = own_columns(packs[layer][0], rows)
        joined_w, output_w = first_w[:, : 3 * f], first_w[:, 3 * f :]
        gains = [table[:, layer, n] for n in range(len(smalls))]
        own = table[0, layer]
        zero = jnp.zeros((heads_local, HEAD_DIM), F32)
        joined_bias = jnp.stack(
            (own[2].reshape(heads_local, HEAD_DIM), zero, own[3].reshape(heads_local, HEAD_DIM)), axis=1
        ).reshape(3 * f)
        joined, kept = [], []
        for k in chunks:
            if layer > 0:
                slots[k] = gather_slots(shard_of(residual[k]))
            slots[k], _ = lax.optimization_barrier((slots[k], turn))
            normed_one, centred_one, inverse_one = assemble_norm(
                slots[k], residual[k], gains[0], gains[1]
            )
            joined.append(
                (jnp.dot(normed_one, joined_w, preferred_element_type=F32) + joined_bias).astype(BF16)
            )
            if last:
                first_slots[k] = gather_slots(after(gradient[k].astype(BF16), normed_one))
            context, log_total = attend(k, joined, lengths, slopes)
            if last:
                context = after(context, *first_slots[k])
            pair = column_sum(context, output_w, no_rows)
            turn = pair
            middle = residual[k] + ring_sum(pair)[:span] + own[4]
            kept.append([normed_one, centred_one, inverse_one, context, log_total, middle])
        up_w = own_columns(after(packs[layer][1], turn), rows)
        for k in chunks:
            middle = kept[k].pop()
            slots[k] = gather_slots(shard_of(middle))
            slots[k], _ = lax.optimization_barrier((slots[k], turn))
            normed_two, centred_two, inverse_two = assemble_norm(slots[k], middle, gains[5], gains[6])
            upper = jnp.dot(normed_two, up_w, preferred_element_type=F32) + own_up[layer]
            activated = gelu_tanh(upper).astype(BF16)
            if k == 0:
                down_w = own_columns(after(packs[layer][2], upper), rows)
            turn = (activated,)
            if not last:
                pair = column_sum(activated, down_w, no_rows)
                turn = pair
                residual[k] = middle + ring_sum(pair)[:span] + own[7]
            kept[k] += [normed_two, centred_two, inverse_two, upper, activated, middle]
        weights.append((joined_w, output_w, up_w, down_w))
        saved.append((joined, joined_bias, kept))

    weight_terms = [None] * layers
    small_terms = [None] * layers
    result = [None] * CHUNKS
    middle_grad = [None] * CHUNKS
    passed_one = [None] * CHUNKS

    def term(pieces):
        return added(
            [jnp.einsum("td,tn->dn", a, b, preferred_element_type=F32) for a, b in pieces]
        ).astype(BF16)

    for layer in reversed(range(layers)):
        joined, joined_bias, kept = saved[layer]
        joined_w, output_w, up_w, down_w = weights[layer]
        own = table[0, layer]
        order = slot_blocks()
        gains = [table[order, layer, n].reshape(width) for n in range(len(smalls))]
        up_gain, up_shift = weight_products(gains[5], gains[6], up_w)
        joined_gain, joined_shift = weight_products(gains[0], gains[1], joined_w)
        given = None
        smalls_of, down_ends, up_ends, joined_ends, output_ends = ([None] * CHUNKS for _ in range(5))
        for k in reversed(chunks):
            normed_two, centred_two, inverse_two, upper, activated, middle = kept[k][5:]
            down_bias_term = jnp.sum(gradient[k], axis=0)
            slots = first_slots[k] if layer + 1 == layers else gather_slots(gradient[k].astype(BF16))
            slots, _ = lax.optimization_barrier((slots, turn))
            low_gradient = assemble(slots)
            hidden_grad = jnp.dot(low_gradient, down_w, preferred_element_type=F32)
            upper_grad = jax.vjp(gelu_tanh, upper)[1](hidden_grad)[0].astype(BF16)
            wide_grad = upper_grad.astype(F32)
            first_sum = jnp.sum(wide_grad * up_gain, axis=1)
            second_sum = jnp.sum(wide_grad * (upper - (own_up[layer] + up_shift)), axis=1)
            up_bias_term = jnp.sum(wide_grad, axis=0)
            pair = column_sum(upper_grad, up_w, sums_rows(first_sum, second_sum, f))
            turn = pair
            down_ends[k] = (low_gradient, after(activated, pair))
            normed_two_grad = ring_sum(pair)
            if k == 0:
                down_term = term(down_ends)
                normed_two_grad = after(normed_two_grad, down_term)
                if layer + 1 < layers:
                    normed_two_grad = after(normed_two_grad, joint_sum)
                down_sum = scatter_weight(down_term)
            passed_two, gain_two_term, shift_two_term = norm_backward(
                normed_two_grad, centred_two, inverse_two, own[5], width
            )
            middle_grad[k] = gradient[k] + passed_two
            output_bias_term = jnp.sum(middle_grad[k], axis=0)
            smalls_of[k] = [output_bias_term, gain_two_term, shift_two_term, down_bias_term, up_bias_term]
            up_ends[k] = (normed_two, after(upper_grad, middle_grad[k]))
        for k in reversed(chunks):
            normed_one, centred_one, inverse_one, context, log_total = kept[k][:5]
            activated, middle = kept[k][9:]
            slots = gather_slots(middle_grad[k].astype(BF16))
            slots, _ = lax.optimization_barrier((slots, turn))
            if k == 0:
                up_term = term(up_ends)
                slots, _ = lax.optimization_barrier((slots, (up_term, down_sum)))
                up_sum = scatter_weight(up_term)
            low_middle = assemble(slots)
            context_grad = jnp.dot(low_middle, output_w, preferred_element_type=F32).astype(BF16)
            if layer + 1 == layers:
                last_pair = column_sum(after(activated, context_grad), down_w, no_rows)
                result[k] = middle + ring_sum(last_pair)[:span] + own[7]
            joined_grad, given = attend_back(
                k, joined, given, context_grad, log_total, lengths, slopes
            )
            if layer + 1 == layers:
                joined_grad, result[k] = lax.optimization_barrier((joined_grad, result[k]))
            wide_grad = joined_grad.astype(F32)
            first_sum = jnp.sum(wide_grad * joined_gain, axis=1)
            second_sum = jnp.sum(
                wide_grad * (joined[k].astype(F32) - (joined_bias + joined_shift)), axis=1
            )
            joined_ends[k] = (normed_one, joined_grad)
            output_ends[k] = (low_middle, context)
            if k == 0 and layer == 0:
                first_term = jnp.concatenate([term(joined_ends), term(output_ends)], axis=1)
                first_sum = after(first_sum, first_term)
            pair = column_sum(joined_grad, joined_w, sums_rows(first_sum, second_sum, f))
            turn = pair
            normed_one_grad = ring_sum(pair)
            if k == 0 and layer > 0:
                joined_ends[0] = (normed_one, after(joined_grad, pair))
                output_ends[0] = (low_middle, after(context, pair))
                first_term = jnp.concatenate([term(joined_ends), term(output_ends)], axis=1)
                normed_one_grad = after(normed_one_grad, first_term, up_sum)
            if k == 0:
                joint_sum = scatter_weight(first_term)
            joined_bias_term = jnp.sum(joined_grad.astype(F32), axis=0).reshape(heads_local, 3, HEAD_DIM)
            passed_one[k], gain_one_term, shift_one_term = norm_backward(
                normed_one_grad, centred_one, inverse_one, own[0], width
            )
            gradient[k] = middle_grad[k] + passed_one[k]
            smalls_of[k] = jnp.concatenate(
                [
                    t.reshape(-1, f)
                    for t in (
                        gain_one_term,
                        shift_one_term,
                        joined_bias_term[:, 0],
                        joined_bias_term[:, 2],
                        *smalls_of[k],
                    )
                ],
                axis=0,
            )
        small_terms[layer] = added(smalls_of)
        weight_terms[layer] = [swapped(v) for v in (joint_sum, up_sum, down_sum)]
    input_grad = jnp.concatenate(
        [swap_roles(m) + swap_roles(p.astype(BF16)).astype(F32) for m, p in zip(middle_grad, passed_one)],
        axis=0,
    )
    small = jnp.stack(small_terms)
    for axis in ("rh", "x"):
        size = lax.axis_size(axis)
        small = small + added(
            [lax.ppermute(small, axis, [(r, r ^ k) for r in range(size)]) for k in range(1, size)]
        )
    same = lax.axis_index("c") == lax.axis_index("x")
    small = jnp.where(same, small, partner(small))

    joined_out, output_out = unpack([t[0] for t in weight_terms], (False, True), (3 * f, f))
    (up_out,) = unpack([t[1] for t in weight_terms], (False,), (up_weight.shape[2],))
    (down_out,) = unpack([t[2] for t in weight_terms], (True,), (down_weight.shape[1],))

    return (
        jnp.concatenate([swap_roles(r) for r in result], axis=0),
        input_grad,
        small[:, 0],
        small[:, 1],
        joined_out,
        small[:, 2],
        small[:, 3],
        output_out,
        small[:, 4],
        small[:, 5],
        small[:, 6],
        up_out,
        small[:, 8:].reshape(layers, -1),
        down_out,
        small[:, 7],
    )


def solution(mesh):
    rows, columns = mesh.devices.shape
    inner = Mesh(mesh.devices.reshape(rows // 2, 2, columns // 2, 2), ("rh", "c", "t", "x"))
    row, col = ("rh", "c"), ("t", "x")
    return jax.shard_map(
        on_device,
        mesh=inner,
        in_specs=(
            P(row, col),
            P(row, col),
            P(row),
            P(None, col),
            P(None, col),
            P(None, row, col),
            P(None, col),
            P(None, col),
            P(None, col, row),
            P(None, col),
            P(None, col),
            P(None, col),
            P(None, row, col),
            P(None, col),
            P(None, col, row),
            P(None, col),
        ),
        out_specs=(
            P(row, col),
            P(row, col),
            P(None, col),
            P(None, col),
            P(None, row, col),
            P(None, col),
            P(None, col),
            P(None, col, row),
            P(None, col),
            P(None, col),
            P(None, col),
            P(None, row, col),
            P(None, col),
            P(None, col, row),
            P(None, col),
        ),
        check_vma=False,
    )
```

time: 1560 us -> 1160 us (0.74)
  blocking collectives: 116 us -> 0 us
  other arithmetic: 149 us -> 69.5 us
  local copies, waits for them, and re-layouts: 171 us -> 112 us
  starting transfers between devices: 169 us -> 113 us
  matrix products: 137 us -> 84.2 us
  waiting for transfers between devices: 646 us -> 595 us
  Pallas kernels: 133 us -> 156 us
    ppermute x22 -> x15, waiting for transfers between devices: 318 us -> 71.9 us  [the longest x2 32 us: on_device(): lax.ppermute(small, axis, [(r, r ^ k) for r in range(size)])]
    ppermute x48, waiting for transfers between devices: 316 us -> 505 us  [ring(): return lax.ppermute(value, 't', [(i, i ^ k) for i in range(ring_size())])]
    all_gather x1 -> x0, blocking collectives: 100 us -> none  [on_device(): table = lax.all_gather(table, ('zh', 't'), axis=0)]
    another operation x38 -> x4, other arithmetic: 74.3 us -> 7.08 us  [the longest x16 28.1 us: gather_weight(): pair = jnp.stack([jnp.where(first, keep, got), jnp.where(first, got, keep)])]
    ppermute x57 -> x41, starting transfers between devices: 87.5 us -> 28.8 us  [partner(): return lax.ppermute(value, 'c', [(0, 1), (1, 0)])]
    dot_general x26 -> x14, matrix products: 110 us -> 64.8 us  [the longest x8 35.1 us: term(): jnp.einsum('td,tn->dn', a, b, preferred_element_type=F32)]
    dot_general x6 -> x0, local copies, waits for them, and re-layouts: 35.2 us -> none  [the longest x2 13 us: on_device(): jnp.einsum('td,tc->dc', normed_one, joined_grad, preferred_element_type=F32)]
    select_n x20 -> x2, other arithmetic: 32 us -> 4.5 us  [swap_roles(): jnp.where(same, value, lax.ppermute(value, ('c', 'x'), [(1, 2), (2, 1)]))]
  transfers between devices with their start and end apart: 143 -> 116, of which waited for: 59 -> 58; matrix products, arithmetic and copies ran while one was open for 24% -> 15% of each run, Pallas kernels for 8% -> 12%
where the time goes in v2:
time: 1160 us; the launch traced here: 1150 us
  waiting for transfers between devices  595 us (51%)
  Pallas kernels  156 us (13%)
  starting transfers between devices  113 us (10%)
  local copies, waits for them, and re-layouts  112 us (10%)
  matrix products  84.2 us (7%)
  other arithmetic  69.5 us (6%)
  between operations  18.6 us (2%)
    ppermute x48, waiting for transfers between devices, ring(): return lax.ppermute(value, 't', [(i, i ^ k) for i in range(ring_size())])  505 us
    unnamed x294, local copies, waits for them, and re-layouts  59.3 us
    pallas_call x16, Pallas kernels, slot_matmul(): pl.pallas_call(functools.partial(slot_matmul_kernel, tile), grid_spec=plt...  50.6 us
    ppermute x48, starting transfers between devices, ring(): return lax.ppermute(value, 't', [(i, i ^ k) for i in range(ring_size())])  37.9 us
    dot_general x8, matrix products, term(): jnp.einsum('td,tn->dn', a, b, preferred_element_type=F32)  35.1 us
    ppermute x2, waiting for transfers between devices, on_device(): lax.ppermute(small, axis, [(r, r ^ k) for r in range(size)])  32 us
    pallas_call x4, Pallas kernels, assemble_norm(): pl.pallas_call(functools.partial(assemble_norm_kernel, slots, width), gri...  31.1 us
    ppermute x41, starting transfers between devices, partner(): return lax.ppermute(value, 'c', [(0, 1), (1, 0)])  28.8 us
  transfers between devices with their start and end apart: 116, of which 58 were waited for; matrix products, arithmetic and copies ran while one was open for 15% of the time, Pallas kernels for 12%

profile of v2, /device:TPU:1, one launch (start us, length us, event | category | flops | bytes accessed | tf_op | source)
XLA Modules:
  0.0 1148.5 jit_solution(13204679917856170142)
XLA Ops:
  18.0 4.5 collective-permute-start.1
  51.2 13.4 %collective-permute-done.4.refs_2_ = bf16[1120,256]{1,0:T(8,128)(2,1)S(1)} collective-permute-done((bf16[1120,256]{1,0:T(8,128)(2,1)}, bf16[1120,256]{1,0:T(8,128)(2,1)S(1)}, u32[]{:S(2)}, u32[]{:S(2)}) %collective-permute-start.4) | collective-permute-done | bytes 573472 | tf_op jit(solution)/shard_map/ppermute | solution.py:39
  68.8 12.3 %collective-permute-done.8.refs_6_ = bf16[1120,256]{1,0:T(8,128)(2,1)S(1)} collective-permute-done((bf16[1120,256]{1,0:T(8,128)(2,1)S(1)}, bf16[1120,256]{1,0:T(8,128)(2,1)S(1)}, u32[]{:S(2)}, u32[]{:S(2)}) %collective-permute-start.8) | collective-permute-done | bytes 573472 | tf_op jit(solution)/shard_map/ppermute | solution.py:39
  85.6 6.9 all-gather.7.cloned.1.call-done
  99.8 16.9 %collective-permute-done.32 = f32[1024,256]{1,0:T(8,128)} collective-permute-done((f32[1024,256]{1,0:T(8,128)}, f32[1024,256]{1,0:T(8,128)}, u32[]{:S(2)}, u32[]{:S(2)}) %collective-permute-start.32) | collective-permute-done | bytes 1048608 | tf_op jit(solution)/shard_map/ppermute | solution.py:48
  120.2 6.4 assemble_norm.4
  133.9 9.0 attend.2
  160.6 10.3 collective-permute-done.12
  175.5 15.7 %collective-permute-done.11 = bf16[1040,256]{1,0:T(8,128)(2,1)S(1)} collective-permute-done((bf16[1040,256]{1,0:T(8,128)(2,1)}, bf16[1040,256]{1,0:T(8,128)(2,1)S(1)}, u32[]{:S(2)}, u32[]{:S(2)}) %collective-permute-start.11) | collective-permute-done | bytes 532512 | tf_op jit(solution)/shard_map/ppermute | solution.py:39
  191.2 5.4 collective-permute-done.13
  200.6 22.3 %collective-permute-done.17.refs_4_ = bf16[1040,256]{1,0:T(8,128)(2,1)S(1)} collective-permute-done((bf16[1040,256]{1,0:T(8,128)(2,1)S(1)}, bf16[1040,256]{1,0:T(8,128)(2,1)S(1)}, u32[]{:S(2)}, u32[]{:S(2)}) %collective-permute-start.17) | collective-permute-done | bytes 532512 | tf_op jit(solution)/shard_map/ppermute | solution.py:39
  224.7 10.5 collective-permute-done.19.refs_6_
  245.6 8.2 assemble_norm.5
  257.6 6.9 multiply_convert_fusion.1
  277.9 12.1 %collective-permute-done.23 = bf16[1040,256]{1,0:T(8,128)(2,1)S(1)} collective-permute-done((bf16[1040,256]{1,0:T(8,128)(2,1)S(1)}, bf16[1040,256]{1,0:T(8,128)(2,1)S(1)}, u32[]{:S(2)}, u32[]{:S(2)}) %collective-permute-start.23) | collective-permute-done | bytes 532512 | tf_op jit(solution)/shard_map/ppermute | solution.py:39
  290.3 18.7 %collective-permute-done.22 = bf16[1040,256]{1,0:T(8,128)(2,1)S(1)} collective-permute-done((bf16[1040,256]{1,0:T(8,128)(2,1)S(1)}, bf16[1040,256]{1,0:T(8,128)(2,1)S(1)}, u32[]{:S(2)}, u32[]{:S(2)}) %collective-permute-start.22) | collective-permute-done | bytes 532512 | tf_op jit(solution)/shard_map/ppermute | solution.py:39
  309.0 5.7 collective-permute-done.24
  316.6 23.8 %collective-permute-done.28.refs_4_ = bf16[1040,256]{1,0:T(8,128)(2,1)} collective-permute-done((bf16[1040,256]{1,0:T(8,128)(2,1)S(1)}, bf16[1040,256]{1,0:T(8,128)(2,1)}, u32[]{:S(2)}, u32[]{:S(2)}) %collective-permute-start.28) | collective-permute-done | bytes 532512 | tf_op jit(solution)/shard_map/ppermute | solution.py:39
  341.5 12.3 %collective-permute-done.30.refs_6_ = bf16[1040,256]{1,0:T(8,128)(2,1)} collective-permute-done((bf16[1040,256]{1,0:T(8,128)(2,1)}, bf16[1040,256]{1,0:T(8,128)(2,1)}, u32[]{:S(2)}, u32[]{:S(2)}) %collective-permute-start.30) | collective-permute-done | bytes 532512 | tf_op jit(solution)/shard_map/ppermute | solution.py:39
  363.9 8.5 assemble_norm.6
  379.1 23.1 %collective-permute-done.36.refs_4_ = bf16[1024,256]{1,0:T(8,128)(2,1)S(1)} collective-permute-done((bf16[1024,256]{1,0:T(8,128)(2,1)S(1)}, bf16[1024,256]{1,0:T(8,128)(2,1)S(1)}, u32[]{:S(2)}, u32[]{:S(2)}) %collective-permute-start.36) | collective-permute-done | bytes 524320 | tf_op jit(solution)/shard_map/ppermute | solution.py:39
  406.4 8.4 collective-permute-done.38.refs_6_
  420.0 9.0 attend.3
  437.6 12.1 %collective-permute-done.42 = bf16[1040,256]{1,0:T(8,128)(2,1)S(1)} collective-permute-done((bf16[1040,256]{1,0:T(8,128)(2,1)S(1)}, bf16[1040,256]{1,0:T(8,128)(2,1)S(1)}, u32[]{:S(2)}, u32[]{:S(2)}) %collective-permute-start.42) | collective-permute-done | bytes 532512 | tf_op jit(solution)/shard_map/ppermute | solution.py:39
  451.1 19.0 %collective-permute-done.41 = bf16[1040,256]{1,0:T(8,128)(2,1)S(1)} collective-permute-done((bf16[1040,256]{1,0:T(8,128)(2,1)S(1)}, bf16[1040,256]{1,0:T(8,128)(2,1)S(1)}, u32[]{:S(2)}, u32[]{:S(2)}) %collective-permute-start.41) | collective-permute-done | bytes 532512 | tf_op jit(solution)/shard_map/ppermute | solution.py:39
  479.0 22.5 %collective-permute-done.47.refs_4_ = bf16[1040,256]{1,0:T(8,128)(2,1)} collective-permute-done((bf16[1040,256]{1,0:T(8,128)(2,1)S(1)}, bf16[1040,256]{1,0:T(8,128)(2,1)}, u32[]{:S(2)}, u32[]{:S(2)}) %collective-permute-start.47) | collective-permute-done | bytes 532512 | tf_op jit(solution)/shard_map/ppermute | solution.py:39
  505.3 9.6 collective-permute-done.49.refs_6_
  520.2 8.0 assemble_norm.7
  531.9 7.2 multiply_convert_fusion
  546.3 8.7 convert_reduce_fusion.1
  567.7 6.2 convolution_convert_fusion.3
  575.8 12.2 %collective-permute-done.53 = bf16[1040,256]{1,0:T(8,128)(2,1)S(1)} collective-permute-done((bf16[1040,256]{1,0:T(8,128)(2,1)}, bf16[1040,256]{1,0:T(8,128)(2,1)S(1)}, u32[]{:S(2)}, u32[]{:S(2)}) %collective-permute-start.53) | collective-permute-done | bytes 532512 | tf_op jit(solution)/shard_map/ppermute | solution.py:39
  590.5 15.6 %collective-permute-done.52 = bf16[1040,256]{1,0:T(8,128)(2,1)S(1)} collective-permute-done((bf16[1040,256]{1,0:T(8,128)(2,1)}, bf16[1040,256]{1,0:T(8,128)(2,1)S(1)}, u32[]{:S(2)}, u32[]{:S(2)}) %collective-permute-start.52) | collective-permute-done | bytes 532512 | tf_op jit(solution)/shard_map/ppermute | solution.py:39
  606.1 7.3 collective-permute-done.54
  616.7 23.4 %collective-permute-done.58.refs_4_ = bf16[1024,256]{1,0:T(8,128)(2,1)S(1)} collective-permute-done((bf16[1024,256]{1,0:T(8,128)(2,1)S(1)}, bf16[1024,256]{1,0:T(8,128)(2,1)S(1)}, u32[]{:S(2)}, u32[]{:S(2)}) %collective-permute-start.58) | collective-permute-done | bytes 524320 | tf_op jit(solution)/shard_map/ppermute | solution.py:39
  641.2 11.9 %collective-permute-done.60.refs_6_ = bf16[1024,256]{1,0:T(8,128)(2,1)} collective-permute-done((bf16[1024,256]{1,0:T(8,128)(2,1)S(1)}, bf16[1024,256]{1,0:T(8,128)(2,1)}, u32[]{:S(2)}, u32[]{:S(2)}) %collective-permute-start.60) | collective-permute-done | bytes 524320 | tf_op jit(solution)/shard_map/ppermute | solution.py:39
  654.5 6.2 convolution_convert_fusion.2
  693.1 11.8 %attend_back.2.x_ref = bf16[1024,768]{1,0:T(8,128)(2,1)S(1)} custom-call(s32[1]{0:T(128)} %select_n.78.length_ref, f32[2]{0:T(128)S(1)} %multiply_exponential_fusion.slope_ref, bf16[1024,768]{1,0:T(8,128)(2,1)S(1)} %copy-done.12, bf16[1024,768]{1,0:T(8,128)(2,1)S(1)} %copy-done.12, bf16[1024,768]{1,0:T(8,128)(2,1)S(1)} %copy-done.12, ...), custom_call_target="tpu_custom_call" | custom-call | flops 2684354560 | bytes 9437184 | tf_op jit(solution)/shard_map/attend_back/pallas_call | solution.py:447
  710.4 17.3 %collective-permute-done.63 = bf16[1040,256]{1,0:T(8,128)(2,1)S(1)} collective-permute-done((bf16[1040,256]{1,0:T(8,128)(2,1)S(1)}, bf16[1040,256]{1,0:T(8,128)(2,1)S(1)}, u32[]{:S(2)}, u32[]{:S(2)}) %collective-permute-start.63) | collective-permute-done | bytes 532512 | tf_op jit(solution)/shard_map/ppermute | solution.py:39
  733.8 6.3 collective-permute-start.67
  752.7 8.0 collective-permute-done.69
  766.9 13.5 %collective-permute-done.68 = bf16[1040,256]{1,0:T(8,128)(2,1)} collective-permute-done((bf16[1040,256]{1,0:T(8,128)(2,1)}, bf16[1040,256]{1,0:T(8,128)(2,1)}, u32[]{:S(2)}, u32[]{:S(2)}) %collective-permute-start.68) | collective-permute-done | bytes 532512 | tf_op jit(solution)/shard_map/ppermute | solution.py:39
  780.4 5.5 collective-permute-done.70
  793.8 22.5 %collective-permute-done.74.refs_4_ = bf16[1024,256]{1,0:T(8,128)(2,1)S(1)} collective-permute-done((bf16[1024,256]{1,0:T(8,128)(2,1)S(1)}, bf16[1024,256]{1,0:T(8,128)(2,1)S(1)}, u32[]{:S(2)}, u32[]{:S(2)}) %collective-permute-start.74) | collective-permute-done | bytes 524320 | tf_op jit(solution)/shard_map/ppermute | solution.py:39
  818.1 11.1 collective-permute-done.76.refs_6_
  837.7 8.1 convert_reduce_fusion
  858.6 6.2 convolution_convert_fusion.1
  866.4 12.4 %collective-permute-done.80 = bf16[1040,256]{1,0:T(8,128)(2,1)S(1)} collective-permute-done((bf16[1040,256]{1,0:T(8,128)(2,1)}, bf16[1040,256]{1,0:T(8,128)(2,1)S(1)}, u32[]{:S(2)}, u32[]{:S(2)}) %collective-permute-start.80) | collective-permute-done | bytes 532512 | tf_op jit(solution)/shard_map/ppermute | solution.py:39
  881.3 15.4 %collective-permute-done.79 = bf16[1040,256]{1,0:T(8,128)(2,1)S(1)} collective-permute-done((bf16[1040,256]{1,0:T(8,128)(2,1)}, bf16[1040,256]{1,0:T(8,128)(2,1)S(1)}, u32[]{:S(2)}, u32[]{:S(2)}) %collective-permute-start.79) | collective-permute-done | bytes 532512 | tf_op jit(solution)/shard_map/ppermute | solution.py:39
  896.7 8.0 collective-permute-done.81
  911.1 6.2 convolution_convert_fusion
  919.6 23.4 %collective-permute-done.86.refs_4_ = bf16[1024,256]{1,0:T(8,128)(2,1)S(1)} collective-permute-done((bf16[1024,256]{1,0:T(8,128)(2,1)S(1)}, bf16[1024,256]{1,0:T(8,128)(2,1)S(1)}, u32[]{:S(2)}, u32[]{:S(2)}) %collective-permute-start.86) | collective-permute-done | bytes 524320 | tf_op jit(solution)/shard_map/ppermute | solution.py:39
  944.3 11.7 %collective-permute-done.88.refs_6_ = bf16[1024,256]{1,0:T(8,128)(2,1)S(1)} collective-permute-done((bf16[1024,256]{1,0:T(8,128)(2,1)S(1)}, bf16[1024,256]{1,0:T(8,128)(2,1)S(1)}, u32[]{:S(2)}, u32[]{:S(2)}) %collective-permute-start.88) | collective-permute-done | bytes 524320 | tf_op jit(solution)/shard_map/ppermute | solution.py:39
  964.6 11.8 %attend_back.3.x_ref = bf16[1024,768]{1,0:T(8,128)(2,1)S(1)} custom-call(s32[1]{0:T(128)} %select_n.78.length_ref, f32[2]{0:T(128)S(1)} %multiply_exponential_fusion.slope_ref, bf16[1024,768]{1,0:T(8,128)(2,1)S(1)} %copy-done.10, bf16[1024,768]{1,0:T(8,128)(2,1)S(1)} %copy-done.10, bf16[1024,768]{1,0:T(8,128)(2,1)S(1)} %copy-done.10, ...), custom_call_target="tpu_custom_call" | custom-call | flops 2684354560 | bytes 9437184 | tf_op jit(solution)/shard_map/attend_back/pallas_call | solution.py:447
  1001.9 11.9 %collective-permute-done.92 = bf16[1040,256]{1,0:T(8,128)(2,1)S(1)} collective-permute-done((bf16[1040,256]{1,0:T(8,128)(2,1)S(1)}, bf16[1040,256]{1,0:T(8,128)(2,1)S(1)}, u32[]{:S(2)}, u32[]{:S(2)}) %collective-permute-start.92) | collective-permute-done | bytes 532512 | tf_op jit(solution)/shard_map/ppermute | solution.py:39
  1016.1 5.1 collective-permute-start.103
  1026.9 6.5 collective-permute-done.91
  1048.0 30.4 %collective-permute-done.96 = f32[2,12,256]{2,0,1:T(2,128)S(1)} collective-permute-done((f32[2,12,256]{2,0,1:T(2,128)S(1)}, f32[2,12,256]{2,0,1:T(2,128)S(1)}, u32[]{:S(2)}, u32[]{:S(2)}) %collective-permute-start.96) | collective-permute-done | bytes 24608 | tf_op jit(solution)/shard_map/ppermute | solution.py:799
  1097.6 6.6 unpack.5
  1105.5 7.4 collective-permute-done.94
  1115.5 8.7 collective-permute-done.100.refs_1_
  1124.2 6.2 unpack.4
  1130.4 4.9 collective-permute-done.98.refs_1_
  1135.3 5.9 unpack.3
  (713 shorter events, 397.1 us)
Async XLA Ops:
  7.2 85.4 %all-gather.7.cloned.1.call-start = ((), (), s32[]{:S(2)}) async-start(), calls=%async_computation.6 | async-start | bytes 9437184 | tf_op jit(solution)/shard_map/all_gather | solution.py:535
  35.0 203.3 %all-gather.9.cloned.1.call-start = ((), (), s32[]{:S(2)}) async-start(), calls=%async_computation.7 | async-start | bytes 9437184 | tf_op jit(solution)/shard_map/all_gather | solution.py:535
  35.8 228.7 %all-gather.11.cloned.1.call-start = ((), (), s32[]{:S(2)}) async-start(), calls=%async_computation.8 | async-start | bytes 9437184 | tf_op jit(solution)/shard_map/all_gather | solution.py:535
  36.5 365.6 %all-gather.13.cloned.1.call-start = ((), (), s32[]{:S(2)}) async-start(), calls=%async_computation.9 | async-start | bytes 9437184 | tf_op jit(solution)/shard_map/all_gather | solution.py:535
  39.4 462.2 %all-gather.15.cloned.1.call-start = ((), (), s32[]{:S(2)}) async-start(), calls=%async_computation.10 | async-start | bytes 9437184 | tf_op jit(solution)/shard_map/all_gather | solution.py:535
  39.4 25.2 %collective-permute-start.4 = (bf16[1120,256]{1,0:T(8,128)(2,1)}, bf16[1120,256]{1,0:T(8,128)(2,1)S(1)}, u32[]{:S(2)}, u32[]{:S(2)}) collective-permute-start(bf16[1120,256]{1,0:T(8,128)(2,1)} %broadcast_select_fusion.refs_0_), channel_id=1, source_target_pairs={{0,2},{2,0},{4,6},{6,4},{1,3},{3,1},{5,7},{7,5},{8,10},{10,8},{12,... | collective-permute-start | bytes 1720328 | tf_op jit(solution)/shard_map/ppermute | solution.py:39
  40.8 27.2 %collective-permute-start.6 = (bf16[1120,256]{1,0:T(8,128)(2,1)}, bf16[1120,256]{1,0:T(8,128)(2,1)S(1)}, u32[]{:S(2)}, u32[]{:S(2)}) collective-permute-start(bf16[1120,256]{1,0:T(8,128)(2,1)} %broadcast_select_fusion.refs_0_), channel_id=1, source_target_pairs={{0,4},{2,6},{4,0},{6,2},{1,5},{3,7},{5,1},{7,3},{8,12},{10,14},{12... | collective-permute-start | bytes 1720328 | tf_op jit(solution)/shard_map/ppermute | solution.py:39
  45.6 23.2 %collective-permute-start.3 = (bf16[1120,256]{1,0:T(8,128)(2,1)}, bf16[1120,256]{1,0:T(8,128)(2,1)S(1)}, u32[]{:S(2)}, u32[]{:S(2)}) collective-permute-start(bf16[1120,256]{1,0:T(8,128)(2,1)} %broadcast_select_fusion.refs_0_), channel_id=1, source_target_pairs={{0,8},{8,0},{1,9},{9,1},{2,10},{10,2},{3,11},{11,3},{4,12},{12,4},... | collective-permute-start | bytes 1720328 | tf_op jit(solution)/shard_map/ppermute | solution.py:43
  49.2 50.6 %collective-permute-start.2 = (f32[1024,256]{1,0:T(8,128)}, f32[1024,256]{1,0:T(8,128)}, u32[]{:S(2)}, u32[]{:S(2)}) collective-permute-start(f32[1024,256]{1,0:T(8,128)} %param.16), channel_id=1, source_target_pairs={{1,8},{8,1},{3,10},{10,3},{5,12},{12,5},{7,14},{14,7},{17,24},{24,... | collective-permute-start | bytes 3145736 | tf_op jit(solution)/shard_map/ppermute | solution.py:48
  92.5 24.2 %collective-permute-start.32 = (f32[1024,256]{1,0:T(8,128)}, f32[1024,256]{1,0:T(8,128)}, u32[]{:S(2)}, u32[]{:S(2)}) collective-permute-start(f32[1024,256]{1,0:T(8,128)} %param.17), channel_id=1, source_target_pairs={{1,8},{8,1},{3,10},{10,3},{5,12},{12,5},{7,14},{14,7},{17,24},{24,... | collective-permute-start | bytes 3145736 | tf_op jit(solution)/shard_map/ppermute | solution.py:48
  160.0 379.1 %all-gather.17.cloned.1.call-start = ((), (), s32[]{:S(2)}) async-start(), calls=%async_computation.11 | async-start | bytes 9437184 | tf_op jit(solution)/shard_map/all_gather | solution.py:535
  160.2 30.9 %collective-permute-start.11 = (bf16[1040,256]{1,0:T(8,128)(2,1)}, bf16[1040,256]{1,0:T(8,128)(2,1)S(1)}, u32[]{:S(2)}, u32[]{:S(2)}) collective-permute-start(bf16[1040,256]{1,0:T(8,128)(2,1)} %get-tuple-element.337), channel_id=1, source_target_pairs={{0,2},{2,0},{4,6},{6,4},{1,3},{3,1},{5,7},{7,5},{8,10},{10,8},{12,... | collective-permute-start | bytes 1597448 | tf_op jit(solution)/shard_map/ppermute | solution.py:39
  172.0 24.6 %collective-permute-start.13 = (bf16[1040,256]{1,0:T(8,128)(2,1)S(1)}, bf16[1040,256]{1,0:T(8,128)(2,1)S(1)}, u32[]{:S(2)}, u32[]{:S(2)}) collective-permute-start(bf16[1040,256]{1,0:T(8,128)(2,1)S(1)} %add_convert_fusion.7), channel_id=1, source_target_pairs={{0,4},{2,6},{4,0},{6,2},{1,5},{3,7},{5,1},{7,3},{8,12},{10,14},{12... | collective-permute-start | bytes 1597448 | tf_op jit(solution)/shard_map/ppermute | solution.py:39
  197.2 25.7 %collective-permute-start.17 = (bf16[1040,256]{1,0:T(8,128)(2,1)S(1)}, bf16[1040,256]{1,0:T(8,128)(2,1)S(1)}, u32[]{:S(2)}, u32[]{:S(2)}) collective-permute-start(bf16[1040,256]{1,0:T(8,128)(2,1)S(1)} %fusion.45.refs_0_), channel_id=1, source_target_pairs={{0,4},{2,6},{4,0},{6,2},{1,5},{3,7},{5,1},{7,3},{8,12},{10,14},{12... | collective-permute-start | bytes 1597448 | tf_op jit(solution)/shard_map/ppermute | solution.py:39
  197.3 26.9 %collective-permute-start.15 = (bf16[1040,256]{1,0:T(8,128)(2,1)S(1)}, bf16[1040,256]{1,0:T(8,128)(2,1)S(1)}, u32[]{:S(2)}, u32[]{:S(2)}) collective-permute-start(bf16[1040,256]{1,0:T(8,128)(2,1)S(1)} %fusion.45.refs_0_), channel_id=1, source_target_pairs={{0,2},{2,0},{4,6},{6,4},{1,3},{3,1},{5,7},{7,5},{8,10},{10,8},{12,... | collective-permute-start | bytes 1597448 | tf_op jit(solution)/shard_map/ppermute | solution.py:39
  222.9 19.2 %collective-permute-start.14 = (bf16[1040,256]{1,0:T(8,128)(2,1)S(1)}, bf16[1040,256]{1,0:T(8,128)(2,1)}, u32[]{:S(2)}, u32[]{:S(2)}) collective-permute-start(bf16[1040,256]{1,0:T(8,128)(2,1)S(1)} %fusion.45.refs_0_), channel_id=1, source_target_pairs={{0,8},{8,0},{1,9},{9,1},{2,10},{10,2},{3,11},{11,3},{4,12},{12,4},... | collective-permute-start | bytes 1597448 | tf_op jit(solution)/shard_map/ppermute | solution.py:43
  276.5 32.6 %collective-permute-start.22 = (bf16[1040,256]{1,0:T(8,128)(2,1)S(1)}, bf16[1040,256]{1,0:T(8,128)(2,1)S(1)}, u32[]{:S(2)}, u32[]{:S(2)}) collective-permute-start(bf16[1040,256]{1,0:T(8,128)(2,1)S(1)} %get-tuple-element.333), channel_id=1, source_target_pairs={{0,2},{2,0},{4,6},{6,4},{1,3},{3,1},{5,7},{7,5},{8,10},{10,8},{12,... | collective-permute-start | bytes 1597448 | tf_op jit(solution)/shard_map/ppermute | solution.py:39
  290.2 24.5 %collective-permute-start.24 = (bf16[1040,256]{1,0:T(8,128)(2,1)S(1)}, bf16[1040,256]{1,0:T(8,128)(2,1)S(1)}, u32[]{:S(2)}, u32[]{:S(2)}) collective-permute-start(bf16[1040,256]{1,0:T(8,128)(2,1)S(1)} %add_convert_fusion.6), channel_id=1, source_target_pairs={{0,4},{2,6},{4,0},{6,2},{1,5},{3,7},{5,1},{7,3},{8,12},{10,14},{12... | collective-permute-start | bytes 1597448 | tf_op jit(solution)/shard_map/ppermute | solution.py:39
  315.3 25.1 %collective-permute-start.28 = (bf16[1040,256]{1,0:T(8,128)(2,1)S(1)}, bf16[1040,256]{1,0:T(8,128)(2,1)}, u32[]{:S(2)}, u32[]{:S(2)}) collective-permute-start(bf16[1040,256]{1,0:T(8,128)(2,1)S(1)} %fusion.46.refs_0_), channel_id=1, source_target_pairs={{0,4},{2,6},{4,0},{6,2},{1,5},{3,7},{5,1},{7,3},{8,12},{10,14},{12... | collective-permute-start | bytes 1597448 | tf_op jit(solution)/shard_map/ppermute | solution.py:39
  315.4 25.6 %collective-permute-start.26 = (bf16[1040,256]{1,0:T(8,128)(2,1)S(1)}, bf16[1040,256]{1,0:T(8,128)(2,1)}, u32[]{:S(2)}, u32[]{:S(2)}) collective-permute-start(bf16[1040,256]{1,0:T(8,128)(2,1)S(1)} %fusion.46.refs_0_), channel_id=1, source_target_pairs={{0,2},{2,0},{4,6},{6,4},{1,3},{3,1},{5,7},{7,5},{8,10},{10,8},{12,... | collective-permute-start | bytes 1597448 | tf_op jit(solution)/shard_map/ppermute | solution.py:39
  357.3 303.4 %reduce-scatter.7.cloned.1.call-start = ((), (), s32[]{:S(2)}) async-start(), calls=%async_computation.12 | async-start | bytes 5242880 | tf_op jit(solution)/shard_map/reduce_scatter | solution.py:545
  376.3 25.9 %collective-permute-start.36 = (bf16[1024,256]{1,0:T(8,128)(2,1)S(1)}, bf16[1024,256]{1,0:T(8,128)(2,1)S(1)}, u32[]{:S(2)}, u32[]{:S(2)}) collective-permute-start(bf16[1024,256]{1,0:T(8,128)(2,1)S(1)} %convert_element_type.656.refs_0_), channel_id=1, source_target_pairs={{0,4},{2,6},{4,0},{6,2},{1,5},{3,7},{5,1},{7,3},{8,12},{10,14},{12... | collective-permute-start | bytes 1572872 | tf_op jit(solution)/shard_map/ppermute | solution.py:39
  377.5 28.5 %collective-permute-start.34 = (bf16[1024,256]{1,0:T(8,128)(2,1)S(1)}, bf16[1024,256]{1,0:T(8,128)(2,1)S(1)}, u32[]{:S(2)}, u32[]{:S(2)}) collective-permute-start(bf16[1024,256]{1,0:T(8,128)(2,1)S(1)} %convert_element_type.656.refs_0_), channel_id=1, source_target_pairs={{0,2},{2,0},{4,6},{6,4},{1,3},{3,1},{5,7},{7,5},{8,10},{10,8},{12,... | collective-permute-start | bytes 1572872 | tf_op jit(solution)/shard_map/ppermute | solution.py:39
  405.2 23.8 %collective-permute-start.33 = (bf16[1024,256]{1,0:T(8,128)(2,1)S(1)}, bf16[1024,256]{1,0:T(8,128)(2,1)S(1)}, u32[]{:S(2)}, u32[]{:S(2)}) collective-permute-start(bf16[1024,256]{1,0:T(8,128)(2,1)S(1)} %convert_element_type.656.refs_0_), channel_id=1, source_target_pairs={{0,8},{8,0},{1,9},{9,1},{2,10},{10,2},{3,11},{11,3},{4,12},{12,4},... | collective-permute-start | bytes 1572872 | tf_op jit(solution)/shard_map/ppermute | solution.py:43
  405.9 23.2 %collective-permute-start.37 = (bf16[1024,256]{1,0:T(8,128)(2,1)S(1)}, bf16[1024,256]{1,0:T(8,128)(2,1)S(1)}, u32[]{:S(2)}, u32[]{:S(2)}) collective-permute-start(bf16[1024,256]{1,0:T(8,128)(2,1)S(1)} %collective-permute-done.36.refs_4_), channel_id=1, source_target_pairs={{0,8},{8,0},{1,9},{9,1},{2,10},{10,2},{3,11},{11,3},{4,12},{12,4},... | collective-permute-start | bytes 1572872 | tf_op jit(solution)/shard_map/ppermute | solution.py:43
  406.0 23.0 %collective-permute-start.35 = (bf16[1024,256]{1,0:T(8,128)(2,1)S(1)}, bf16[1024,256]{1,0:T(8,128)(2,1)S(1)}, u32[]{:S(2)}, u32[]{:S(2)}) collective-permute-start(bf16[1024,256]{1,0:T(8,128)(2,1)S(1)} %collective-permute-done.34.refs_2_), channel_id=1, source_target_pairs={{0,8},{8,0},{1,9},{9,1},{2,10},{10,2},{3,11},{11,3},{4,12},{12,4},... | collective-permute-start | bytes 1572872 | tf_op jit(solution)/shard_map/ppermute | solution.py:43
  436.1 34.0 %collective-permute-start.41 = (bf16[1040,256]{1,0:T(8,128)(2,1)S(1)}, bf16[1040,256]{1,0:T(8,128)(2,1)S(1)}, u32[]{:S(2)}, u32[]{:S(2)}) collective-permute-start(bf16[1040,256]{1,0:T(8,128)(2,1)S(1)} %get-tuple-element.332), channel_id=1, source_target_pairs={{0,2},{2,0},{4,6},{6,4},{1,3},{3,1},{5,7},{7,5},{8,10},{10,8},{12,... | collective-permute-start | bytes 1597448 | tf_op jit(solution)/shard_map/ppermute | solution.py:39
  449.8 24.5 %collective-permute-start.43 = (bf16[1040,256]{1,0:T(8,128)(2,1)S(1)}, bf16[1040,256]{1,0:T(8,128)(2,1)S(1)}, u32[]{:S(2)}, u32[]{:S(2)}) collective-permute-start(bf16[1040,256]{1,0:T(8,128)(2,1)S(1)} %add_convert_fusion.5), channel_id=1, source_target_pairs={{0,4},{2,6},{4,0},{6,2},{1,5},{3,7},{5,1},{7,3},{8,12},{10,14},{12... | collective-permute-start | bytes 1597448 | tf_op jit(solution)/shard_map/ppermute | solution.py:39
  475.0 26.5 %collective-permute-start.47 = (bf16[1040,256]{1,0:T(8,128)(2,1)S(1)}, bf16[1040,256]{1,0:T(8,128)(2,1)}, u32[]{:S(2)}, u32[]{:S(2)}) collective-permute-start(bf16[1040,256]{1,0:T(8,128)(2,1)S(1)} %fusion.47.refs_0_), channel_id=1, source_target_pairs={{0,4},{2,6},{4,0},{6,2},{1,5},{3,7},{5,1},{7,3},{8,12},{10,14},{12... | collective-permute-start | bytes 1597448 | tf_op jit(solution)/shard_map/ppermute | solution.py:39
  476.3 28.6 %collective-permute-start.45 = (bf16[1040,256]{1,0:T(8,128)(2,1)S(1)}, bf16[1040,256]{1,0:T(8,128)(2,1)}, u32[]{:S(2)}, u32[]{:S(2)}) collective-permute-start(bf16[1040,256]{1,0:T(8,128)(2,1)S(1)} %fusion.47.refs_0_), channel_id=1, source_target_pairs={{0,2},{2,0},{4,6},{6,4},{1,3},{3,1},{5,7},{7,5},{8,10},{10,8},{12,... | collective-permute-start | bytes 1597448 | tf_op jit(solution)/shard_map/ppermute | solution.py:39
  574.0 213.7 %reduce-scatter.9.cloned.1.call-start = ((), (), s32[]{:S(2)}) async-start(), calls=%async_computation.13 | async-start | bytes 5242880 | tf_op jit(solution)/shard_map/reduce_scatter | solution.py:545
  574.3 31.7 %collective-permute-start.52 = (bf16[1040,256]{1,0:T(8,128)(2,1)}, bf16[1040,256]{1,0:T(8,128)(2,1)S(1)}, u32[]{:S(2)}, u32[]{:S(2)}) collective-permute-start(bf16[1040,256]{1,0:T(8,128)(2,1)} %get-tuple-element.329), channel_id=1, source_target_pairs={{0,2},{2,0},{4,6},{6,4},{1,3},{3,1},{5,7},{7,5},{8,10},{10,8},{12,... | collective-permute-start | bytes 1597448 | tf_op jit(solution)/shard_map/ppermute | solution.py:39
  589.1 24.2 %collective-permute-start.54 = (bf16[1040,256]{1,0:T(8,128)(2,1)S(1)}, bf16[1040,256]{1,0:T(8,128)(2,1)S(1)}, u32[]{:S(2)}, u32[]{:S(2)}) collective-permute-start(bf16[1040,256]{1,0:T(8,128)(2,1)S(1)} %add_convert_fusion.4), channel_id=1, source_target_pairs={{0,4},{2,6},{4,0},{6,2},{1,5},{3,7},{5,1},{7,3},{8,12},{10,14},{12... | collective-permute-start | bytes 1597448 | tf_op jit(solution)/shard_map/ppermute | solution.py:39
  615.4 24.7 %collective-permute-start.58 = (bf16[1024,256]{1,0:T(8,128)(2,1)S(1)}, bf16[1024,256]{1,0:T(8,128)(2,1)S(1)}, u32[]{:S(2)}, u32[]{:S(2)}) collective-permute-start(bf16[1024,256]{1,0:T(8,128)(2,1)S(1)} %convert_element_type.689.refs_0_), channel_id=1, source_target_pairs={{0,4},{2,6},{4,0},{6,2},{1,5},{3,7},{5,1},{7,3},{8,12},{10,14},{12... | collective-permute-start | bytes 1572872 | tf_op jit(solution)/shard_map/ppermute | solution.py:39
  615.5 25.1 %collective-permute-start.56 = (bf16[1024,256]{1,0:T(8,128)(2,1)S(1)}, bf16[1024,256]{1,0:T(8,128)(2,1)}, u32[]{:S(2)}, u32[]{:S(2)}) collective-permute-start(bf16[1024,256]{1,0:T(8,128)(2,1)S(1)} %convert_element_type.689.refs_0_), channel_id=1, source_target_pairs={{0,2},{2,0},{4,6},{6,4},{1,3},{3,1},{5,7},{7,5},{8,10},{10,8},{12,... | collective-permute-start | bytes 1572872 | tf_op jit(solution)/shard_map/ppermute | solution.py:39
  640.1 20.7 %collective-permute-start.55 = (bf16[1024,256]{1,0:T(8,128)(2,1)S(1)}, bf16[1024,256]{1,0:T(8,128)(2,1)}, u32[]{:S(2)}, u32[]{:S(2)}) collective-permute-start(bf16[1024,256]{1,0:T(8,128)(2,1)S(1)} %convert_element_type.689.refs_0_), channel_id=1, source_target_pairs={{0,8},{8,0},{1,9},{9,1},{2,10},{10,2},{3,11},{11,3},{4,12},{12,4},... | collective-permute-start | bytes 1572872 | tf_op jit(solution)/shard_map/ppermute | solution.py:43
  640.6 20.1 %collective-permute-start.59 = (bf16[1024,256]{1,0:T(8,128)(2,1)S(1)}, bf16[1024,256]{1,0:T(8,128)(2,1)}, u32[]{:S(2)}, u32[]{:S(2)}) collective-permute-start(bf16[1024,256]{1,0:T(8,128)(2,1)S(1)} %collective-permute-done.58.refs_4_), channel_id=1, source_target_pairs={{0,8},{8,0},{1,9},{9,1},{2,10},{10,2},{3,11},{11,3},{4,12},{12,4},... | collective-permute-start | bytes 1572872 | tf_op jit(solution)/shard_map/ppermute | solution.py:43
  640.6 20.1 %collective-permute-start.57 = (bf16[1024,256]{1,0:T(8,128)(2,1)}, bf16[1024,256]{1,0:T(8,128)(2,1)}, u32[]{:S(2)}, u32[]{:S(2)}) collective-permute-start(bf16[1024,256]{1,0:T(8,128)(2,1)} %collective-permute-done.56.refs_2_), channel_id=1, source_target_pairs={{0,8},{8,0},{1,9},{9,1},{2,10},{10,2},{3,11},{11,3},{4,12},{12,4},... | collective-permute-start | bytes 1572872 | tf_op jit(solution)/shard_map/ppermute | solution.py:43
  688.9 218.1 %reduce-scatter.11.cloned.1.call-start = ((), (), s32[]{:S(2)}) async-start(), calls=%async_computation.14 | async-start | bytes 5242880 | tf_op jit(solution)/shard_map/reduce_scatter | solution.py:545
  704.9 22.8 %collective-permute-start.63 = (bf16[1040,256]{1,0:T(8,128)(2,1)S(1)}, bf16[1040,256]{1,0:T(8,128)(2,1)S(1)}, u32[]{:S(2)}, u32[]{:S(2)}) collective-permute-start(bf16[1040,256]{1,0:T(8,128)(2,1)S(1)} %copy-done.118), channel_id=1, source_target_pairs={{0,2},{2,0},{4,6},{6,4},{1,3},{3,1},{5,7},{7,5},{8,10},{10,8},{12,... | collective-permute-start | bytes 1597448 | tf_op jit(solution)/shard_map/ppermute | solution.py:39
  707.9 20.7 %collective-permute-start.65 = (bf16[1040,256]{1,0:T(8,128)(2,1)S(1)}, bf16[1040,256]{1,0:T(8,128)(2,1)S(1)}, u32[]{:S(2)}, u32[]{:S(2)}) collective-permute-start(bf16[1040,256]{1,0:T(8,128)(2,1)S(1)} %fusion.30), channel_id=1, source_target_pairs={{0,4},{2,6},{4,0},{6,2},{1,5},{3,7},{5,1},{7,3},{8,12},{10,14},{12... | collective-permute-start | bytes 1597448 | tf_op jit(solution)/shard_map/ppermute | solution.py:39
  747.3 33.1 %collective-permute-start.68 = (bf16[1040,256]{1,0:T(8,128)(2,1)}, bf16[1040,256]{1,0:T(8,128)(2,1)}, u32[]{:S(2)}, u32[]{:S(2)}) collective-permute-start(bf16[1040,256]{1,0:T(8,128)(2,1)} %get-tuple-element.324), channel_id=1, source_target_pairs={{0,2},{2,0},{4,6},{6,4},{1,3},{3,1},{5,7},{7,5},{8,10},{10,8},{12,... | collective-permute-start | bytes 1597448 | tf_op jit(solution)/shard_map/ppermute | solution.py:39
  761.6 24.3 %collective-permute-start.70 = (bf16[1040,256]{1,0:T(8,128)(2,1)}, bf16[1040,256]{1,0:T(8,128)(2,1)}, u32[]{:S(2)}, u32[]{:S(2)}) collective-permute-start(bf16[1040,256]{1,0:T(8,128)(2,1)} %add_convert_fusion.3), channel_id=1, source_target_pairs={{0,4},{2,6},{4,0},{6,2},{1,5},{3,7},{5,1},{7,3},{8,12},{10,14},{12... | collective-permute-start | bytes 1597448 | tf_op jit(solution)/shard_map/ppermute | solution.py:39
  790.4 25.9 %collective-permute-start.74 = (bf16[1024,256]{1,0:T(8,128)(2,1)S(1)}, bf16[1024,256]{1,0:T(8,128)(2,1)S(1)}, u32[]{:S(2)}, u32[]{:S(2)}) collective-permute-start(bf16[1024,256]{1,0:T(8,128)(2,1)S(1)} %convert_element_type.720.refs_0_), channel_id=1, source_target_pairs={{0,4},{2,6},{4,0},{6,2},{1,5},{3,7},{5,1},{7,3},{8,12},{10,14},{12... | collective-permute-start | bytes 1572872 | tf_op jit(solution)/shard_map/ppermute | solution.py:39
  791.1 167.9 %reduce-scatter.13.cloned.1.call-start = ((), (), s32[]{:S(2)}) async-start(), calls=%async_computation.15 | async-start | bytes 5242880 | tf_op jit(solution)/shard_map/reduce_scatter | solution.py:545
  791.3 26.3 %collective-permute-start.72 = (bf16[1024,256]{1,0:T(8,128)(2,1)S(1)}, bf16[1024,256]{1,0:T(8,128)(2,1)S(1)}, u32[]{:S(2)}, u32[]{:S(2)}) collective-permute-start(bf16[1024,256]{1,0:T(8,128)(2,1)S(1)} %convert_element_type.720.refs_0_), channel_id=1, source_target_pairs={{0,2},{2,0},{4,6},{6,4},{1,3},{3,1},{5,7},{7,5},{8,10},{10,8},{12,... | collective-permute-start | bytes 1572872 | tf_op jit(solution)/shard_map/ppermute | solution.py:39
  864.8 223.6 %reduce-scatter.17.cloned.1.call-start = ((), (), s32[]{:S(2)}) async-start(), calls=%async_computation.17 | async-start | bytes 5242880 | tf_op jit(solution)/shard_map/reduce_scatter | solution.py:545
  864.9 31.7 %collective-permute-start.79 = (bf16[1040,256]{1,0:T(8,128)(2,1)}, bf16[1040,256]{1,0:T(8,128)(2,1)S(1)}, u32[]{:S(2)}, u32[]{:S(2)}) collective-permute-start(bf16[1040,256]{1,0:T(8,128)(2,1)} %get-tuple-element.321), channel_id=1, source_target_pairs={{0,2},{2,0},{4,6},{6,4},{1,3},{3,1},{5,7},{7,5},{8,10},{10,8},{12,... | collective-permute-start | bytes 1597448 | tf_op jit(solution)/shard_map/ppermute | solution.py:39
  880.0 24.7 %collective-permute-start.81 = (bf16[1040,256]{1,0:T(8,128)(2,1)S(1)}, bf16[1040,256]{1,0:T(8,128)(2,1)S(1)}, u32[]{:S(2)}, u32[]{:S(2)}) collective-permute-start(bf16[1040,256]{1,0:T(8,128)(2,1)S(1)} %add_convert_fusion.2), channel_id=1, source_target_pairs={{0,4},{2,6},{4,0},{6,2},{1,5},{3,7},{5,1},{7,3},{8,12},{10,14},{12... | collective-permute-start | bytes 1597448 | tf_op jit(solution)/shard_map/ppermute | solution.py:39
  917.3 173.8 %reduce-scatter.15.cloned.1.call-start = ((), (), s32[]{:S(2)}) async-start(), calls=%async_computation.16 | async-start | bytes 5242880 | tf_op jit(solution)/shard_map/reduce_scatter | solution.py:545
  918.5 24.4 %collective-permute-start.86 = (bf16[1024,256]{1,0:T(8,128)(2,1)S(1)}, bf16[1024,256]{1,0:T(8,128)(2,1)S(1)}, u32[]{:S(2)}, u32[]{:S(2)}) collective-permute-start(bf16[1024,256]{1,0:T(8,128)(2,1)S(1)} %convert_element_type.738.refs_0_), channel_id=1, source_target_pairs={{0,4},{2,6},{4,0},{6,2},{1,5},{3,7},{5,1},{7,3},{8,12},{10,14},{12... | collective-permute-start | bytes 1572872 | tf_op jit(solution)/shard_map/ppermute | solution.py:39
  918.6 24.9 %collective-permute-start.84 = (bf16[1024,256]{1,0:T(8,128)(2,1)S(1)}, bf16[1024,256]{1,0:T(8,128)(2,1)S(1)}, u32[]{:S(2)}, u32[]{:S(2)}) collective-permute-start(bf16[1024,256]{1,0:T(8,128)(2,1)S(1)} %convert_element_type.738.refs_0_), channel_id=1, source_target_pairs={{0,2},{2,0},{4,6},{6,4},{1,3},{3,1},{5,7},{7,5},{8,10},{10,8},{12,... | collective-permute-start | bytes 1572872 | tf_op jit(solution)/shard_map/ppermute | solution.py:39
  1000.5 32.9 %collective-permute-start.91 = (bf16[1040,256]{1,0:T(8,128)(2,1)}, bf16[1040,256]{1,0:T(8,128)(2,1)}, u32[]{:S(2)}, u32[]{:S(2)}) collective-permute-start(bf16[1040,256]{1,0:T(8,128)(2,1)} %get-tuple-element.317), channel_id=1, source_target_pairs={{0,2},{2,0},{4,6},{6,4},{1,3},{3,1},{5,7},{7,5},{8,10},{10,8},{12,... | collective-permute-start | bytes 1597448 | tf_op jit(solution)/shard_map/ppermute | solution.py:39
  1014.9 24.4 %collective-permute-start.93 = (bf16[1040,256]{1,0:T(8,128)(2,1)}, bf16[1040,256]{1,0:T(8,128)(2,1)}, u32[]{:S(2)}, u32[]{:S(2)}) collective-permute-start(bf16[1040,256]{1,0:T(8,128)(2,1)} %fusion.29), channel_id=1, source_target_pairs={{0,4},{2,6},{4,0},{6,2},{1,5},{3,7},{5,1},{7,3},{8,12},{10,14},{12... | collective-permute-start | bytes 1597448 | tf_op jit(solution)/shard_map/ppermute | solution.py:39
  1016.1 63.8 %collective-permute-start.103 = (bf16[512,1024]{1,0:T(8,128)(2,1)S(1)}, bf16[512,1024]{1,0:T(8,128)(2,1)}, u32[]{:S(2)}, u32[]{:S(2)}) collective-permute-start(bf16[512,1024]{1,0:T(8,128)(2,1)S(1)} %copy-done.39), channel_id=1, source_target_pairs={{1,8},{8,1},{3,10},{10,3},{5,12},{12,5},{7,14},{14,7},{17,24},{24,... | collective-permute-start | bytes 3145736 | tf_op jit(solution)/shard_map/ppermute | solution.py:549
  1021.2 61.6 %collective-permute-start.66 = (f32[1024,256]{1,0:T(8,128)}, f32[1024,256]{1,0:T(8,128)}, u32[]{:S(2)}, u32[]{:S(2)}) collective-permute-start(f32[1024,256]{1,0:T(8,128)} %fusion.33), channel_id=1, source_target_pairs={{1,8},{8,1},{3,10},{10,3},{5,12},{12,5},{7,14},{14,7},{17,24},{24,... | collective-permute-start | bytes 3145736 | tf_op jit(solution)/shard_map/ppermute | solution.py:48
  1023.2 62.3 %collective-permute-start.82 = (f32[1024,256]{1,0:T(8,128)}, f32[1024,256]{1,0:T(8,128)}, u32[]{:S(2)}, u32[]{:S(2)}) collective-permute-start(f32[1024,256]{1,0:T(8,128)} %get-tuple-element.339), channel_id=1, source_target_pairs={{1,8},{8,1},{3,10},{10,3},{5,12},{12,5},{7,14},{14,7},{17,24},{24,... | collective-permute-start | bytes 3145736 | tf_op jit(solution)/shard_map/ppermute | solution.py:48
  1033.4 55.0 %collective-permute-start.102 = (bf16[512,1024]{1,0:T(8,128)(2,1)}, bf16[512,1024]{1,0:T(8,128)(2,1)}, u32[]{:S(2)}, u32[]{:S(2)}) collective-permute-start(bf16[512,1024]{1,0:T(8,128)(2,1)} %reduce-scatter.13.cloned.1.call-done.refs_0_), channel_id=1, source_target_pairs={{1,8},{8,1},{3,10},{10,3},{5,12},{12,5},{7,14},{14,7},{17,24},{24,... | collective-permute-start | bytes 3145736 | tf_op jit(solution)/shard_map/ppermute | solution.py:549
  1046.3 32.0 %collective-permute-start.96 = (f32[2,12,256]{2,0,1:T(2,128)S(1)}, f32[2,12,256]{2,0,1:T(2,128)S(1)}, u32[]{:S(2)}, u32[]{:S(2)}) collective-permute-start(f32[2,12,256]{2,0,1:T(2,128)S(1)} %fusion.127), channel_id=1, source_target_pairs={{0,1},{1,0},{2,3},{3,2},{4,5},{5,4},{6,7},{7,6},{8,9},{9,8},{10,11... | collective-permute-start | bytes 73736 | tf_op jit(solution)/shard_map/ppermute | solution.py:799
  1079.9 35.6 %collective-permute-start.101 = (bf16[512,1024]{1,0:T(8,128)(2,1)S(1)}, bf16[512,1024]{1,0:T(8,128)(2,1)}, u32[]{:S(2)}, u32[]{:S(2)}) collective-permute-start(bf16[512,1024]{1,0:T(8,128)(2,1)S(1)} %copy-done.40), channel_id=1, source_target_pairs={{1,8},{8,1},{3,10},{10,3},{5,12},{12,5},{7,14},{14,7},{17,24},{24,... | collective-permute-start | bytes 3145736 | tf_op jit(solution)/shard_map/ppermute | solution.py:549
  1082.8 47.6 %collective-permute-start.99 = (bf16[512,1024]{1,0:T(8,128)(2,1)S(1)}, bf16[512,1024]{1,0:T(8,128)(2,1)}, u32[]{:S(2)}, u32[]{:S(2)}) collective-permute-start(bf16[512,1024]{1,0:T(8,128)(2,1)S(1)} %copy-done.41), channel_id=1, source_target_pairs={{1,8},{8,1},{3,10},{10,3},{5,12},{12,5},{7,14},{14,7},{17,24},{24,... | collective-permute-start | bytes 3145736 | tf_op jit(solution)/shard_map/ppermute | solution.py:549
  1085.5 27.5 %collective-permute-start.94 = (bf16[1024,256]{1,0:T(8,128)(2,1)}, bf16[1024,256]{1,0:T(8,128)(2,1)}, u32[]{:S(2)}, u32[]{:S(2)}) collective-permute-start(bf16[1024,256]{1,0:T(8,128)(2,1)} %get-tuple-element.340), channel_id=1, source_target_pairs={{1,8},{8,1},{3,10},{10,3},{5,12},{12,5},{7,14},{14,7},{17,24},{24,... | collective-permute-start | bytes 1572872 | tf_op jit(solution)/shard_map/ppermute | solution.py:48
  1088.4 35.7 %collective-permute-start.100 = (bf16[512,1024]{1,0:T(8,128)(2,1)}, bf16[512,1024]{1,0:T(8,128)(2,1)}, u32[]{:S(2)}, u32[]{:S(2)}) collective-permute-start(bf16[512,1024]{1,0:T(8,128)(2,1)} %reduce-scatter.17.cloned.1.call-done.refs_0_), channel_id=1, source_target_pairs={{1,8},{8,1},{3,10},{10,3},{5,12},{12,5},{7,14},{14,7},{17,24},{24,... | collective-permute-start | bytes 3145736 | tf_op jit(solution)/shard_map/ppermute | solution.py:549
  1091.1 44.2 %collective-permute-start.98 = (bf16[512,1024]{1,0:T(8,128)(2,1)}, bf16[512,1024]{1,0:T(8,128)(2,1)S(1)}, u32[]{:S(2)}, u32[]{:S(2)}) collective-permute-start(bf16[512,1024]{1,0:T(8,128)(2,1)} %reduce-scatter.15.cloned.1.call-done.refs_0_), channel_id=1, source_target_pairs={{1,8},{8,1},{3,10},{10,3},{5,12},{12,5},{7,14},{14,7},{17,24},{24,... | collective-permute-start | bytes 3145736 | tf_op jit(solution)/shard_map/ppermute | solution.py:549
  (181 other events, 2548.9 us)
Sparse Core Ops, SparseCore 0:
  35.1 57.3 all-gather.6
  95.0 57.6 all-gather.8
  155.1 54.3 all-gather.10
  211.3 54.3 all-gather.12
  267.4 54.3 all-gather.14
  357.4 53.7 all-gather.16
  574.1 50.7 reduce-scatter.6
  689.0 52.3 reduce-scatter.8
  791.2 54.9 reduce-scatter.10
  864.9 50.6 reduce-scatter.12
  919.1 52.6 reduce-scatter.16
  985.1 57.2 reduce-scatter.14

commit v3 on v2

--- a/solution.py
+++ b/solution.py
@@ -15,6 +15,15 @@
 LANES = 128
 CHUNKS = 1
 MIB = 2**20
+SCALE = 0.25
+
+
+def cost(flops, bytes_accessed, transcendentals):
+    return pl.CostEstimate(
+        flops=int(flops * SCALE),
+        bytes_accessed=int(bytes_accessed * SCALE),
+        transcendentals=int(transcendentals * SCALE),
+    )
 
 norm_eps = 1e-05
 masked_score = -1e30
@@ -66,9 +75,8 @@
 
 
 def pair_blocks(mine, other):
-    got = partner(other)
-    pair = mine.astype(F32) + got.astype(F32)
-    return [pair[0]] + [pair[k].astype(BF16) for k in range(1, ring_size())]
+    pair = [m.astype(F32) + partner(o).astype(F32) for m, o in zip(mine, other)]
+    return [pair[0]] + [p.astype(BF16) for p in pair[1:]]
 
 
 def ring_sum(pair):
@@ -84,109 +92,230 @@
     return pl.BlockSpec(shape, lambda *_: (0,) * len(shape))
 
 
-def assemble_norm_kernel(slots, width, blocks_ref, *refs):
+class Columns:
+    def __init__(self, blocks, n, at=0):
+        self.blocks, self.n, self.at = blocks, n, at
+
+    def whole(self):
+        rows, _, size, _ = self.blocks.shape
+        at = self.at
+        return pl.BlockSpec((rows, 1, size, self.n), lambda g, b, c, *_: (0, c[0], 0, at))
+
+    def block(self, k, f):
+        per, at = self.blocks.shape[2] // f, self.at
+        return pl.BlockSpec((1, 1, f, self.n), lambda g, b, c, *_: (b[k] // per, c[0], b[k] % per, at))
+
+
+def core_index():
+    return lax.axis_index("c").astype(jnp.int32).reshape(1)
+
+
+def matrix(ref):
+    return ref[...].reshape(-1, ref.shape[-1])
+
+
+def assembled(shards, blocks_ref, out_ref):
+    f = shards[0].shape[1]
+    for s, shard in enumerate(shards):
+        out_ref[:, pl.ds(pl.multiple_of(blocks_ref[s] * f, f), f)] = shard[...].astype(BF16)
+
+
+def norm_kernel(slots, width, gelu, blocks_ref, core_ref, *refs):
     shards = refs[:slots]
-    means_ref, spread_ref, gain_ref, shift_ref, own_ref = refs[slots : slots + 5]
-    out_ref, centred_ref, inverse_ref = refs[slots + 5 :]
+    means_ref, spread_ref, gain_ref, shift_ref, own_ref, w_ref, bias_ref, rows_ref = refs[slots : slots + 8]
+    out_ref, centred_ref, inverse_ref, products_ref, *hidden_refs = refs[slots + 8 :]
     f = shards[0].shape[1]
-    offsets = lax.dot_general(
-        means_ref[0].astype(BF16),
-        spread_ref[...],
-        (((0,), (0,)), ((), ())),
-        preferred_element_type=F32,
-    )
-    values = [shards[s][...].astype(F32) + offsets[:, s * f : (s + 1) * f] for s in range(slots)]
-    total = values[0]
-    for v in values[1:]:
-        total = total + v
-    mean = jnp.sum(total, axis=1, keepdims=True) / width
-    values = [v - mean for v in values]
-    squares = values[0] * values[0]
-    for v in values[1:]:
-        squares = squares + v * v
-    inverse = lax.rsqrt(jnp.sum(squares, axis=1, keepdims=True) / width + norm_eps)
-    for s in range(slots):
-        block = blocks_ref[s]
-        normed = values[s] * inverse * gain_ref[s] + shift_ref[s]
-        out_ref[:, pl.ds(pl.multiple_of(block * f, f), f)] = normed.astype(BF16)
-    centred_ref[...] = (own_ref[...] - mean) * inverse
-    inverse_ref[...] = jnp.broadcast_to(inverse, inverse_ref.shape)
-
-
-def assemble_norm(shards, own, gain, shift):
+    tokens = own_ref.shape[0]
+    for g in range(tokens // LANES):
+        at = pl.ds(g * LANES, LANES)
+        offsets = lax.dot_general(
+            means_ref[g].astype(BF16),
+            spread_ref[...],
+            (((0,), (0,)), ((), ())),
+            preferred_element_type=F32,
+        )
+        values = [shards[s][at, :].astype(F32) + offsets[:, s * f : (s + 1) * f] for s in range(slots)]
+        mean = jnp.sum(added(values), axis=1, keepdims=True) / width
+        values = [v - mean for v in values]
+        squares = added([v * v for v in values])
+        inverse = lax.rsqrt(jnp.sum(squares, axis=1, keepdims=True) / width + norm_eps)
+        for s in range(slots):
+            normed = values[s] * inverse * gain_ref[s] + shift_ref[s]
+            out_ref[at, pl.ds(pl.multiple_of(blocks_ref[s] * f, f), f)] = normed.astype(BF16)
+        centred_ref[at, :] = (own_ref[at, :] - mean) * inverse
+        inverse_ref[at, :] = jnp.broadcast_to(inverse, (LANES, LANES))
+    hidden = jnp.dot(out_ref[...], matrix(w_ref), preferred_element_type=F32) + bias_ref[...]
+
+    @pl.when(pl.program_id(0) == 0)
+    def _():
+        products_ref[...] = jnp.dot(rows_ref[...], matrix(w_ref), preferred_element_type=F32)
+
+    if gelu:
+        upper_ref, active_ref = hidden_refs
+        upper_ref[...] = hidden
+        active_ref[...] = gelu_tanh(hidden).astype(BF16)
+    else:
+        hidden_refs[0][...] = hidden.astype(BF16)
+
+
+def norm_matmul(shards, own, gain, shift, w, bias, rows_to_multiply, gelu):
     slots = len(shards)
     tokens, f = own.shape
     width = slots * f
+    n = w.n
     groups = tokens // LANES
     means = jnp.stack([s[tokens : tokens + groups, :LANES] for s in shards], axis=1).astype(F32)
     spread = jnp.repeat(jnp.eye(slots, dtype=BF16), f, axis=1)
-    tile = LANES
+    tile = min(tokens, 256)
+    rows = lambda columns: pl.BlockSpec((tile, columns), lambda g, *_: (g, 0))
+    outs = [(width, BF16), (f, F32), (LANES, F32)]
+    hidden_outs = [(n, F32), (n, BF16)] if gelu else [(n, BF16)]
+    many = rows_to_multiply.shape[0]
     return pl.pallas_call(
-        functools.partial(assemble_norm_kernel, slots, width),
+        functools.partial(norm_kernel, slots, width, gelu),
         grid_spec=pltpu.PrefetchScalarGridSpec(
-            num_scalar_prefetch=1,
+            num_scalar_prefetch=2,
             grid=(tokens // tile,),
-            in_specs=[pl.BlockSpec((tile, f), lambda g, b: (g, 0))] * slots
+            in_specs=[rows(f)] * slots
             + [
-                pl.BlockSpec((1, slots, LANES), lambda g, b: (g, 0, 0)),
+                pl.BlockSpec((tile // LANES, slots, LANES), lambda g, *_: (g, 0, 0)),
                 whole((slots, width)),
                 whole((slots, 1, f)),
                 whole((slots, 1, f)),
-                pl.BlockSpec((tile, f), lambda g, b: (g, 0)),
+                rows(f),
+                w.whole(),
+                whole((1, n)),
+                whole((many, width)),
             ],
-            out_specs=[
-                pl.BlockSpec((tile, width), lambda g, b: (g, 0)),
-                pl.BlockSpec((tile, f), lambda g, b: (g, 0)),
-                pl.BlockSpec((tile, LANES), lambda g, b: (g, 0)),
-            ],
-        ),
-        out_shape=[
-            jax.ShapeDtypeStruct((tokens, width), BF16),
-            jax.ShapeDtypeStruct((tokens, f), F32),
-            jax.ShapeDtypeStruct((tokens, LANES), F32),
-        ],
-        compiler_params=pltpu.CompilerParams(vmem_limit_bytes=24 * MIB),
-        cost_estimate=pl.CostEstimate(
-            flops=12 * tokens * width, bytes_accessed=6 * tokens * width, transcendentals=tokens
-        ),
-        name="assemble_norm",
+            out_specs=[rows(columns) for columns, _ in outs]
+            + [whole((many, n))]
+            + [rows(columns) for columns, _ in hidden_outs],
+        ),
+        out_shape=[jax.ShapeDtypeStruct((tokens, columns), kind) for columns, kind in outs]
+        + [jax.ShapeDtypeStruct((many, n), F32)]
+        + [jax.ShapeDtypeStruct((tokens, columns), kind) for columns, kind in hidden_outs],
+        compiler_params=pltpu.CompilerParams(vmem_limit_bytes=60 * MIB),
+        cost_estimate=cost(
+            flops=2 * tokens * width * n, bytes_accessed=8 * tokens * width, transcendentals=tokens
+        ),
+        name="norm_matmul",
     )(
         slot_blocks(),
+        core_index(),
         *shards,
         means,
         spread,
         gain.reshape(slots, 1, f),
         shift.reshape(slots, 1, f),
         own,
+        w.blocks,
+        bias.reshape(1, n),
+        rows_to_multiply,
     )
 
 
-def assemble_kernel(slots, blocks_ref, *refs):
-    out_ref = refs[slots]
-    f = refs[0].shape[1]
-    for s in range(slots):
-        out_ref[:, pl.ds(pl.multiple_of(blocks_ref[s] * f, f), f)] = refs[s][...]
-
-
-def assemble(shards):
+def hidden_back_kernel(slots, blocks_ref, core_ref, *refs):
+    shards = refs[:slots]
+    w_ref, upper_ref, rows_ref, base_ref = refs[slots : slots + 4]
+    out_ref, grad_ref, sums_ref, bias_ref = refs[slots + 4 :]
+    assembled(shards, blocks_ref, out_ref)
+    tokens = upper_ref.shape[0]
+    u = upper_ref[...]
+    k = math.sqrt(2.0 / math.pi)
+    t = jnp.tanh(k * (u + 0.044715 * (u * u * u)))
+    slope = 0.5 * (1.0 + t) + 0.5 * u * (1.0 - t * t) * (k * (1.0 + 3 * 0.044715 * (u * u)))
+    grad = (jnp.dot(out_ref[...], matrix(w_ref), preferred_element_type=F32) * slope).astype(BF16)
+    grad_ref[...] = grad
+    wide = grad.astype(F32)
+    second = (wide * (u - base_ref[...])).astype(BF16)
+    by_columns = (((1,), (1,)), ((), ()))
+    for g in range(tokens // LANES):
+        at = slice(g * LANES, (g + 1) * LANES)
+        first = lax.dot_general(rows_ref[...], grad[at], by_columns, preferred_element_type=F32)
+        ones = jnp.ones(rows_ref.shape, BF16)
+        other = lax.dot_general(ones, second[at], by_columns, preferred_element_type=F32)
+        sums_ref[g, 0:1, :] = first[0:1] + first[1:2]
+        sums_ref[g, 1:2, :] = other[0:1]
+        sums_ref[g, 2:, :] = jnp.zeros((6, LANES), F32)
+
+    @pl.when(pl.program_id(0) == 0)
+    def _():
+        bias_ref[...] = jnp.zeros(bias_ref.shape, F32)
+
+    bias_ref[...] += jnp.broadcast_to(jnp.sum(wide, axis=0, keepdims=True), bias_ref.shape)
+
+
+def hidden_back(shards, w, upper, product, base):
+    slots = len(shards)
+    f = shards[0].shape[1]
+    tokens, n = upper.shape
+    width = slots * f
+    tile = min(tokens, 256)
+    high = lax.reduce_precision(product, 8, 7)
+    pair = jnp.stack([high, product - high]).astype(BF16)
+    pair = jnp.pad(pair, ((0, 14), (0, 0)))
+    rows = lambda columns: pl.BlockSpec((tile, columns), lambda g, *_: (g, 0))
+    out, grad, sums, bias = pl.pallas_call(
+        functools.partial(hidden_back_kernel, slots),
+        grid_spec=pltpu.PrefetchScalarGridSpec(
+            num_scalar_prefetch=2,
+            grid=(tokens // tile,),
+            in_specs=[rows(f)] * slots + [w.whole(), rows(n), whole((16, n)), whole((1, n))],
+            out_specs=[
+                rows(width),
+                rows(n),
+                pl.BlockSpec((tile // LANES, 8, LANES), lambda g, *_: (g, 0, 0)),
+                whole((8, n)),
+            ],
+        ),
+        out_shape=[
+            jax.ShapeDtypeStruct((tokens, width), BF16),
+            jax.ShapeDtypeStruct((tokens, n), BF16),
+            jax.ShapeDtypeStruct((tokens // LANES, 8, LANES), F32),
+            jax.ShapeDtypeStruct((8, n), F32),
+        ],
+        compiler_params=pltpu.CompilerParams(vmem_limit_bytes=60 * MIB),
+        cost_estimate=cost(
+            flops=2 * tokens * width * n, bytes_accessed=8 * tokens * width, transcendentals=tokens * n
+        ),
+        name="hidden_back",
+    )(slot_blocks(), core_index(), *shards, w.blocks, upper, pair, base.reshape(1, n))
+    extra = jnp.concatenate([sums[:, 0], sums[:, 1]], axis=0).astype(BF16)
+    extra = jnp.pad(extra, ((0, PAD - extra.shape[0]), (0, f - LANES)))
+    return out, grad, extra, bias[0]
+
+
+def gather_matmul_kernel(slots, blocks_ref, core_ref, *refs):
+    w_ref, out_ref, product_ref = refs[slots:]
+    assembled(refs[:slots], blocks_ref, out_ref)
+    product_ref[...] = jnp.dot(out_ref[...], matrix(w_ref), preferred_element_type=F32).astype(BF16)
+
+
+def gather_matmul(shards, w):
     slots = len(shards)
     tokens, f = shards[0].shape
+    width = slots * f
+    n = w.n
     tile = min(tokens, 256)
+    rows = lambda columns: pl.BlockSpec((tile, columns), lambda g, *_: (g, 0))
     return pl.pallas_call(
-        functools.partial(assemble_kernel, slots),
+        functools.partial(gather_matmul_kernel, slots),
         grid_spec=pltpu.PrefetchScalarGridSpec(
-            num_scalar_prefetch=1,
+            num_scalar_prefetch=2,
             grid=(tokens // tile,),
-            in_specs=[pl.BlockSpec((tile, f), lambda g, b: (g, 0))] * slots,
-            out_specs=pl.BlockSpec((tile, slots * f), lambda g, b: (g, 0)),
-        ),
-        out_shape=jax.ShapeDtypeStruct((tokens, slots * f), BF16),
-        compiler_params=pltpu.CompilerParams(vmem_limit_bytes=24 * MIB),
-        cost_estimate=pl.CostEstimate(
-            flops=0, bytes_accessed=4 * tokens * slots * f, transcendentals=0
-        ),
-        name="assemble",
-    )(slot_blocks(), *shards)
+            in_specs=[rows(f)] * slots + [w.whole()],
+            out_specs=[rows(width), rows(n)],
+        ),
+        out_shape=[
+            jax.ShapeDtypeStruct((tokens, width), BF16),
+            jax.ShapeDtypeStruct((tokens, n), BF16),
+        ],
+        compiler_params=pltpu.CompilerParams(vmem_limit_bytes=60 * MIB),
+        cost_estimate=cost(
+            flops=2 * tokens * width * n, bytes_accessed=6 * tokens * width, transcendentals=0
+        ),
+        name="gather_matmul",
+    )(slot_blocks(), core_index(), *shards, w.blocks)
 
 
 def pack_kernel(turned, *refs):
@@ -199,7 +328,7 @@
 
 
 def pack(blocks, turned, layer):
-    tile = LANES
+    tile = min(blocks[0].shape[2 if turned[0] else 1], 256)
     rows = blocks[0].shape[2 if turned[0] else 1]
     counts = [b.shape[1 if t else 2] for b, t in zip(blocks, turned)]
     return pl.pallas_call(
@@ -214,7 +343,7 @@
         out_specs=pl.BlockSpec((tile, sum(counts)), lambda g: (g, 0)),
         out_shape=jax.ShapeDtypeStruct((rows, sum(counts)), BF16),
         compiler_params=pltpu.CompilerParams(vmem_limit_bytes=24 * MIB),
-        cost_estimate=pl.CostEstimate(
+        cost_estimate=cost(
             flops=0, bytes_accessed=6 * rows * sum(counts), transcendentals=0
         ),
         name="pack",
@@ -239,7 +368,7 @@
 def unpack(pairs, turned, counts):
     layers = len(pairs)
     rows, columns = pairs[0][0].shape
-    tile = LANES
+    tile = min(rows, 256)
     same = (lax.axis_index("c") == lax.axis_index("x")).astype(jnp.int32).reshape(1)
     return pl.pallas_call(
         functools.partial(unpack_kernel, layers, turned, counts),
@@ -262,22 +391,24 @@
             jax.ShapeDtypeStruct((layers, n, rows) if t else (layers, rows, n), F32)
             for n, t in zip(counts, turned)
         ],
-        compiler_params=pltpu.CompilerParams(vmem_limit_bytes=24 * MIB),
-        cost_estimate=pl.CostEstimate(
+        compiler_params=pltpu.CompilerParams(vmem_limit_bytes=32 * MIB),
+        cost_estimate=cost(
             flops=0, bytes_accessed=8 * layers * rows * columns, transcendentals=0
         ),
         name="unpack",
     )(same, *[v for pair in pairs for v in pair])
 
 
-def slot_matmul_kernel(tile, blocks_ref, x_ref, w_ref, extra_ref, out_ref):
+def slot_matmul_kernel(count, tile, blocks_ref, core_ref, x_ref, *refs):
+    weights, extra_ref, outs = refs[:count], refs[count], refs[count + 1 :]
     tokens = x_ref.shape[0]
-    for g in range(tokens // tile):
-        at = pl.ds(g * tile, tile)
-        out_ref[0, at, :] = lax.dot_general(
-            x_ref[at, :], w_ref[...], (((1,), (1,)), ((), ())), preferred_element_type=F32
-        ).astype(BF16)
-    out_ref[0, tokens:, :] = extra_ref[...]
+    for w_ref, out_ref in zip(weights, outs):
+        for g in range(tokens // tile):
+            at = pl.ds(g * tile, tile)
+            out_ref[at, :] = lax.dot_general(
+                x_ref[at, :], matrix(w_ref), (((1,), (1,)), ((), ())), preferred_element_type=F32
+            ).astype(BF16)
+        out_ref[tokens:, :] = extra_ref[...]
 
 
 def slot_matmul(x, w, extra, other):
@@ -287,26 +418,24 @@
     blocks = slot_blocks()[1 if other else 0 :: 2]
     tile = min(tokens, 512)
     return pl.pallas_call(
-        functools.partial(slot_matmul_kernel, tile),
+        functools.partial(slot_matmul_kernel, n, tile),
         grid_spec=pltpu.PrefetchScalarGridSpec(
-            num_scalar_prefetch=1,
-            grid=(n,),
-            in_specs=[
-                whole((tokens, depth)),
-                pl.BlockSpec((f, depth), lambda k, b: (b[k], 0)),
-                whole((PAD, f)),
-            ],
-            out_specs=pl.BlockSpec((1, tokens + PAD, f), lambda k, b: (k, 0, 0)),
-        ),
-        out_shape=jax.ShapeDtypeStruct((n, tokens + PAD, f), BF16),
-        compiler_params=pltpu.CompilerParams(vmem_limit_bytes=24 * MIB),
-        cost_estimate=pl.CostEstimate(
+            num_scalar_prefetch=2,
+            grid=(1,),
+            in_specs=[whole((tokens, depth))]
+            + [w.block(k, f) for k in range(n)]
+            + [whole((PAD, f))],
+            out_specs=[whole((tokens + PAD, f))] * n,
+        ),
+        out_shape=[jax.ShapeDtypeStruct((tokens + PAD, f), BF16)] * n,
+        compiler_params=pltpu.CompilerParams(vmem_limit_bytes=32 * MIB),
+        cost_estimate=cost(
             flops=2 * tokens * depth * n * f,
             bytes_accessed=2 * (tokens * depth + n * f * (depth + tokens)),
             transcendentals=0,
         ),
         name="slot_matmul",
-    )(blocks, x, w, extra)
+    )(blocks, core_index(), x, *[w.blocks] * n, extra)
 
 
 def column_sum(x, w, extra):
@@ -331,17 +460,33 @@
     context_ref, log_ref = refs[2 * chunk + 2 :]
     h, g = pl.program_id(0), pl.program_id(1)
     span = keys[0].shape[0]
+    for step in range(span // tile):
+
+        @pl.when(g == step)
+        def _():
+            attend_tile(
+                chunk, tile, step, length_ref[0], slope_ref[h], q_ref, keys, values, context_ref, log_ref
+            )
+
+
+def reach(chunk, m, tile, step, span):
+    return span if m < chunk else (step + 1) * tile
+
+
+def attend_tile(chunk, tile, step, length, slope, q_ref, keys, values, context_ref, log_ref):
+    span = keys[0].shape[0]
     query = q_ref[...]
+    ends = [reach(chunk, m, tile, step, span) for m in range(chunk + 1)]
     scores = [
-        block_scores(query, keys[m][...], chunk * span + g * tile, m * span, length_ref[0], slope_ref[h])
+        block_scores(query, keys[m][: ends[m]], chunk * span + step * tile, m * span, length, slope)
         for m in range(chunk + 1)
     ]
     highest = functools.reduce(jnp.maximum, [jnp.max(s, axis=1, keepdims=True) for s in scores])
     raised = [jnp.exp(s - highest) for s in scores]
     total = sum(jnp.sum(r, axis=1, keepdims=True) for r in raised)
     context = sum(
-        jnp.dot((r / total).astype(BF16), v[...], preferred_element_type=F32)
-        for r, v in zip(raised, values)
+        jnp.dot((r / total).astype(BF16), v[:end], preferred_element_type=F32)
+        for r, v, end in zip(raised, values, ends)
     )
     context_ref[...] = context.astype(BF16)
     log_ref[...] = jnp.broadcast_to(highest + jnp.log(total), log_ref.shape)
@@ -367,7 +512,7 @@
             jax.ShapeDtypeStruct((span, heads * HEAD_DIM), F32),
         ],
         compiler_params=pltpu.CompilerParams(vmem_limit_bytes=32 * MIB),
-        cost_estimate=pl.CostEstimate(
+        cost_estimate=cost(
             flops=4 * span * span * (chunk + 1) * heads * HEAD_DIM,
             bytes_accessed=8 * span * columns * (chunk + 1),
             transcendentals=span * span * (chunk + 1) * heads,
@@ -399,33 +544,22 @@
                 key_sums[m][...] = given[m][:, :d]
                 value_sums[m][...] = given[m][:, d:]
 
-    query, grad = q_ref[...], grad_ref[...]
-    log_total = log_ref[:, :1]
-    by_rows = (((0,), (0,)), ((), ()))
-    chances, chance_grads = [], []
-    for m in range(n):
-        scores = block_scores(
-            query, keys[m][...], chunk * span + g * tile, m * span, length_ref[0], slope_ref[h]
-        )
-        chances.append(jnp.exp(scores - log_total))
-        chance_grads.append(
-            lax.dot_general(grad, values[m][...], (((1,), (1,)), ((), ())), preferred_element_type=F32)
-        )
-    row_dot = sum(
-        jnp.sum(p * c, axis=1, keepdims=True) for p, c in zip(chances, chance_grads)
-    )
-    query_grad = jnp.zeros((tile, d), F32)
-    for m in range(n):
-        value_sums[m][...] += lax.dot_general(
-            chances[m].astype(BF16), grad, by_rows, preferred_element_type=F32
-        )
-        score_grad = (chances[m] * (chance_grads[m] - row_dot)).astype(BF16)
-        query_grad += jnp.dot(score_grad, keys[m][...], preferred_element_type=F32)
-        key_sums[m][...] += lax.dot_general(
-            score_grad, query, by_rows, preferred_element_type=F32
-        )
+    for step in range(span // tile):
+
+        @pl.when(g == step)
+        def _():
+            query_grad = attend_back_tile(
+                chunk,
+                tile,
+                step,
+                length_ref[0],
+                slope_ref[h],
+                (q_ref, grad_ref, log_ref),
+                (keys, values, key_sums, value_sums),
+            )
+            out_ref[step * tile : (step + 1) * tile, :d] = query_grad.astype(BF16)
+
     factor = 1.0 / math.sqrt(d)
-    out_ref[pl.ds(pl.multiple_of(g * tile, tile), tile), :d] = (query_grad * factor).astype(BF16)
 
     @pl.when(g == pl.num_programs(1) - 1)
     def _():
@@ -434,6 +568,35 @@
         for m in range(chunk):
             sums[m][:, :d] = key_sums[m][...]
             sums[m][:, d:] = value_sums[m][...]
+
+
+def attend_back_tile(chunk, tile, step, length, slope, own, others):
+    q_ref, grad_ref, log_ref = own
+    keys, values, key_sums, value_sums = others
+    span, d = keys[0].shape
+    query, grad = q_ref[...], grad_ref[...]
+    log_total = log_ref[:, :1]
+    by_rows = (((0,), (0,)), ((), ()))
+    ends = [reach(chunk, m, tile, step, span) for m in range(chunk + 1)]
+    chances, chance_grads = [], []
+    for m, end in enumerate(ends):
+        scores = block_scores(
+            query, keys[m][:end], chunk * span + step * tile, m * span, length, slope
+        )
+        chances.append(jnp.exp(scores - log_total))
+        chance_grads.append(
+            lax.dot_general(grad, values[m][:end], (((1,), (1,)), ((), ())), preferred_element_type=F32)
+        )
+    row_dot = added([jnp.sum(p * c, axis=1, keepdims=True) for p, c in zip(chances, chance_grads)])
+    query_grad = jnp.zeros((tile, d), F32)
+    for m, end in enumerate(ends):
+        value_sums[m][:end] += lax.dot_general(
+            chances[m].astype(BF16), grad, by_rows, preferred_element_type=F32
+        )
+        score_grad = (chances[m] * (chance_grads[m] - row_dot)).astype(BF16)
+        query_grad += jnp.dot(score_grad, keys[m][:end], preferred_element_type=F32)
+        key_sums[m][:end] += lax.dot_general(score_grad, query, by_rows, preferred_element_type=F32)
+    return query_grad * (1.0 / math.sqrt(d))
 
 
 def attend_back(chunk, joined, given, context_grad, log_total, length, slopes):
@@ -459,8 +622,8 @@
         ),
         out_shape=[jax.ShapeDtypeStruct((span, columns), BF16)]
         + [jax.ShapeDtypeStruct((span, heads * 2 * HEAD_DIM), F32)] * chunk,
-        compiler_params=pltpu.CompilerParams(vmem_limit_bytes=40 * MIB),
-        cost_estimate=pl.CostEstimate(
+        compiler_params=pltpu.CompilerParams(vmem_limit_bytes=32 * MIB),
+        cost_estimate=cost(
             flops=10 * span * span * n * heads * HEAD_DIM,
             bytes_accessed=12 * span * columns * n,
             transcendentals=span * span * n * heads,
@@ -493,14 +656,12 @@
     return packed((value - mean).astype(BF16), rows_of(mean), value.shape[1])
 
 
-def weight_products(gain, shift, weight):
-    def parts(v):
-        high = lax.reduce_precision(v, 8, 7)
-        return [high.astype(BF16), (v - high).astype(BF16)]
-
-    rows = jnp.stack(parts(gain) + parts(shift))
-    out = jnp.dot(rows, weight, preferred_element_type=F32)
-    return out[0] + out[1], out[2] + out[3]
+def rows_for_products(gain, shift):
+    rows = []
+    for value in (gain, shift):
+        high = lax.reduce_precision(value, 8, 7)
+        rows += [high.astype(BF16), (value - high).astype(BF16)]
+    return jnp.pad(jnp.stack(rows), ((0, PAD - len(rows)), (0, 0)))
 
 
 def sums_rows(first, second, width):
@@ -535,10 +696,8 @@
     return lax.all_gather(block, ("rh", "c", "x"), axis=0, tiled=True)
 
 
-def own_columns(blocks, rows):
-    n = blocks.shape[1]
-    blocks = blocks.reshape(-1, 2, rows, n)
-    return lax.dynamic_index_in_dim(blocks, lax.axis_index("c"), 1, keepdims=False).reshape(-1, n)
+def by_blocks(gathered, rows):
+    return gathered.reshape(-1, 2, rows, gathered.shape[1])
 
 
 def scatter_weight(term):
@@ -577,10 +736,10 @@
     def cut(value):
         return [value[k * span : (k + 1) * span] for k in chunks]
 
+    masked = cotangent * (jnp.arange(tokens) < lengths[0]).reshape(tokens, 1)
     lengths = swap_roles(lengths)
     head_index = block_index() * heads_local + jnp.arange(heads_local)
     slopes = jnp.exp2(-8.0 * (head_index + 1).astype(F32) / HEADS)
-    valid = (jnp.arange(tokens) < lengths[0]).reshape(tokens, 1)
 
     smalls = (
         first_gain,
@@ -615,25 +774,35 @@
             blocks, _ = lax.optimization_barrier((blocks, shards))
         packs.append([gather_weight(b) for b in blocks])
         if layer == 0:
-            gradient = [swap_roles(after(v, packs[0][0])) * m for v, m in zip(cut(cotangent), cut(valid))]
+            gradient = [swap_roles(after(v, packs[0][0])) for v in cut(masked)]
     rows = joined_weight.shape[1]
     weights = []
 
+    low_shards = [swap_roles(after(v.astype(BF16), *shards)) for v in cut(masked)]
     slots = [gather_slots(s) for s in shards]
+    first_slots = [gather_slots(after(v, *[s[3] for s in slots])) for v in low_shards]
     held = jnp.stack([s[span + PAD :][: 3 * count] for s in slots[0]]).astype(F32)
     table = (held[:, :count] + held[:, count : 2 * count] + held[:, 2 * count :]).reshape(
         len(slots[0]), layers, table_rows, f
     )
     own_up = table[0, :, len(smalls) :].reshape(layers, -1)
+    natural = table[slot_blocks()]
+    product_rows = [
+        [
+            rows_for_products(*(natural[:, layer, n].reshape(width) for n in pair))
+            for pair in ((0, 1), (5, 6))
+        ]
+        for layer in range(layers)
+    ]
 
     no_rows = jnp.zeros((PAD, f), BF16)
     saved = []
-    first_slots = [None] * CHUNKS
     turn = ()
     for layer in range(layers):
         last = layer + 1 == layers
-        first_w = own_columns(packs[layer][0], rows)
-        joined_w, output_w = first_w[:, : 3 * f], first_w[:, 3 * f :]
+        first_w = by_blocks(packs[layer][0], rows)
+        joined_w, output_w = Columns(first_w, 3 * f), Columns(first_w, f, 3)
+        products = []
         gains = [table[:, layer, n] for n in range(len(smalls))]
         own = table[0, layer]
         zero = jnp.zeros((heads_local, HEAD_DIM), F32)
@@ -642,46 +811,42 @@
         ).reshape(3 * f)
         joined, kept = [], []
         for k in chunks:
-            if layer > 0:
-                slots[k] = gather_slots(shard_of(residual[k]))
             slots[k], _ = lax.optimization_barrier((slots[k], turn))
-            normed_one, centred_one, inverse_one = assemble_norm(
-                slots[k], residual[k], gains[0], gains[1]
+            normed_one, centred_one, inverse_one, product_one, hidden = norm_matmul(
+                slots[k], residual[k], gains[0], gains[1], joined_w, joined_bias, product_rows[layer][0], False
             )
-            joined.append(
-                (jnp.dot(normed_one, joined_w, preferred_element_type=F32) + joined_bias).astype(BF16)
-            )
-            if last:
-                first_slots[k] = gather_slots(after(gradient[k].astype(BF16), normed_one))
+            joined.append(hidden)
+            if layer == 0:
+                joined[k] = after(joined[k], *first_slots[k])
             context, log_total = attend(k, joined, lengths, slopes)
-            if last:
-                context = after(context, *first_slots[k])
             pair = column_sum(context, output_w, no_rows)
             turn = pair
             middle = residual[k] + ring_sum(pair)[:span] + own[4]
+            slots[k] = gather_slots(shard_of(middle))
             kept.append([normed_one, centred_one, inverse_one, context, log_total, middle])
-        up_w = own_columns(after(packs[layer][1], turn), rows)
+        up_w = Columns(by_blocks(after(packs[layer][1], turn), rows), up_weight.shape[2])
         for k in chunks:
             middle = kept[k].pop()
-            slots[k] = gather_slots(shard_of(middle))
             slots[k], _ = lax.optimization_barrier((slots[k], turn))
-            normed_two, centred_two, inverse_two = assemble_norm(slots[k], middle, gains[5], gains[6])
-            upper = jnp.dot(normed_two, up_w, preferred_element_type=F32) + own_up[layer]
-            activated = gelu_tanh(upper).astype(BF16)
+            normed_two, centred_two, inverse_two, product_two, upper, activated = norm_matmul(
+                slots[k], middle, gains[5], gains[6], up_w, own_up[layer], product_rows[layer][1], True
+            )
             if k == 0:
-                down_w = own_columns(after(packs[layer][2], upper), rows)
+                down_w = Columns(by_blocks(after(packs[layer][2], upper), rows), down_weight.shape[1])
             turn = (activated,)
             if not last:
                 pair = column_sum(activated, down_w, no_rows)
                 turn = pair
                 residual[k] = middle + ring_sum(pair)[:span] + own[7]
+                slots[k] = gather_slots(shard_of(residual[k]))
             kept[k] += [normed_two, centred_two, inverse_two, upper, activated, middle]
         weights.append((joined_w, output_w, up_w, down_w))
-        saved.append((joined, joined_bias, kept))
+        saved.append((joined, joined_bias, kept, product_one, product_two))
 
     weight_terms = [None] * layers
     small_terms = [None] * layers
-    result = [None] * CHUNKS
+    result, last_pairs, back_middle = ([None] * CHUNKS for _ in range(3))
+    last_down_w = weights[-1][3]
     middle_grad = [None] * CHUNKS
     passed_one = [None] * CHUNKS
 
@@ -691,36 +856,37 @@
         ).astype(BF16)
 
     for layer in reversed(range(layers)):
-        joined, joined_bias, kept = saved[layer]
+        joined, joined_bias, kept, product_one, product_two = saved[layer]
         joined_w, output_w, up_w, down_w = weights[layer]
         own = table[0, layer]
-        order = slot_blocks()
-        gains = [table[order, layer, n].reshape(width) for n in range(len(smalls))]
-        up_gain, up_shift = weight_products(gains[5], gains[6], up_w)
-        joined_gain, joined_shift = weight_products(gains[0], gains[1], joined_w)
+        up_gain, up_shift = product_two[0] + product_two[1], product_two[2] + product_two[3]
+        joined_gain, joined_shift = product_one[0] + product_one[1], product_one[2] + product_one[3]
         given = None
-        smalls_of, down_ends, up_ends, joined_ends, output_ends = ([None] * CHUNKS for _ in range(5))
+        middle_slots, smalls_of, down_ends, up_ends, joined_ends, output_ends = ([None] * CHUNKS for _ in range(6))
         for k in reversed(chunks):
             normed_two, centred_two, inverse_two, upper, activated, middle = kept[k][5:]
             down_bias_term = jnp.sum(gradient[k], axis=0)
-            slots = first_slots[k] if layer + 1 == layers else gather_slots(gradient[k].astype(BF16))
+            slots = first_slots[k]
             slots, _ = lax.optimization_barrier((slots, turn))
-            low_gradient = assemble(slots)
-            hidden_grad = jnp.dot(low_gradient, down_w, preferred_element_type=F32)
-            upper_grad = jax.vjp(gelu_tanh, upper)[1](hidden_grad)[0].astype(BF16)
-            wide_grad = upper_grad.astype(F32)
-            first_sum = jnp.sum(wide_grad * up_gain, axis=1)
-            second_sum = jnp.sum(wide_grad * (upper - (own_up[layer] + up_shift)), axis=1)
-            up_bias_term = jnp.sum(wide_grad, axis=0)
-            pair = column_sum(upper_grad, up_w, sums_rows(first_sum, second_sum, f))
+            low_gradient, upper_grad, extra, up_bias_term = hidden_back(
+                slots, down_w, upper, up_gain, own_up[layer] + up_shift
+            )
+            pair = column_sum(upper_grad, up_w, extra)
             turn = pair
             down_ends[k] = (low_gradient, after(activated, pair))
+            if layer == 0:
+                last_active = after(saved[-1][2][k][9], pair)
+                last_pairs[k] = column_sum(last_active, last_down_w, no_rows)
             normed_two_grad = ring_sum(pair)
+            if layer == 0:
+                normed_two_grad = after(normed_two_grad, last_pairs[k])
             if k == 0:
                 down_term = term(down_ends)
                 normed_two_grad = after(normed_two_grad, down_term)
                 if layer + 1 < layers:
-                    normed_two_grad = after(normed_two_grad, joint_sum)
+                    normed_two_grad = after(normed_two_grad, joint_sum, up_pair[1])
+                    joint_pair = swapped(joint_sum)
+                    weight_terms[layer + 1] = [joint_pair, up_pair, down_pair]
                 down_sum = scatter_weight(down_term)
             passed_two, gain_two_term, shift_two_term = norm_backward(
                 normed_two_grad, centred_two, inverse_two, own[5], width
@@ -729,25 +895,24 @@
             output_bias_term = jnp.sum(middle_grad[k], axis=0)
             smalls_of[k] = [output_bias_term, gain_two_term, shift_two_term, down_bias_term, up_bias_term]
             up_ends[k] = (normed_two, after(upper_grad, middle_grad[k]))
+            middle_slots[k] = gather_slots(middle_grad[k].astype(BF16))
         for k in reversed(chunks):
             normed_one, centred_one, inverse_one, context, log_total = kept[k][:5]
-            activated, middle = kept[k][9:]
-            slots = gather_slots(middle_grad[k].astype(BF16))
+            slots = middle_slots[k]
             slots, _ = lax.optimization_barrier((slots, turn))
             if k == 0:
                 up_term = term(up_ends)
                 slots, _ = lax.optimization_barrier((slots, (up_term, down_sum)))
                 up_sum = scatter_weight(up_term)
-            low_middle = assemble(slots)
-            context_grad = jnp.dot(low_middle, output_w, preferred_element_type=F32).astype(BF16)
-            if layer + 1 == layers:
-                last_pair = column_sum(after(activated, context_grad), down_w, no_rows)
-                result[k] = middle + ring_sum(last_pair)[:span] + own[7]
+                down_pair = swapped(down_sum)
+            low_middle, context_grad = gather_matmul(slots, output_w)
+            if layer == 0:
+                back_middle[k] = swap_roles(after(middle_grad[k], low_middle))
+                last_total = ring_sum(after(last_pairs[k], slots))
+                result[k] = saved[-1][2][k][10] + last_total[:span] + table[0, layers - 1, 7]
             joined_grad, given = attend_back(
                 k, joined, given, context_grad, log_total, lengths, slopes
             )
-            if layer + 1 == layers:
-                joined_grad, result[k] = lax.optimization_barrier((joined_grad, result[k]))
             wide_grad = joined_grad.astype(F32)
             first_sum = jnp.sum(wide_grad * joined_gain, axis=1)
             second_sum = jnp.sum(
@@ -757,15 +922,22 @@
             output_ends[k] = (low_middle, context)
             if k == 0 and layer == 0:
                 first_term = jnp.concatenate([term(joined_ends), term(output_ends)], axis=1)
-                first_sum = after(first_sum, first_term)
+                first_sum = after(first_sum, first_term, result[k], back_middle, weight_terms[-1][0][1])
+                back_result = [swap_roles(r) for r in result]
             pair = column_sum(joined_grad, joined_w, sums_rows(first_sum, second_sum, f))
             turn = pair
             normed_one_grad = ring_sum(pair)
+            if k == 0:
+                up_pair = swapped(up_sum)
+            if k == 0 and layer == 0:
+                normed_one_grad = after(
+                    normed_one_grad, down_pair[1], back_result
+                )
             if k == 0 and layer > 0:
                 joined_ends[0] = (normed_one, after(joined_grad, pair))
                 output_ends[0] = (low_middle, after(context, pair))
                 first_term = jnp.concatenate([term(joined_ends), term(output_ends)], axis=1)
-                normed_one_grad = after(normed_one_grad, first_term, up_sum)
+                normed_one_grad = after(normed_one_grad, first_term, up_sum, down_pair[1])
             if k == 0:
                 joint_sum = scatter_weight(first_term)
             joined_bias_term = jnp.sum(joined_grad.astype(F32), axis=0).reshape(heads_local, 3, HEAD_DIM)
@@ -773,6 +945,8 @@
                 normed_one_grad, centred_one, inverse_one, own[0], width
             )
             gradient[k] = middle_grad[k] + passed_one[k]
+            if layer > 0:
+                first_slots[k] = gather_slots(gradient[k].astype(BF16))
             smalls_of[k] = jnp.concatenate(
                 [
                     t.reshape(-1, f)
@@ -787,11 +961,7 @@
                 axis=0,
             )
         small_terms[layer] = added(smalls_of)
-        weight_terms[layer] = [swapped(v) for v in (joint_sum, up_sum, down_sum)]
-    input_grad = jnp.concatenate(
-        [swap_roles(m) + swap_roles(p.astype(BF16)).astype(F32) for m, p in zip(middle_grad, passed_one)],
-        axis=0,
-    )
+    back_passed = [swap_roles(p.astype(BF16)) for p in passed_one]
     small = jnp.stack(small_terms)
     for axis in ("rh", "x"):
         size = lax.axis_size(axis)
@@ -801,12 +971,17 @@
     same = lax.axis_index("c") == lax.axis_index("x")
     small = jnp.where(same, small, partner(small))
 
+    input_grad = jnp.concatenate(
+        [m + after(p, small).astype(F32) for m, p in zip(back_middle, back_passed)],
+        axis=0,
+    )
+    weight_terms[0] = [swapped(joint_sum), up_pair, down_pair]
     joined_out, output_out = unpack([t[0] for t in weight_terms], (False, True), (3 * f, f))
     (up_out,) = unpack([t[1] for t in weight_terms], (False,), (up_weight.shape[2],))
     (down_out,) = unpack([t[2] for t in weight_terms], (True,), (down_weight.shape[1],))
 
     return (
-        jnp.concatenate([swap_roles(r) for r in result], axis=0),
+        jnp.concatenate(back_result, axis=0),
         input_grad,
         small[:, 0],
         small[:, 1],

time: 1160 us -> 1090 us (0.940)
  waiting for transfers between devices: 595 us -> 502 us
  matrix products: 84.2 us -> 38 us
  Pallas kernels: 156 us -> 192 us
  starting transfers between devices: 113 us -> 145 us
    ppermute x48, waiting for transfers between devices: 505 us -> 418 us  [ring(): return lax.ppermute(value, 't', [(i, i ^ k) for i in range(ring_size())])]
    pallas_call x24, Pallas kernels: 90.3 us -> 146 us  [the longest x4 62.7 us: norm_matmul(): pl.pallas_call(functools.partial(norm_kernel, slots, width, gelu), grid_s...]
    dot_general x12 -> x0, matrix products: 49 us -> none  [the longest x2 16.7 us: on_device(): hidden_grad = jnp.dot(low_gradient, down_w, preferred_element_type=F32)]
    ppermute x48, starting transfers between devices: 37.9 us -> 70.4 us  [ring(): return lax.ppermute(value, 't', [(i, i ^ k) for i in range(ring_size())])]
    ppermute x2, waiting for transfers between devices: 32 us -> 1.22 us  [on_device(): lax.ppermute(small, axis, [(r, r ^ k) for r in range(size)])]
    ppermute x6, waiting for transfers between devices: 13.6 us -> 43.4 us  [swapped(): return (value, lax.ppermute(value, ('c', 'x'), [(1, 2), (2, 1)]))]
    unnamed x294 -> x350, local copies, waits for them, and re-layouts: 59.3 us -> 89 us
    dynamic_slice x6 -> x0, local copies, waits for them, and re-layouts: 18.9 us -> none  [own_columns(): lax.dynamic_index_in_dim(blocks, lax.axis_index('c'), 1, keepdims=False)]
  transfers between devices with their start and end apart: 116 -> 141, of which waited for: 58 -> 57; matrix products, arithmetic and copies ran while one was open for 15% -> 11% of each run, Pallas kernels for 12% -> 16%
where the time goes in v3:
time: 1090 us; the launch traced here: 1080 us
  waiting for transfers between devices  502 us (46%)
  Pallas kernels  192 us (18%)
  starting transfers between devices  145 us (13%)
  local copies, waits for them, and re-layouts  113 us (10%)
  other arithmetic  71.8 us (7%)
  matrix products  38 us (3%)
  between operations  18.1 us (2%)
    ppermute x48, waiting for transfers between devices, ring(): return lax.ppermute(value, 't', [(i, i ^ k) for i in range(ring_size())])  418 us
    unnamed x350, local copies, waits for them, and re-layouts  89 us
    ppermute x48, starting transfers between devices, ring(): return lax.ppermute(value, 't', [(i, i ^ k) for i in range(ring_size())])  70.4 us
    pallas_call x4, Pallas kernels, norm_matmul(): pl.pallas_call(functools.partial(norm_kernel, slots, width, gelu), grid_s...  62.7 us
    ppermute x6, waiting for transfers between devices, swapped(): return (value, lax.ppermute(value, ('c', 'x'), [(1, 2), (2, 1)]))  43.4 us
    pallas_call x16, Pallas kernels, slot_matmul(): pl.pallas_call(functools.partial(slot_matmul_kernel, n, tile), grid_spec=...  41.1 us
    dot_general x8, matrix products, term(): jnp.einsum('td,tn->dn', a, b, preferred_element_type=F32)  38 us
    ppermute x8, waiting for transfers between devices, swap_roles(): lax.ppermute(value, ('c', 'x'), [(1, 2), (2, 1)])  31.9 us
  transfers between devices with their start and end apart: 141, of which 57 were waited for; matrix products, arithmetic and copies ran while one was open for 11% of the time, Pallas kernels for 16%

profile of v3, /device:TPU:1, one launch (start us, length us, event | category | flops | bytes accessed | tf_op | source)
XLA Modules:
  0.0 1080.6 jit_solution(14474552430302340671)
XLA Ops:
  16.2 4.5 collective-permute-start
  55.3 5.5 collective-permute-done.10
  60.8 10.4 collective-permute-done.6.refs_4_
  73.7 11.4 %collective-permute-done.1 = f32[1024,256]{1,0:T(8,128)S(1)} collective-permute-done((f32[1024,256]{1,0:T(8,128)S(1)}, f32[1024,256]{1,0:T(8,128)S(1)}, u32[]{:S(2)}, u32[]{:S(2)}) %collective-permute-start.1) | collective-permute-done | bytes 1048608 | tf_op jit(solution)/shard_map/ppermute | solution.py:57
  92.2 12.9 %collective-permute-done.14.refs_4_ = bf16[1024,256]{1,0:T(8,128)(2,1)} collective-permute-done((bf16[1024,256]{1,0:T(8,128)(2,1)S(1)}, bf16[1024,256]{1,0:T(8,128)(2,1)}, u32[]{:S(2)}, u32[]{:S(2)}) %collective-permute-start.14) | collective-permute-done | bytes 524320 | tf_op jit(solution)/shard_map/ppermute | solution.py:48
  105.2 6.4 collective-permute-done.12.refs_2_
  122.3 14.2 %norm_matmul.4 = (bf16[1024,2048]{1,0:T(8,128)(2,1)}, f32[1024,256]{1,0:T(8,128)}, f32[1024,128]{1,0:T(8,128)}, f32[16,768]{1,0:T(8,128)}, bf16[1024,768]{1,0:T(8,128)(2,1)}) custom-call(s32[8]{0:T(128)} %copy-done.141, s32[1]{0:T(128)} %bitcast.9.core_ref, bf16[1120,256]{1,0:T(8,128)(2,1)} %broadcast_select_fusion.refs_0_, bf16[1120,256]{1,0:T(8,128)(2,1)} %copy-done.93, ...), custom_call_target="tpu_custom_call" | custom-call | flops 805306368 | bytes 4194304 | tf_op jit(solution)/shard_map/norm_matmul/pallas_call | solution.py:174
  138.8 7.1 attend.2
  161.7 11.0 %collective-permute-done.23 = bf16[1040,256]{1,0:T(8,128)(2,1)S(1)} collective-permute-done((bf16[1040,256]{1,0:T(8,128)(2,1)S(1)}, bf16[1040,256]{1,0:T(8,128)(2,1)S(1)}, u32[]{:S(2)}, u32[]{:S(2)}) %collective-permute-start.23) | collective-permute-done | bytes 532512 | tf_op jit(solution)/shard_map/ppermute | solution.py:48
  176.1 17.9 %collective-permute-done.20 = bf16[1040,256]{1,0:T(8,128)(2,1)S(1)} collective-permute-done((bf16[1040,256]{1,0:T(8,128)(2,1)S(1)}, bf16[1040,256]{1,0:T(8,128)(2,1)S(1)}, u32[]{:S(2)}, u32[]{:S(2)}) %collective-permute-start.20) | collective-permute-done | bytes 532512 | tf_op jit(solution)/shard_map/ppermute | solution.py:48
  202.2 18.3 %collective-permute-done.28.refs_4_ = bf16[1040,256]{1,0:T(8,128)(2,1)S(1)} collective-permute-done((bf16[1040,256]{1,0:T(8,128)(2,1)S(1)}, bf16[1040,256]{1,0:T(8,128)(2,1)S(1)}, u32[]{:S(2)}, u32[]{:S(2)}) %collective-permute-start.28) | collective-permute-done | bytes 532512 | tf_op jit(solution)/shard_map/ppermute | solution.py:48
  225.0 9.7 collective-permute-done.30.refs_6_
  241.7 17.4 %norm_matmul.5 = (bf16[1024,2048]{1,0:T(8,128)(2,1)}, f32[1024,256]{1,0:T(8,128)}, f32[1024,128]{1,0:T(8,128)}, f32[16,1024]{1,0:T(8,128)}, f32[1024,1024]{1,0:T(8,128)}, /*index=5*/bf16[1024,1024]{1,0:T(8,128)(2,1)}) custom-call(s32[8]{0:T(128)} %copy-done.141, s32[1]{0:T(128)} %bitcast.9.core_ref, bf16[1040,256]{1,0:T(8,128)(2,1)} %copy-done.80, ...), custom_call_target="tpu_custom_call" | custom-call | flops 1073741824 | bytes 4194304 | tf_op jit(solution)/shard_map/norm_matmul/pallas_call | solution.py:174
  282.4 10.8 %collective-permute-done.37 = bf16[1040,256]{1,0:T(8,128)(2,1)S(1)} collective-permute-done((bf16[1040,256]{1,0:T(8,128)(2,1)S(1)}, bf16[1040,256]{1,0:T(8,128)(2,1)S(1)}, u32[]{:S(2)}, u32[]{:S(2)}) %collective-permute-start.37) | collective-permute-done | bytes 532512 | tf_op jit(solution)/shard_map/ppermute | solution.py:48
  297.3 17.8 %collective-permute-done.34 = bf16[1040,256]{1,0:T(8,128)(2,1)S(1)} collective-permute-done((bf16[1040,256]{1,0:T(8,128)(2,1)S(1)}, bf16[1040,256]{1,0:T(8,128)(2,1)S(1)}, u32[]{:S(2)}, u32[]{:S(2)}) %collective-permute-start.34) | collective-permute-done | bytes 532512 | tf_op jit(solution)/shard_map/ppermute | solution.py:48
  323.6 11.3 %collective-permute-done.42.refs_4_ = bf16[1040,256]{1,0:T(8,128)(2,1)S(1)} collective-permute-done((bf16[1040,256]{1,0:T(8,128)(2,1)S(1)}, bf16[1040,256]{1,0:T(8,128)(2,1)S(1)}, u32[]{:S(2)}, u32[]{:S(2)}) %collective-permute-start.42) | collective-permute-done | bytes 532512 | tf_op jit(solution)/shard_map/ppermute | solution.py:48
  334.9 6.6 collective-permute-start.44
  346.5 6.2 collective-permute-done.44.refs_6_
  359.4 14.1 %norm_matmul.6 = (bf16[1024,2048]{1,0:T(8,128)(2,1)}, f32[1024,256]{1,0:T(8,128)}, f32[1024,128]{1,0:T(8,128)}, f32[16,768]{1,0:T(8,128)}, bf16[1024,768]{1,0:T(8,128)(2,1)}) custom-call(s32[8]{0:T(128)} %copy-done.141, s32[1]{0:T(128)} %bitcast.9.core_ref, bf16[1040,256]{1,0:T(8,128)(2,1)} %copy-done.79, bf16[1040,256]{1,0:T(8,128)(2,1)} %copy-done.101, ...), custom_call_target="tpu_custom_call" | custom-call | flops 805306368 | bytes 4194304 | tf_op jit(solution)/shard_map/norm_matmul/pallas_call | solution.py:174
  374.9 7.1 attend.3
  392.6 11.6 %collective-permute-done.51 = bf16[1040,256]{1,0:T(8,128)(2,1)S(1)} collective-permute-done((bf16[1040,256]{1,0:T(8,128)(2,1)S(1)}, bf16[1040,256]{1,0:T(8,128)(2,1)S(1)}, u32[]{:S(2)}, u32[]{:S(2)}) %collective-permute-start.51) | collective-permute-done | bytes 532512 | tf_op jit(solution)/shard_map/ppermute | solution.py:48
  404.4 6.9 collective-permute-start.52
  411.5 14.0 %collective-permute-done.48 = bf16[1040,256]{1,0:T(8,128)(2,1)S(1)} collective-permute-done((bf16[1040,256]{1,0:T(8,128)(2,1)S(1)}, bf16[1040,256]{1,0:T(8,128)(2,1)S(1)}, u32[]{:S(2)}, u32[]{:S(2)}) %collective-permute-start.48) | collective-permute-done | bytes 532512 | tf_op jit(solution)/shard_map/ppermute | solution.py:48
  425.5 8.8 collective-permute-done.52
  438.4 23.5 %collective-permute-done.56.refs_4_ = bf16[1040,256]{1,0:T(8,128)(2,1)S(1)} collective-permute-done((bf16[1040,256]{1,0:T(8,128)(2,1)S(1)}, bf16[1040,256]{1,0:T(8,128)(2,1)S(1)}, u32[]{:S(2)}, u32[]{:S(2)}) %collective-permute-start.56) | collective-permute-done | bytes 532512 | tf_op jit(solution)/shard_map/ppermute | solution.py:48
  463.0 11.7 %collective-permute-done.58.refs_6_ = bf16[1040,256]{1,0:T(8,128)(2,1)S(1)} collective-permute-done((bf16[1040,256]{1,0:T(8,128)(2,1)S(1)}, bf16[1040,256]{1,0:T(8,128)(2,1)S(1)}, u32[]{:S(2)}, u32[]{:S(2)}) %collective-permute-start.58) | collective-permute-done | bytes 532512 | tf_op jit(solution)/shard_map/ppermute | solution.py:48
  481.4 17.0 %norm_matmul.7 = (bf16[1024,2048]{1,0:T(8,128)(2,1)}, f32[1024,256]{1,0:T(8,128)}, f32[1024,128]{1,0:T(8,128)}, f32[16,1024]{1,0:T(8,128)}, f32[1024,1024]{1,0:T(8,128)}, /*index=5*/bf16[1024,1024]{1,0:T(8,128)(2,1)}) custom-call(s32[8]{0:T(128)} %copy-done.141, s32[1]{0:T(128)} %bitcast.9.core_ref, bf16[1040,256]{1,0:T(8,128)(2,1)} %copy-done.81, ...), custom_call_target="tpu_custom_call" | custom-call | flops 1073741824 | bytes 4194304 | tf_op jit(solution)/shard_map/norm_matmul/pallas_call | solution.py:174
  500.6 13.8 %hidden_back.2 = (bf16[1024,2048]{1,0:T(8,128)(2,1)}, bf16[1024,1024]{1,0:T(8,128)(2,1)}, f32[8,8,128]{2,1,0:T(8,128)}, f32[8,1024]{1,0:T(8,128)}) custom-call(s32[8]{0:T(128)} %copy-done.141, s32[1]{0:T(128)} %bitcast.9.core_ref, bf16[1024,256]{1,0:T(8,128)(2,1)} %copy-done.85, bf16[1024,256]{1,0:T(8,128)(2,1)} %collective-permute-done.11.refs_1_, ...), custom_call_target="tpu_custom_call" | custom-call | flops 1073741824 | bytes 4194304 | tf_op jit(solution)/shard_map/hidden_back/pallas_call | solution.py:258
  529.6 11.2 %collective-permute-done.66 = bf16[1040,256]{1,0:T(8,128)(2,1)S(1)} collective-permute-done((bf16[1040,256]{1,0:T(8,128)(2,1)S(1)}, bf16[1040,256]{1,0:T(8,128)(2,1)S(1)}, u32[]{:S(2)}, u32[]{:S(2)}) %collective-permute-start.66) | collective-permute-done | bytes 532512 | tf_op jit(solution)/shard_map/ppermute | solution.py:48
  542.6 6.3 convolution_convert_fusion.3
  553.5 18.9 %collective-permute-done.63 = bf16[1040,256]{1,0:T(8,128)(2,1)S(1)} collective-permute-done((bf16[1040,256]{1,0:T(8,128)(2,1)}, bf16[1040,256]{1,0:T(8,128)(2,1)S(1)}, u32[]{:S(2)}, u32[]{:S(2)}) %collective-permute-start.63) | collective-permute-done | bytes 532512 | tf_op jit(solution)/shard_map/ppermute | solution.py:48
  573.8 12.7 %collective-permute-done.60 = f32[1024,256]{1,0:T(8,128)S(1)} collective-permute-done((f32[1024,256]{1,0:T(8,128)}, f32[1024,256]{1,0:T(8,128)S(1)}, u32[]{:S(2)}, u32[]{:S(2)}) %collective-permute-start.60) | collective-permute-done | bytes 1048608 | tf_op jit(solution)/shard_map/ppermute | solution.py:57
  588.7 6.2 convolution_convert_fusion.2
  597.5 15.5 %collective-permute-done.71.refs_4_ = bf16[1024,256]{1,0:T(8,128)(2,1)S(1)} collective-permute-done((bf16[1024,256]{1,0:T(8,128)(2,1)S(1)}, bf16[1024,256]{1,0:T(8,128)(2,1)S(1)}, u32[]{:S(2)}, u32[]{:S(2)}) %collective-permute-start.71) | collective-permute-done | bytes 524320 | tf_op jit(solution)/shard_map/ppermute | solution.py:48
  614.1 11.1 %collective-permute-done.73.refs_6_ = bf16[1024,256]{1,0:T(8,128)(2,1)S(1)} collective-permute-done((bf16[1024,256]{1,0:T(8,128)(2,1)S(1)}, bf16[1024,256]{1,0:T(8,128)(2,1)S(1)}, u32[]{:S(2)}, u32[]{:S(2)}) %collective-permute-start.73) | collective-permute-done | bytes 524320 | tf_op jit(solution)/shard_map/ppermute | solution.py:48
  628.0 7.3 gather_matmul.2
  637.6 8.8 attend_back.2.x_ref
  659.3 11.1 %collective-permute-done.80 = bf16[1040,256]{1,0:T(8,128)(2,1)S(1)} collective-permute-done((bf16[1040,256]{1,0:T(8,128)(2,1)S(1)}, bf16[1040,256]{1,0:T(8,128)(2,1)S(1)}, u32[]{:S(2)}, u32[]{:S(2)}) %collective-permute-start.80) | collective-permute-done | bytes 532512 | tf_op jit(solution)/shard_map/ppermute | solution.py:48
  686.7 17.3 %collective-permute-done.77 = bf16[1040,256]{1,0:T(8,128)(2,1)S(1)} collective-permute-done((bf16[1040,256]{1,0:T(8,128)(2,1)}, bf16[1040,256]{1,0:T(8,128)(2,1)S(1)}, u32[]{:S(2)}, u32[]{:S(2)}) %collective-permute-start.77) | collective-permute-done | bytes 532512 | tf_op jit(solution)/shard_map/ppermute | solution.py:48
  706.4 15.6 %collective-permute-done.82.refs_3_ = bf16[512,1024]{1,0:T(8,128)(2,1)} collective-permute-done((bf16[512,1024]{1,0:T(8,128)(2,1)}, bf16[512,1024]{1,0:T(8,128)(2,1)}, u32[]{:S(2)}, u32[]{:S(2)}) %collective-permute-start.82) | collective-permute-done | bytes 1048608 | tf_op jit(solution)/shard_map/ppermute | solution.py:708
  726.3 13.7 %collective-permute-done.86.refs_4_ = bf16[1024,256]{1,0:T(8,128)(2,1)S(1)} collective-permute-done((bf16[1024,256]{1,0:T(8,128)(2,1)S(1)}, bf16[1024,256]{1,0:T(8,128)(2,1)S(1)}, u32[]{:S(2)}, u32[]{:S(2)}) %collective-permute-start.86) | collective-permute-done | bytes 524320 | tf_op jit(solution)/shard_map/ppermute | solution.py:48
  740.6 10.6 collective-permute-done.88.refs_6_
  755.4 13.6 %hidden_back.3 = (bf16[1024,2048]{1,0:T(8,128)(2,1)}, bf16[1024,1024]{1,0:T(8,128)(2,1)}, f32[8,8,128]{2,1,0:T(8,128)}, f32[8,1024]{1,0:T(8,128)}) custom-call(s32[8]{0:T(128)} %copy-done.141, s32[1]{0:T(128)} %bitcast.9.core_ref, bf16[1024,256]{1,0:T(8,128)(2,1)} %copy-done.82, bf16[1024,256]{1,0:T(8,128)(2,1)} %copy-done.124, ...), custom_call_target="tpu_custom_call" | custom-call | flops 1073741824 | bytes 4194304 | tf_op jit(solution)/shard_map/hidden_back/pallas_call | solution.py:258
  784.2 11.1 %collective-permute-done.99 = bf16[1040,256]{1,0:T(8,128)(2,1)S(1)} collective-permute-done((bf16[1040,256]{1,0:T(8,128)(2,1)S(1)}, bf16[1040,256]{1,0:T(8,128)(2,1)S(1)}, u32[]{:S(2)}, u32[]{:S(2)}) %collective-permute-start.99) | collective-permute-done | bytes 532512 | tf_op jit(solution)/shard_map/ppermute | solution.py:48
  797.1 6.3 convolution_convert_fusion.1
  823.8 14.3 %collective-permute-done.98 = bf16[1040,256]{1,0:T(8,128)(2,1)S(1)} collective-permute-done((bf16[1040,256]{1,0:T(8,128)(2,1)S(1)}, bf16[1040,256]{1,0:T(8,128)(2,1)S(1)}, u32[]{:S(2)}, u32[]{:S(2)}) %collective-permute-start.98) | collective-permute-done | bytes 532512 | tf_op jit(solution)/shard_map/ppermute | solution.py:48
  840.7 6.4 collective-permute-done.101.refs_3_
  850.6 9.0 convolution_convert_fusion
  863.2 15.1 %collective-permute-done.105.refs_4_ = bf16[1024,256]{1,0:T(8,128)(2,1)S(1)} collective-permute-done((bf16[1024,256]{1,0:T(8,128)(2,1)S(1)}, bf16[1024,256]{1,0:T(8,128)(2,1)S(1)}, u32[]{:S(2)}, u32[]{:S(2)}) %collective-permute-start.105) | collective-permute-done | bytes 524320 | tf_op jit(solution)/shard_map/ppermute | solution.py:48
  878.9 12.4 %collective-permute-done.107.refs_6_ = bf16[1024,256]{1,0:T(8,128)(2,1)S(1)} collective-permute-done((bf16[1024,256]{1,0:T(8,128)(2,1)S(1)}, bf16[1024,256]{1,0:T(8,128)(2,1)S(1)}, u32[]{:S(2)}, u32[]{:S(2)}) %collective-permute-start.107) | collective-permute-done | bytes 524320 | tf_op jit(solution)/shard_map/ppermute | solution.py:48
  893.4 7.0 gather_matmul.3
  902.7 8.8 attend_back.3.x_ref
  928.5 5.2 collective-permute-done.110
  940.4 12.5 %collective-permute-done.109 = bf16[1040,256]{1,0:T(8,128)(2,1)S(1)} collective-permute-done((bf16[1040,256]{1,0:T(8,128)(2,1)}, bf16[1040,256]{1,0:T(8,128)(2,1)S(1)}, u32[]{:S(2)}, u32[]{:S(2)}) %collective-permute-start.109) | collective-permute-done | bytes 532512 | tf_op jit(solution)/shard_map/ppermute | solution.py:48
  953.0 6.1 collective-permute-done.111
  960.3 9.9 collective-permute-done.114.refs_3_
  993.4 7.1 collective-permute-done.120
  1011.8 8.4 collective-permute-done.117
  1020.2 6.7 collective-permute-done.121
  1035.7 5.6 collective-permute-start.123
  1047.1 4.5 unpack.5
  1055.2 4.5 collective-permute-done.128.refs_1_
  1059.7 4.1 unpack.4
  1063.8 7.0 collective-permute-done.127.refs_1_
  (801 shorter events, 382.6 us)
Async XLA Ops:
  7.2 114.4 %all-gather.7.cloned.1.call-start = ((), (), s32[]{:S(2)}) async-start(), calls=%async_computation.6 | async-start | bytes 9437184 | tf_op jit(solution)/shard_map/all_gather | solution.py:696
  33.2 204.9 %all-gather.9.cloned.1.call-start = ((), (), s32[]{:S(2)}) async-start(), calls=%async_computation.7 | async-start | bytes 9437184 | tf_op jit(solution)/shard_map/all_gather | solution.py:696
  33.9 225.2 %all-gather.11.cloned.1.call-start = ((), (), s32[]{:S(2)}) async-start(), calls=%async_computation.8 | async-start | bytes 9437184 | tf_op jit(solution)/shard_map/all_gather | solution.py:696
  34.6 324.7 %all-gather.13.cloned.1.call-start = ((), (), s32[]{:S(2)}) async-start(), calls=%async_computation.9 | async-start | bytes 9437184 | tf_op jit(solution)/shard_map/all_gather | solution.py:696
  37.2 439.8 %all-gather.15.cloned.1.call-start = ((), (), s32[]{:S(2)}) async-start(), calls=%async_computation.10 | async-start | bytes 9437184 | tf_op jit(solution)/shard_map/all_gather | solution.py:696
  40.5 458.0 %all-gather.17.cloned.1.call-start = ((), (), s32[]{:S(2)}) async-start(), calls=%async_computation.11 | async-start | bytes 9437184 | tf_op jit(solution)/shard_map/all_gather | solution.py:696
  48.4 22.8 %collective-permute-start.6 = (bf16[1120,256]{1,0:T(8,128)(2,1)S(1)}, bf16[1120,256]{1,0:T(8,128)(2,1)S(1)}, u32[]{:S(2)}, u32[]{:S(2)}) collective-permute-start(bf16[1120,256]{1,0:T(8,128)(2,1)S(1)} %copy-done.78), channel_id=1, source_target_pairs={{0,4},{2,6},{4,0},{6,2},{1,5},{3,7},{5,1},{7,3},{8,12},{10,14},{12... | collective-permute-start | bytes 1720328 | tf_op jit(solution)/shard_map/ppermute | solution.py:48
  50.8 21.9 %collective-permute-start.4 = (bf16[1120,256]{1,0:T(8,128)(2,1)S(1)}, bf16[1120,256]{1,0:T(8,128)(2,1)S(1)}, u32[]{:S(2)}, u32[]{:S(2)}) collective-permute-start(bf16[1120,256]{1,0:T(8,128)(2,1)S(1)} %copy-done.78), channel_id=1, source_target_pairs={{0,2},{2,0},{4,6},{6,4},{1,3},{3,1},{5,7},{7,5},{8,10},{10,8},{12,... | collective-permute-start | bytes 1720328 | tf_op jit(solution)/shard_map/ppermute | solution.py:48
  52.1 20.7 %collective-permute-start.3 = (bf16[1120,256]{1,0:T(8,128)(2,1)S(1)}, bf16[1120,256]{1,0:T(8,128)(2,1)S(1)}, u32[]{:S(2)}, u32[]{:S(2)}) collective-permute-start(bf16[1120,256]{1,0:T(8,128)(2,1)S(1)} %copy-done.78), channel_id=1, source_target_pairs={{0,8},{8,0},{1,9},{9,1},{2,10},{10,2},{3,11},{11,3},{4,12},{12,4},... | collective-permute-start | bytes 1720328 | tf_op jit(solution)/shard_map/ppermute | solution.py:52
  52.1 33.0 %collective-permute-start.1 = (f32[1024,256]{1,0:T(8,128)S(1)}, f32[1024,256]{1,0:T(8,128)S(1)}, u32[]{:S(2)}, u32[]{:S(2)}) collective-permute-start(f32[1024,256]{1,0:T(8,128)S(1)} %copy-done.68), channel_id=1, source_target_pairs={{1,8},{8,1},{3,10},{10,3},{5,12},{12,5},{7,14},{14,7},{17,24},{24,... | collective-permute-start | bytes 3145736 | tf_op jit(solution)/shard_map/ppermute | solution.py:57
  71.2 20.8 %collective-permute-start.8 = (bf16[1120,256]{1,0:T(8,128)(2,1)S(1)}, bf16[1120,256]{1,0:T(8,128)(2,1)S(1)}, u32[]{:S(2)}, u32[]{:S(2)}) collective-permute-start(bf16[1120,256]{1,0:T(8,128)(2,1)S(1)} %collective-permute-done.6.refs_4_), channel_id=1, source_target_pairs={{0,2},{2,0},{4,6},{6,4},{1,3},{3,1},{5,7},{7,5},{8,10},{10,8},{12,... | collective-permute-start | bytes 1720328 | tf_op jit(solution)/shard_map/ppermute | solution.py:48
  72.2 20.0 %collective-permute-start.7 = (bf16[1120,256]{1,0:T(8,128)(2,1)S(1)}, bf16[1120,256]{1,0:T(8,128)(2,1)S(1)}, u32[]{:S(2)}, u32[]{:S(2)}) collective-permute-start(bf16[1120,256]{1,0:T(8,128)(2,1)S(1)} %collective-permute-done.6.refs_4_), channel_id=1, source_target_pairs={{0,8},{8,0},{1,9},{9,1},{2,10},{10,2},{3,11},{11,3},{4,12},{12,4},... | collective-permute-start | bytes 1720328 | tf_op jit(solution)/shard_map/ppermute | solution.py:52
  86.2 18.9 %collective-permute-start.14 = (bf16[1024,256]{1,0:T(8,128)(2,1)S(1)}, bf16[1024,256]{1,0:T(8,128)(2,1)}, u32[]{:S(2)}, u32[]{:S(2)}) collective-permute-start(bf16[1024,256]{1,0:T(8,128)(2,1)S(1)} %broadcast_select_fusion.5.refs_0_), channel_id=1, source_target_pairs={{0,4},{2,6},{4,0},{6,2},{1,5},{3,7},{5,1},{7,3},{8,12},{10,14},{12... | collective-permute-start | bytes 1572872 | tf_op jit(solution)/shard_map/ppermute | solution.py:48
  88.4 23.1 %collective-permute-start.12 = (bf16[1024,256]{1,0:T(8,128)(2,1)S(1)}, bf16[1024,256]{1,0:T(8,128)(2,1)}, u32[]{:S(2)}, u32[]{:S(2)}) collective-permute-start(bf16[1024,256]{1,0:T(8,128)(2,1)S(1)} %broadcast_select_fusion.5.refs_0_), channel_id=1, source_target_pairs={{0,2},{2,0},{4,6},{6,4},{1,3},{3,1},{5,7},{7,5},{8,10},{10,8},{12,... | collective-permute-start | bytes 1572872 | tf_op jit(solution)/shard_map/ppermute | solution.py:48
  89.6 46.8 %collective-permute-start.11 = (bf16[1024,256]{1,0:T(8,128)(2,1)S(1)}, bf16[1024,256]{1,0:T(8,128)(2,1)}, u32[]{:S(2)}, u32[]{:S(2)}) collective-permute-start(bf16[1024,256]{1,0:T(8,128)(2,1)S(1)} %broadcast_select_fusion.5.refs_0_), channel_id=1, source_target_pairs={{0,8},{8,0},{1,9},{9,1},{2,10},{10,2},{3,11},{11,3},{4,12},{12,4},... | collective-permute-start | bytes 1572872 | tf_op jit(solution)/shard_map/ppermute | solution.py:52
  92.0 19.5 %collective-permute-start.9 = (bf16[1120,256]{1,0:T(8,128)(2,1)S(1)}, bf16[1120,256]{1,0:T(8,128)(2,1)S(1)}, u32[]{:S(2)}, u32[]{:S(2)}) collective-permute-start(bf16[1120,256]{1,0:T(8,128)(2,1)S(1)} %collective-permute-done.8.refs_6_), channel_id=1, source_target_pairs={{0,8},{8,0},{1,9},{9,1},{2,10},{10,2},{3,11},{11,3},{4,12},{12,4},... | collective-permute-start | bytes 1720328 | tf_op jit(solution)/shard_map/ppermute | solution.py:52
  105.1 31.3 %collective-permute-start.15 = (bf16[1024,256]{1,0:T(8,128)(2,1)}, bf16[1024,256]{1,0:T(8,128)(2,1)}, u32[]{:S(2)}, u32[]{:S(2)}) collective-permute-start(bf16[1024,256]{1,0:T(8,128)(2,1)} %collective-permute-done.14.refs_4_), channel_id=1, source_target_pairs={{0,8},{8,0},{1,9},{9,1},{2,10},{10,2},{3,11},{11,3},{4,12},{12,4},... | collective-permute-start | bytes 1572872 | tf_op jit(solution)/shard_map/ppermute | solution.py:52
  111.5 25.0 %collective-permute-start.13 = (bf16[1024,256]{1,0:T(8,128)(2,1)}, bf16[1024,256]{1,0:T(8,128)(2,1)}, u32[]{:S(2)}, u32[]{:S(2)}) collective-permute-start(bf16[1024,256]{1,0:T(8,128)(2,1)} %collective-permute-done.12.refs_2_), channel_id=1, source_target_pairs={{0,8},{8,0},{1,9},{9,1},{2,10},{10,2},{3,11},{11,3},{4,12},{12,4},... | collective-permute-start | bytes 1572872 | tf_op jit(solution)/shard_map/ppermute | solution.py:52
  119.9 16.5 %collective-permute-start.17 = (bf16[1024,256]{1,0:T(8,128)(2,1)}, bf16[1024,256]{1,0:T(8,128)(2,1)S(1)}, u32[]{:S(2)}, u32[]{:S(2)}) collective-permute-start(bf16[1024,256]{1,0:T(8,128)(2,1)} %collective-permute-done.16.refs_6_), channel_id=1, source_target_pairs={{0,8},{8,0},{1,9},{9,1},{2,10},{10,2},{3,11},{11,3},{4,12},{12,4},... | collective-permute-start | bytes 1572872 | tf_op jit(solution)/shard_map/ppermute | solution.py:52
  161.0 33.1 %collective-permute-start.20 = (bf16[1040,256]{1,0:T(8,128)(2,1)S(1)}, bf16[1040,256]{1,0:T(8,128)(2,1)S(1)}, u32[]{:S(2)}, u32[]{:S(2)}) collective-permute-start(bf16[1040,256]{1,0:T(8,128)(2,1)S(1)} %add_convert_fusion.31), channel_id=1, source_target_pairs={{0,2},{2,0},{4,6},{6,4},{1,3},{3,1},{5,7},{7,5},{8,10},{10,8},{12,... | collective-permute-start | bytes 1597448 | tf_op jit(solution)/shard_map/ppermute | solution.py:48
  172.9 21.9 %collective-permute-start.24 = (bf16[1040,256]{1,0:T(8,128)(2,1)S(1)}, bf16[1040,256]{1,0:T(8,128)(2,1)S(1)}, u32[]{:S(2)}, u32[]{:S(2)}) collective-permute-start(bf16[1040,256]{1,0:T(8,128)(2,1)S(1)} %add_convert_fusion.28), channel_id=1, source_target_pairs={{0,4},{2,6},{4,0},{6,2},{1,5},{3,7},{5,1},{7,3},{8,12},{10,14},{12... | collective-permute-start | bytes 1597448 | tf_op jit(solution)/shard_map/ppermute | solution.py:48
  196.1 24.4 %collective-permute-start.28 = (bf16[1040,256]{1,0:T(8,128)(2,1)S(1)}, bf16[1040,256]{1,0:T(8,128)(2,1)S(1)}, u32[]{:S(2)}, u32[]{:S(2)}) collective-permute-start(bf16[1040,256]{1,0:T(8,128)(2,1)S(1)} %fusion.23.refs_0_), channel_id=1, source_target_pairs={{0,4},{2,6},{4,0},{6,2},{1,5},{3,7},{5,1},{7,3},{8,12},{10,14},{12... | collective-permute-start | bytes 1597448 | tf_op jit(solution)/shard_map/ppermute | solution.py:48
  199.2 25.2 %collective-permute-start.26 = (bf16[1040,256]{1,0:T(8,128)(2,1)S(1)}, bf16[1040,256]{1,0:T(8,128)(2,1)S(1)}, u32[]{:S(2)}, u32[]{:S(2)}) collective-permute-start(bf16[1040,256]{1,0:T(8,128)(2,1)S(1)} %fusion.23.refs_0_), channel_id=1, source_target_pairs={{0,2},{2,0},{4,6},{6,4},{1,3},{3,1},{5,7},{7,5},{8,10},{10,8},{12,... | collective-permute-start | bytes 1597448 | tf_op jit(solution)/shard_map/ppermute | solution.py:48
  271.5 356.5 %reduce-scatter.7.cloned.1.call-start = ((), (), s32[]{:S(2)}) async-start(), calls=%async_computation.12 | async-start | bytes 5242880 | tf_op jit(solution)/shard_map/reduce_scatter | solution.py:704
  282.3 32.8 %collective-permute-start.34 = (bf16[1040,256]{1,0:T(8,128)(2,1)S(1)}, bf16[1040,256]{1,0:T(8,128)(2,1)S(1)}, u32[]{:S(2)}, u32[]{:S(2)}) collective-permute-start(bf16[1040,256]{1,0:T(8,128)(2,1)S(1)} %add_convert_fusion.27), channel_id=1, source_target_pairs={{0,2},{2,0},{4,6},{6,4},{1,3},{3,1},{5,7},{7,5},{8,10},{10,8},{12,... | collective-permute-start | bytes 1597448 | tf_op jit(solution)/shard_map/ppermute | solution.py:48
  293.4 21.9 %collective-permute-start.38 = (bf16[1040,256]{1,0:T(8,128)(2,1)S(1)}, bf16[1040,256]{1,0:T(8,128)(2,1)S(1)}, u32[]{:S(2)}, u32[]{:S(2)}) collective-permute-start(bf16[1040,256]{1,0:T(8,128)(2,1)S(1)} %add_convert_fusion.24), channel_id=1, source_target_pairs={{0,4},{2,6},{4,0},{6,2},{1,5},{3,7},{5,1},{7,3},{8,12},{10,14},{12... | collective-permute-start | bytes 1597448 | tf_op jit(solution)/shard_map/ppermute | solution.py:48
  316.7 18.2 %collective-permute-start.42 = (bf16[1040,256]{1,0:T(8,128)(2,1)S(1)}, bf16[1040,256]{1,0:T(8,128)(2,1)S(1)}, u32[]{:S(2)}, u32[]{:S(2)}) collective-permute-start(bf16[1040,256]{1,0:T(8,128)(2,1)S(1)} %fusion.24.refs_0_), channel_id=1, source_target_pairs={{0,4},{2,6},{4,0},{6,2},{1,5},{3,7},{5,1},{7,3},{8,12},{10,14},{12... | collective-permute-start | bytes 1597448 | tf_op jit(solution)/shard_map/ppermute | solution.py:48
  319.8 26.2 %collective-permute-start.40 = (bf16[1040,256]{1,0:T(8,128)(2,1)S(1)}, bf16[1040,256]{1,0:T(8,128)(2,1)S(1)}, u32[]{:S(2)}, u32[]{:S(2)}) collective-permute-start(bf16[1040,256]{1,0:T(8,128)(2,1)S(1)} %fusion.24.refs_0_), channel_id=1, source_target_pairs={{0,2},{2,0},{4,6},{6,4},{1,3},{3,1},{5,7},{7,5},{8,10},{10,8},{12,... | collective-permute-start | bytes 1597448 | tf_op jit(solution)/shard_map/ppermute | solution.py:48
  334.9 17.8 %collective-permute-start.44 = (bf16[1040,256]{1,0:T(8,128)(2,1)S(1)}, bf16[1040,256]{1,0:T(8,128)(2,1)S(1)}, u32[]{:S(2)}, u32[]{:S(2)}) collective-permute-start(bf16[1040,256]{1,0:T(8,128)(2,1)S(1)} %collective-permute-done.42.refs_4_), channel_id=1, source_target_pairs={{0,2},{2,0},{4,6},{6,4},{1,3},{3,1},{5,7},{7,5},{8,10},{10,8},{12,... | collective-permute-start | bytes 1597448 | tf_op jit(solution)/shard_map/ppermute | solution.py:48
  391.2 20.1 %collective-permute-start.46 = (bf16[1040,256]{1,0:T(8,128)(2,1)S(1)}, bf16[1040,256]{1,0:T(8,128)(2,1)S(1)}, u32[]{:S(2)}, u32[]{:S(2)}) collective-permute-start(bf16[1040,256]{1,0:T(8,128)(2,1)S(1)} %get-tuple-element.287), channel_id=1, source_target_pairs={{0,8},{8,0},{1,9},{9,1},{2,10},{10,2},{3,11},{11,3},{4,12},{12,4},... | collective-permute-start | bytes 1597448 | tf_op jit(solution)/shard_map/ppermute | solution.py:52
  391.8 33.7 %collective-permute-start.48 = (bf16[1040,256]{1,0:T(8,128)(2,1)S(1)}, bf16[1040,256]{1,0:T(8,128)(2,1)S(1)}, u32[]{:S(2)}, u32[]{:S(2)}) collective-permute-start(bf16[1040,256]{1,0:T(8,128)(2,1)S(1)} %add_convert_fusion.23), channel_id=1, source_target_pairs={{0,2},{2,0},{4,6},{6,4},{1,3},{3,1},{5,7},{7,5},{8,10},{10,8},{12,... | collective-permute-start | bytes 1597448 | tf_op jit(solution)/shard_map/ppermute | solution.py:48
  404.4 29.9 %collective-permute-start.52 = (bf16[1040,256]{1,0:T(8,128)(2,1)S(1)}, bf16[1040,256]{1,0:T(8,128)(2,1)S(1)}, u32[]{:S(2)}, u32[]{:S(2)}) collective-permute-start(bf16[1040,256]{1,0:T(8,128)(2,1)S(1)} %add_convert_fusion.20), channel_id=1, source_target_pairs={{0,4},{2,6},{4,0},{6,2},{1,5},{3,7},{5,1},{7,3},{8,12},{10,14},{12... | collective-permute-start | bytes 1597448 | tf_op jit(solution)/shard_map/ppermute | solution.py:48
  435.6 26.2 %collective-permute-start.56 = (bf16[1040,256]{1,0:T(8,128)(2,1)S(1)}, bf16[1040,256]{1,0:T(8,128)(2,1)S(1)}, u32[]{:S(2)}, u32[]{:S(2)}) collective-permute-start(bf16[1040,256]{1,0:T(8,128)(2,1)S(1)} %fusion.25.refs_0_), channel_id=1, source_target_pairs={{0,4},{2,6},{4,0},{6,2},{1,5},{3,7},{5,1},{7,3},{8,12},{10,14},{12... | collective-permute-start | bytes 1597448 | tf_op jit(solution)/shard_map/ppermute | solution.py:48
  435.6 27.0 %collective-permute-start.54 = (bf16[1040,256]{1,0:T(8,128)(2,1)S(1)}, bf16[1040,256]{1,0:T(8,128)(2,1)S(1)}, u32[]{:S(2)}, u32[]{:S(2)}) collective-permute-start(bf16[1040,256]{1,0:T(8,128)(2,1)S(1)} %fusion.25.refs_0_), channel_id=1, source_target_pairs={{0,2},{2,0},{4,6},{6,4},{1,3},{3,1},{5,7},{7,5},{8,10},{10,8},{12,... | collective-permute-start | bytes 1597448 | tf_op jit(solution)/shard_map/ppermute | solution.py:48
  548.8 157.5 %reduce-scatter.9.cloned.1.call-start = ((), (), s32[]{:S(2)}) async-start(), calls=%async_computation.13 | async-start | bytes 5242880 | tf_op jit(solution)/shard_map/reduce_scatter | solution.py:704
  548.9 23.4 %collective-permute-start.63 = (bf16[1040,256]{1,0:T(8,128)(2,1)}, bf16[1040,256]{1,0:T(8,128)(2,1)S(1)}, u32[]{:S(2)}, u32[]{:S(2)}) collective-permute-start(bf16[1040,256]{1,0:T(8,128)(2,1)} %add_convert_fusion.19), channel_id=1, source_target_pairs={{0,2},{2,0},{4,6},{6,4},{1,3},{3,1},{5,7},{7,5},{8,10},{10,8},{12,... | collective-permute-start | bytes 1597448 | tf_op jit(solution)/shard_map/ppermute | solution.py:48
  549.0 23.3 %collective-permute-start.67 = (bf16[1040,256]{1,0:T(8,128)(2,1)}, bf16[1040,256]{1,0:T(8,128)(2,1)S(1)}, u32[]{:S(2)}, u32[]{:S(2)}) collective-permute-start(bf16[1040,256]{1,0:T(8,128)(2,1)} %add_convert_fusion.16), channel_id=1, source_target_pairs={{0,4},{2,6},{4,0},{6,2},{1,5},{3,7},{5,1},{7,3},{8,12},{10,14},{12... | collective-permute-start | bytes 1597448 | tf_op jit(solution)/shard_map/ppermute | solution.py:48
  550.3 36.2 %collective-permute-start.60 = (f32[1024,256]{1,0:T(8,128)}, f32[1024,256]{1,0:T(8,128)S(1)}, u32[]{:S(2)}, u32[]{:S(2)}) collective-permute-start(f32[1024,256]{1,0:T(8,128)} %get-tuple-element.304), channel_id=1, source_target_pairs={{1,8},{8,1},{3,10},{10,3},{5,12},{12,5},{7,14},{14,7},{17,24},{24,... | collective-permute-start | bytes 3145736 | tf_op jit(solution)/shard_map/ppermute | solution.py:57
  594.9 253.1 %reduce-scatter.11.cloned.1.call-start = ((), (), s32[]{:S(2)}) async-start(), calls=%async_computation.14 | async-start | bytes 5242880 | tf_op jit(solution)/shard_map/reduce_scatter | solution.py:704
  596.8 16.1 %collective-permute-start.71 = (bf16[1024,256]{1,0:T(8,128)(2,1)S(1)}, bf16[1024,256]{1,0:T(8,128)(2,1)S(1)}, u32[]{:S(2)}, u32[]{:S(2)}) collective-permute-start(bf16[1024,256]{1,0:T(8,128)(2,1)S(1)} %convert_element_type.817.refs_0_), channel_id=1, source_target_pairs={{0,4},{2,6},{4,0},{6,2},{1,5},{3,7},{5,1},{7,3},{8,12},{10,14},{12... | collective-permute-start | bytes 1572872 | tf_op jit(solution)/shard_map/ppermute | solution.py:48
  596.9 17.2 %collective-permute-start.69 = (bf16[1024,256]{1,0:T(8,128)(2,1)S(1)}, bf16[1024,256]{1,0:T(8,128)(2,1)S(1)}, u32[]{:S(2)}, u32[]{:S(2)}) collective-permute-start(bf16[1024,256]{1,0:T(8,128)(2,1)S(1)} %convert_element_type.817.refs_0_), channel_id=1, source_target_pairs={{0,2},{2,0},{4,6},{6,4},{1,3},{3,1},{5,7},{7,5},{8,10},{10,8},{12,... | collective-permute-start | bytes 1572872 | tf_op jit(solution)/shard_map/ppermute | solution.py:48
  679.9 213.5 %reduce-scatter.13.cloned.1.call-start = ((), (), s32[]{:S(2)}) async-start(), calls=%async_computation.15 | async-start | bytes 5242880 | tf_op jit(solution)/shard_map/reduce_scatter | solution.py:704
  679.9 24.1 %collective-permute-start.77 = (bf16[1040,256]{1,0:T(8,128)(2,1)}, bf16[1040,256]{1,0:T(8,128)(2,1)S(1)}, u32[]{:S(2)}, u32[]{:S(2)}) collective-permute-start(bf16[1040,256]{1,0:T(8,128)(2,1)} %add_convert_fusion.15), channel_id=1, source_target_pairs={{0,2},{2,0},{4,6},{6,4},{1,3},{3,1},{5,7},{7,5},{8,10},{10,8},{12,... | collective-permute-start | bytes 1597448 | tf_op jit(solution)/shard_map/ppermute | solution.py:48
  680.3 23.8 %collective-permute-start.81 = (bf16[1040,256]{1,0:T(8,128)(2,1)}, bf16[1040,256]{1,0:T(8,128)(2,1)S(1)}, u32[]{:S(2)}, u32[]{:S(2)}) collective-permute-start(bf16[1040,256]{1,0:T(8,128)(2,1)} %add_convert_fusion.12), channel_id=1, source_target_pairs={{0,4},{2,6},{4,0},{6,2},{1,5},{3,7},{5,1},{7,3},{8,12},{10,14},{12... | collective-permute-start | bytes 1597448 | tf_op jit(solution)/shard_map/ppermute | solution.py:48
  683.2 38.8 %collective-permute-start.82 = (bf16[512,1024]{1,0:T(8,128)(2,1)}, bf16[512,1024]{1,0:T(8,128)(2,1)}, u32[]{:S(2)}, u32[]{:S(2)}) collective-permute-start(bf16[512,1024]{1,0:T(8,128)(2,1)} %reduce-scatter.7.cloned.1.call-done.refs_2_), channel_id=1, source_target_pairs={{1,8},{8,1},{3,10},{10,3},{5,12},{12,5},{7,14},{14,7},{17,24},{24,... | collective-permute-start | bytes 3145736 | tf_op jit(solution)/shard_map/ppermute | solution.py:708
  803.4 238.0 %reduce-scatter.17.cloned.1.call-start = ((), (), s32[]{:S(2)}) async-start(), calls=%async_computation.17 | async-start | bytes 5242880 | tf_op jit(solution)/shard_map/reduce_scatter | solution.py:704
  811.5 35.6 %collective-permute-start.101 = (bf16[512,1024]{1,0:T(8,128)(2,1)S(1)}, bf16[512,1024]{1,0:T(8,128)(2,1)S(1)}, u32[]{:S(2)}, u32[]{:S(2)}) collective-permute-start(bf16[512,1024]{1,0:T(8,128)(2,1)S(1)} %copy-done.41), channel_id=1, source_target_pairs={{1,8},{8,1},{3,10},{10,3},{5,12},{12,5},{7,14},{14,7},{17,24},{24,... | collective-permute-start | bytes 3145736 | tf_op jit(solution)/shard_map/ppermute | solution.py:708
  813.4 24.8 %collective-permute-start.98 = (bf16[1040,256]{1,0:T(8,128)(2,1)S(1)}, bf16[1040,256]{1,0:T(8,128)(2,1)S(1)}, u32[]{:S(2)}, u32[]{:S(2)}) collective-permute-start(bf16[1040,256]{1,0:T(8,128)(2,1)S(1)} %copy-done.115), channel_id=1, source_target_pairs={{0,2},{2,0},{4,6},{6,4},{1,3},{3,1},{5,7},{7,5},{8,10},{10,8},{12,... | collective-permute-start | bytes 1597448 | tf_op jit(solution)/shard_map/ppermute | solution.py:48
  813.5 25.9 %collective-permute-start.100 = (bf16[1040,256]{1,0:T(8,128)(2,1)S(1)}, bf16[1040,256]{1,0:T(8,128)(2,1)S(1)}, u32[]{:S(2)}, u32[]{:S(2)}) collective-permute-start(bf16[1040,256]{1,0:T(8,128)(2,1)S(1)} %copy-done.116), channel_id=1, source_target_pairs={{0,4},{2,6},{4,0},{6,2},{1,5},{3,7},{5,1},{7,3},{8,12},{10,14},{12... | collective-permute-start | bytes 1597448 | tf_op jit(solution)/shard_map/ppermute | solution.py:48
  859.6 183.7 %reduce-scatter.15.cloned.1.call-start = ((), (), s32[]{:S(2)}) async-start(), calls=%async_computation.16 | async-start | bytes 5242880 | tf_op jit(solution)/shard_map/reduce_scatter | solution.py:704
  860.0 18.3 %collective-permute-start.105 = (bf16[1024,256]{1,0:T(8,128)(2,1)S(1)}, bf16[1024,256]{1,0:T(8,128)(2,1)S(1)}, u32[]{:S(2)}, u32[]{:S(2)}) collective-permute-start(bf16[1024,256]{1,0:T(8,128)(2,1)S(1)} %convert_element_type.868.refs_0_), channel_id=1, source_target_pairs={{0,4},{2,6},{4,0},{6,2},{1,5},{3,7},{5,1},{7,3},{8,12},{10,14},{12... | collective-permute-start | bytes 1572872 | tf_op jit(solution)/shard_map/ppermute | solution.py:48
  862.0 16.8 %collective-permute-start.103 = (bf16[1024,256]{1,0:T(8,128)(2,1)S(1)}, bf16[1024,256]{1,0:T(8,128)(2,1)S(1)}, u32[]{:S(2)}, u32[]{:S(2)}) collective-permute-start(bf16[1024,256]{1,0:T(8,128)(2,1)S(1)} %convert_element_type.868.refs_0_), channel_id=1, source_target_pairs={{0,2},{2,0},{4,6},{6,4},{1,3},{3,1},{5,7},{7,5},{8,10},{10,8},{12,... | collective-permute-start | bytes 1572872 | tf_op jit(solution)/shard_map/ppermute | solution.py:48
  920.2 19.1 %collective-permute-start.113 = (f32[1024,256]{1,0:T(8,128)}, f32[1024,256]{1,0:T(8,128)S(1)}, u32[]{:S(2)}, u32[]{:S(2)}) collective-permute-start(f32[1024,256]{1,0:T(8,128)} %copy-done.70), channel_id=1, source_target_pairs={{1,8},{8,1},{3,10},{10,3},{5,12},{12,5},{7,14},{14,7},{17,24},{24,... | collective-permute-start | bytes 3145736 | tf_op jit(solution)/shard_map/ppermute | solution.py:57
  923.1 47.1 %collective-permute-start.114 = (bf16[512,1024]{1,0:T(8,128)(2,1)}, bf16[512,1024]{1,0:T(8,128)(2,1)S(1)}, u32[]{:S(2)}, u32[]{:S(2)}) collective-permute-start(bf16[512,1024]{1,0:T(8,128)(2,1)} %reduce-scatter.11.cloned.1.call-done.refs_2_), channel_id=1, source_target_pairs={{1,8},{8,1},{3,10},{10,3},{5,12},{12,5},{7,14},{14,7},{17,24},{24,... | collective-permute-start | bytes 3145736 | tf_op jit(solution)/shard_map/ppermute | solution.py:708
  927.0 26.0 %collective-permute-start.109 = (bf16[1040,256]{1,0:T(8,128)(2,1)}, bf16[1040,256]{1,0:T(8,128)(2,1)S(1)}, u32[]{:S(2)}, u32[]{:S(2)}) collective-permute-start(bf16[1040,256]{1,0:T(8,128)(2,1)} %add_convert_fusion.8), channel_id=1, source_target_pairs={{0,2},{2,0},{4,6},{6,4},{1,3},{3,1},{5,7},{7,5},{8,10},{10,8},{12,... | collective-permute-start | bytes 1597448 | tf_op jit(solution)/shard_map/ppermute | solution.py:48
  934.9 24.1 %collective-permute-start.111 = (bf16[1040,256]{1,0:T(8,128)(2,1)S(1)}, bf16[1040,256]{1,0:T(8,128)(2,1)S(1)}, u32[]{:S(2)}, u32[]{:S(2)}) collective-permute-start(bf16[1040,256]{1,0:T(8,128)(2,1)S(1)} %add_convert_fusion.4), channel_id=1, source_target_pairs={{0,4},{2,6},{4,0},{6,2},{1,5},{3,7},{5,1},{7,3},{8,12},{10,14},{12... | collective-permute-start | bytes 1597448 | tf_op jit(solution)/shard_map/ppermute | solution.py:48
  988.8 20.6 %collective-permute-start.112 = (f32[1024,256]{1,0:T(8,128)}, f32[1024,256]{1,0:T(8,128)}, u32[]{:S(2)}, u32[]{:S(2)}) collective-permute-start(f32[1024,256]{1,0:T(8,128)} %fusion.11), channel_id=1, source_target_pairs={{1,8},{8,1},{3,10},{10,3},{5,12},{12,5},{7,14},{14,7},{17,24},{24,... | collective-permute-start | bytes 3145736 | tf_op jit(solution)/shard_map/ppermute | solution.py:57
  991.1 20.7 %collective-permute-start.115 = (bf16[1040,256]{1,0:T(8,128)(2,1)}, bf16[1040,256]{1,0:T(8,128)(2,1)}, u32[]{:S(2)}, u32[]{:S(2)}) collective-permute-start(bf16[1040,256]{1,0:T(8,128)(2,1)} %get-tuple-element.433), channel_id=1, source_target_pairs={{0,8},{8,0},{1,9},{9,1},{2,10},{10,2},{3,11},{11,3},{4,12},{12,4},... | collective-permute-start | bytes 1597448 | tf_op jit(solution)/shard_map/ppermute | solution.py:52
  993.4 26.8 %collective-permute-start.117 = (bf16[1040,256]{1,0:T(8,128)(2,1)}, bf16[1040,256]{1,0:T(8,128)(2,1)}, u32[]{:S(2)}, u32[]{:S(2)}) collective-permute-start(bf16[1040,256]{1,0:T(8,128)(2,1)} %add_convert_fusion.3), channel_id=1, source_target_pairs={{0,2},{2,0},{4,6},{6,4},{1,3},{3,1},{5,7},{7,5},{8,10},{10,8},{12,... | collective-permute-start | bytes 1597448 | tf_op jit(solution)/shard_map/ppermute | solution.py:48
  1002.7 24.2 %collective-permute-start.121 = (bf16[1040,256]{1,0:T(8,128)(2,1)}, bf16[1040,256]{1,0:T(8,128)(2,1)}, u32[]{:S(2)}, u32[]{:S(2)}) collective-permute-start(bf16[1040,256]{1,0:T(8,128)(2,1)} %add_convert_fusion), channel_id=1, source_target_pairs={{0,4},{2,6},{4,0},{6,2},{1,5},{3,7},{5,1},{7,3},{8,12},{10,14},{12... | collective-permute-start | bytes 1597448 | tf_op jit(solution)/shard_map/ppermute | solution.py:48
  1005.6 23.0 %collective-permute-start.122 = (bf16[512,1024]{1,0:T(8,128)(2,1)S(1)}, bf16[512,1024]{1,0:T(8,128)(2,1)S(1)}, u32[]{:S(2)}, u32[]{:S(2)}) collective-permute-start(bf16[512,1024]{1,0:T(8,128)(2,1)S(1)} %copy-done.46), channel_id=1, source_target_pairs={{1,8},{8,1},{3,10},{10,3},{5,12},{12,5},{7,14},{14,7},{17,24},{24,... | collective-permute-start | bytes 3145736 | tf_op jit(solution)/shard_map/ppermute | solution.py:708
  1035.7 17.1 %collective-permute-start.123 = (bf16[1024,256]{1,0:T(8,128)(2,1)}, bf16[1024,256]{1,0:T(8,128)(2,1)}, u32[]{:S(2)}, u32[]{:S(2)}) collective-permute-start(bf16[1024,256]{1,0:T(8,128)(2,1)} %get-tuple-element.497), channel_id=1, source_target_pairs={{1,8},{8,1},{3,10},{10,3},{5,12},{12,5},{7,14},{14,7},{17,24},{24,... | collective-permute-start | bytes 1572872 | tf_op jit(solution)/shard_map/ppermute | solution.py:57
  1041.3 18.4 %collective-permute-start.128 = (bf16[512,1024]{1,0:T(8,128)(2,1)}, bf16[512,1024]{1,0:T(8,128)(2,1)}, u32[]{:S(2)}, u32[]{:S(2)}) collective-permute-start(bf16[512,1024]{1,0:T(8,128)(2,1)} %reduce-scatter.17.cloned.1.call-done.refs_0_), channel_id=1, source_target_pairs={{1,8},{8,1},{3,10},{10,3},{5,12},{12,5},{7,14},{14,7},{17,24},{24,... | collective-permute-start | bytes 3145736 | tf_op jit(solution)/shard_map/ppermute | solution.py:708
  1043.3 27.5 %collective-permute-start.127 = (bf16[512,1024]{1,0:T(8,128)(2,1)}, bf16[512,1024]{1,0:T(8,128)(2,1)S(1)}, u32[]{:S(2)}, u32[]{:S(2)}) collective-permute-start(bf16[512,1024]{1,0:T(8,128)(2,1)} %reduce-scatter.15.cloned.1.call-done.refs_0_), channel_id=1, source_target_pairs={{1,8},{8,1},{3,10},{10,3},{5,12},{12,5},{7,14},{14,7},{17,24},{24,... | collective-permute-start | bytes 3145736 | tf_op jit(solution)/shard_map/ppermute | solution.py:708
  (238 other events, 2156.4 us)
Sparse Core Ops, SparseCore 0:
  33.3 62.9 all-gather.6
  98.7 54.9 all-gather.8
  155.6 54.6 all-gather.10
  212.0 54.3 all-gather.12
  268.2 54.3 all-gather.14
  324.4 54.3 all-gather.16
  549.0 61.3 reduce-scatter.6
  613.6 52.6 reduce-scatter.8
  680.0 61.4 reduce-scatter.10
  803.5 63.8 reduce-scatter.12
  870.3 52.6 reduce-scatter.16
  926.7 63.8 reduce-scatter.14

commit v4 on v3

--- a/solution.py
+++ b/solution.py
@@ -411,13 +411,14 @@
         out_ref[tokens:, :] = extra_ref[...]
 
 
-def slot_matmul(x, w, extra, other):
+def slot_matmul(x, w, extra):
     tokens, depth = x.shape
-    n = ring_size()
+    n = 2 * ring_size()
     f = extra.shape[1]
-    blocks = slot_blocks()[1 if other else 0 :: 2]
+    blocks = slot_blocks()
+    blocks = jnp.concatenate([blocks[1::2], blocks[::2]])
     tile = min(tokens, 512)
-    return pl.pallas_call(
+    outs = pl.pallas_call(
         functools.partial(slot_matmul_kernel, n, tile),
         grid_spec=pltpu.PrefetchScalarGridSpec(
             num_scalar_prefetch=2,
@@ -436,12 +437,11 @@
         ),
         name="slot_matmul",
     )(blocks, core_index(), x, *[w.blocks] * n, extra)
+    return outs[n // 2 :], outs[: n // 2]
 
 
 def column_sum(x, w, extra):
-    other = slot_matmul(x, w, extra, True)
-    mine = slot_matmul(x, w, extra, False)
-    return pair_blocks(mine, other)
+    return pair_blocks(*slot_matmul(x, w, extra))
 
 
 def block_scores(query, key, row0, column0, length, slope):

time: 1090 us -> 1100 us (level)
  starting transfers between devices: 145 us -> 235 us
  waiting for transfers between devices: 502 us -> 439 us
    ppermute x48, waiting for transfers between devices: 418 us -> 327 us  [ring(): return lax.ppermute(value, 't', [(i, i ^ k) for i in range(ring_size())])]
    ppermute x48, starting transfers between devices: 70.4 us -> 122 us  [ring(): return lax.ppermute(value, 't', [(i, i ^ k) for i in range(ring_size())])]
    ppermute x65, starting transfers between devices: 27.3 us -> 64.9 us  [partner(): return lax.ppermute(value, 'c', [(0, 1), (1, 0)])]
    ppermute x8, waiting for transfers between devices: 31.9 us -> 56.3 us  [swap_roles(): lax.ppermute(value, ('c', 'x'), [(1, 2), (2, 1)])]
    unnamed x350 -> x342, local copies, waits for them, and re-layouts: 89 us -> 80.8 us
    pallas_call x16 -> x8, Pallas kernels: 41.1 us -> 33.5 us  [slot_matmul(): pl.pallas_call(functools.partial(slot_matmul_kernel, n, tile), grid_spec=...]
  transfers between devices with their start and end apart: 141 -> 141, of which waited for: 57 -> 60; matrix products, arithmetic and copies ran while one was open for 11% -> 11% of each run, Pallas kernels for 16% -> 15%
where the time goes in v4:
time: 1100 us; the launch traced here: 1090 us
  waiting for transfers between devices  439 us (40%)
  starting transfers between devices  235 us (21%)
  Pallas kernels  185 us (17%)
  local copies, waits for them, and re-layouts  105 us (10%)
  other arithmetic  70.3 us (6%)
  matrix products  38.6 us (4%)
  between operations  18 us (2%)
    ppermute x48, waiting for transfers between devices, ring(): return lax.ppermute(value, 't', [(i, i ^ k) for i in range(ring_size())])  327 us
    ppermute x48, starting transfers between devices, ring(): return lax.ppermute(value, 't', [(i, i ^ k) for i in range(ring_size())])  122 us
    unnamed x342, local copies, waits for them, and re-layouts  80.8 us
    ppermute x65, starting transfers between devices, partner(): return lax.ppermute(value, 'c', [(0, 1), (1, 0)])  64.9 us
    pallas_call x4, Pallas kernels, norm_matmul(): pl.pallas_call(functools.partial(norm_kernel, slots, width, gelu), grid_s...  62.6 us
    ppermute x8, waiting for transfers between devices, swap_roles(): lax.ppermute(value, ('c', 'x'), [(1, 2), (2, 1)])  56.3 us
    ppermute x6, waiting for transfers between devices, swapped(): return (value, lax.ppermute(value, ('c', 'x'), [(1, 2), (2, 1)]))  39.8 us
    dot_general x8, matrix products, term(): jnp.einsum('td,tn->dn', a, b, preferred_element_type=F32)  38.6 us
  transfers between devices with their start and end apart: 141, of which 60 were waited for; matrix products, arithmetic and copies ran while one was open for 11% of the time, Pallas kernels for 15%

profile of v4, /device:TPU:1, one launch (start us, length us, event | category | flops | bytes accessed | tf_op | source)
XLA Modules:
  0.0 1090.2 jit_solution(7417643846897364272)
XLA Ops:
  60.8 10.5 collective-permute-done.6.refs_4_
  73.8 11.4 %collective-permute-done.1 = f32[1024,256]{1,0:T(8,128)S(1)} collective-permute-done((f32[1024,256]{1,0:T(8,128)S(1)}, f32[1024,256]{1,0:T(8,128)S(1)}, u32[]{:S(2)}, u32[]{:S(2)}) %collective-permute-start.1) | collective-permute-done | bytes 1048608 | tf_op jit(solution)/shard_map/ppermute | solution.py:57
  92.4 12.9 %collective-permute-done.14.refs_4_ = bf16[1024,256]{1,0:T(8,128)(2,1)} collective-permute-done((bf16[1024,256]{1,0:T(8,128)(2,1)S(1)}, bf16[1024,256]{1,0:T(8,128)(2,1)}, u32[]{:S(2)}, u32[]{:S(2)}) %collective-permute-start.14) | collective-permute-done | bytes 524320 | tf_op jit(solution)/shard_map/ppermute | solution.py:48
  105.3 6.3 collective-permute-done.12.refs_2_
  122.4 14.2 %norm_matmul.4 = (bf16[1024,2048]{1,0:T(8,128)(2,1)}, f32[1024,256]{1,0:T(8,128)}, f32[1024,128]{1,0:T(8,128)}, f32[16,768]{1,0:T(8,128)}, bf16[1024,768]{1,0:T(8,128)(2,1)}) custom-call(s32[8]{0:T(128)} %copy-done.138, s32[1]{0:T(128)} %bitcast.9.core_ref, bf16[1120,256]{1,0:T(8,128)(2,1)} %broadcast_select_fusion.refs_0_, bf16[1120,256]{1,0:T(8,128)(2,1)} %copy-done.91, ...), custom_call_target="tpu_custom_call" | custom-call | flops 805306368 | bytes 4194304 | tf_op jit(solution)/shard_map/norm_matmul/pallas_call | solution.py:174
  138.3 7.1 attend.2
  156.4 10.9 %collective-permute-done.23 = bf16[1040,256]{1,0:T(8,128)(2,1)S(1)} collective-permute-done((bf16[1040,256]{1,0:T(8,128)(2,1)S(1)}, bf16[1040,256]{1,0:T(8,128)(2,1)S(1)}, u32[]{:S(2)}, u32[]{:S(2)}) %collective-permute-start.23) | collective-permute-done | bytes 532512 | tf_op jit(solution)/shard_map/ppermute | solution.py:48
  170.8 18.2 %collective-permute-done.20 = bf16[1040,256]{1,0:T(8,128)(2,1)S(1)} collective-permute-done((bf16[1040,256]{1,0:T(8,128)(2,1)S(1)}, bf16[1040,256]{1,0:T(8,128)(2,1)S(1)}, u32[]{:S(2)}, u32[]{:S(2)}) %collective-permute-start.20) | collective-permute-done | bytes 532512 | tf_op jit(solution)/shard_map/ppermute | solution.py:48
  198.1 9.8 collective-permute-done.28.refs_4_
  207.9 7.6 collective-permute-start.30
  219.6 6.5 collective-permute-done.30.refs_6_
  235.8 17.4 %norm_matmul.5 = (bf16[1024,2048]{1,0:T(8,128)(2,1)}, f32[1024,256]{1,0:T(8,128)}, f32[1024,128]{1,0:T(8,128)}, f32[16,1024]{1,0:T(8,128)}, f32[1024,1024]{1,0:T(8,128)}, /*index=5*/bf16[1024,1024]{1,0:T(8,128)(2,1)}) custom-call(s32[8]{0:T(128)} %copy-done.138, s32[1]{0:T(128)} %bitcast.9.core_ref, bf16[1040,256]{1,0:T(8,128)(2,1)} %copy-done.78, ...), custom_call_target="tpu_custom_call" | custom-call | flops 1073741824 | bytes 4194304 | tf_op jit(solution)/shard_map/norm_matmul/pallas_call | solution.py:174
  258.4 5.8 slot_matmul.9
  271.7 11.5 %collective-permute-done.37 = bf16[1040,256]{1,0:T(8,128)(2,1)S(1)} collective-permute-done((bf16[1040,256]{1,0:T(8,128)(2,1)S(1)}, bf16[1040,256]{1,0:T(8,128)(2,1)S(1)}, u32[]{:S(2)}, u32[]{:S(2)}) %collective-permute-start.37) | collective-permute-done | bytes 532512 | tf_op jit(solution)/shard_map/ppermute | solution.py:48
  283.5 7.1 collective-permute-start.38
  290.7 14.1 %collective-permute-done.34 = bf16[1040,256]{1,0:T(8,128)(2,1)S(1)} collective-permute-done((bf16[1040,256]{1,0:T(8,128)(2,1)S(1)}, bf16[1040,256]{1,0:T(8,128)(2,1)S(1)}, u32[]{:S(2)}, u32[]{:S(2)}) %collective-permute-start.34) | collective-permute-done | bytes 532512 | tf_op jit(solution)/shard_map/ppermute | solution.py:48
  309.5 14.0 %collective-permute-start.40 = (bf16[1040,256]{1,0:T(8,128)(2,1)S(1)}, bf16[1040,256]{1,0:T(8,128)(2,1)S(1)}, u32[]{:S(2)}, u32[]{:S(2)}) collective-permute-start(bf16[1040,256]{1,0:T(8,128)(2,1)S(1)} %fusion.24.refs_0_), channel_id=1, source_target_pairs={{0,2},{2,0},{4,6},{6,4},{1,3},{3,1},{5,7},{7,5},{8,10},{10,8},{12,... | collective-permute-start | bytes 1597448 | tf_op jit(solution)/shard_map/ppermute | solution.py:48
  323.5 9.0 collective-permute-start.44
  333.1 14.1 %collective-permute-start.39 = (bf16[1040,256]{1,0:T(8,128)(2,1)S(1)}, bf16[1040,256]{1,0:T(8,128)(2,1)S(1)}, u32[]{:S(2)}, u32[]{:S(2)}) collective-permute-start(bf16[1040,256]{1,0:T(8,128)(2,1)S(1)} %fusion.24.refs_0_), channel_id=1, source_target_pairs={{0,8},{8,0},{1,9},{9,1},{2,10},{10,2},{3,11},{11,3},{4,12},{12,4},... | collective-permute-start | bytes 1597448 | tf_op jit(solution)/shard_map/ppermute | solution.py:52
  347.8 6.1 collective-permute-start.45
  357.6 14.0 %norm_matmul.6 = (bf16[1024,2048]{1,0:T(8,128)(2,1)}, f32[1024,256]{1,0:T(8,128)}, f32[1024,128]{1,0:T(8,128)}, f32[16,768]{1,0:T(8,128)}, bf16[1024,768]{1,0:T(8,128)(2,1)}) custom-call(s32[8]{0:T(128)} %copy-done.138, s32[1]{0:T(128)} %bitcast.9.core_ref, bf16[1040,256]{1,0:T(8,128)(2,1)} %copy-done.77, bf16[1040,256]{1,0:T(8,128)(2,1)} %copy-done.99, ...), custom_call_target="tpu_custom_call" | custom-call | flops 805306368 | bytes 4194304 | tf_op jit(solution)/shard_map/norm_matmul/pallas_call | solution.py:174
  373.2 7.1 attend.3
  391.6 11.3 %collective-permute-done.51 = bf16[1040,256]{1,0:T(8,128)(2,1)S(1)} collective-permute-done((bf16[1040,256]{1,0:T(8,128)(2,1)S(1)}, bf16[1040,256]{1,0:T(8,128)(2,1)S(1)}, u32[]{:S(2)}, u32[]{:S(2)}) %collective-permute-start.51) | collective-permute-done | bytes 532512 | tf_op jit(solution)/shard_map/ppermute | solution.py:48
  403.1 5.9 collective-permute-start.52
  409.1 15.2 %collective-permute-done.48 = bf16[1040,256]{1,0:T(8,128)(2,1)S(1)} collective-permute-done((bf16[1040,256]{1,0:T(8,128)(2,1)S(1)}, bf16[1040,256]{1,0:T(8,128)(2,1)S(1)}, u32[]{:S(2)}, u32[]{:S(2)}) %collective-permute-start.48) | collective-permute-done | bytes 532512 | tf_op jit(solution)/shard_map/ppermute | solution.py:48
  429.1 12.2 %collective-permute-start.54 = (bf16[1040,256]{1,0:T(8,128)(2,1)S(1)}, bf16[1040,256]{1,0:T(8,128)(2,1)S(1)}, u32[]{:S(2)}, u32[]{:S(2)}) collective-permute-start(bf16[1040,256]{1,0:T(8,128)(2,1)S(1)} %fusion.25.refs_0_), channel_id=1, source_target_pairs={{0,2},{2,0},{4,6},{6,4},{1,3},{3,1},{5,7},{7,5},{8,10},{10,8},{12,... | collective-permute-start | bytes 1597448 | tf_op jit(solution)/shard_map/ppermute | solution.py:48
  441.3 9.4 collective-permute-start.58
  450.7 13.8 %collective-permute-start.53 = (bf16[1040,256]{1,0:T(8,128)(2,1)S(1)}, bf16[1040,256]{1,0:T(8,128)(2,1)}, u32[]{:S(2)}, u32[]{:S(2)}) collective-permute-start(bf16[1040,256]{1,0:T(8,128)(2,1)S(1)} %fusion.25.refs_0_), channel_id=1, source_target_pairs={{0,8},{8,0},{1,9},{9,1},{2,10},{10,2},{3,11},{11,3},{4,12},{12,4},... | collective-permute-start | bytes 1597448 | tf_op jit(solution)/shard_map/ppermute | solution.py:52
  465.0 6.7 collective-permute-start.59
  476.8 17.0 %norm_matmul.7 = (bf16[1024,2048]{1,0:T(8,128)(2,1)}, f32[1024,256]{1,0:T(8,128)}, f32[1024,128]{1,0:T(8,128)}, f32[16,1024]{1,0:T(8,128)}, f32[1024,1024]{1,0:T(8,128)}, /*index=5*/bf16[1024,1024]{1,0:T(8,128)(2,1)}) custom-call(s32[8]{0:T(128)} %copy-done.138, s32[1]{0:T(128)} %bitcast.9.core_ref, bf16[1040,256]{1,0:T(8,128)(2,1)} %copy-done.79, ...), custom_call_target="tpu_custom_call" | custom-call | flops 1073741824 | bytes 4194304 | tf_op jit(solution)/shard_map/norm_matmul/pallas_call | solution.py:174
  496.0 13.8 %hidden_back.2 = (bf16[1024,2048]{1,0:T(8,128)(2,1)}, bf16[1024,1024]{1,0:T(8,128)(2,1)}, f32[8,8,128]{2,1,0:T(8,128)}, f32[8,1024]{1,0:T(8,128)}) custom-call(s32[8]{0:T(128)} %copy-done.138, s32[1]{0:T(128)} %bitcast.9.core_ref, bf16[1024,256]{1,0:T(8,128)(2,1)} %copy-done.83, bf16[1024,256]{1,0:T(8,128)(2,1)} %collective-permute-done.11.refs_1_, ...), custom_call_target="tpu_custom_call" | custom-call | flops 1073741824 | bytes 4194304 | tf_op jit(solution)/shard_map/hidden_back/pallas_call | solution.py:258
  525.6 11.2 %collective-permute-done.66 = bf16[1040,256]{1,0:T(8,128)(2,1)S(1)} collective-permute-done((bf16[1040,256]{1,0:T(8,128)(2,1)S(1)}, bf16[1040,256]{1,0:T(8,128)(2,1)S(1)}, u32[]{:S(2)}, u32[]{:S(2)}) %collective-permute-start.66) | collective-permute-done | bytes 532512 | tf_op jit(solution)/shard_map/ppermute | solution.py:48
  538.6 6.3 convolution_convert_fusion.3
  546.1 6.3 collective-permute-start.67
  555.6 13.8 %collective-permute-done.63 = bf16[1040,256]{1,0:T(8,128)(2,1)S(1)} collective-permute-done((bf16[1040,256]{1,0:T(8,128)(2,1)}, bf16[1040,256]{1,0:T(8,128)(2,1)S(1)}, u32[]{:S(2)}, u32[]{:S(2)}) %collective-permute-start.63) | collective-permute-done | bytes 532512 | tf_op jit(solution)/shard_map/ppermute | solution.py:48
  570.9 20.4 %collective-permute-done.60 = f32[1024,256]{1,0:T(8,128)S(1)} collective-permute-done((f32[1024,256]{1,0:T(8,128)}, f32[1024,256]{1,0:T(8,128)S(1)}, u32[]{:S(2)}, u32[]{:S(2)}) %collective-permute-start.60) | collective-permute-done | bytes 1048608 | tf_op jit(solution)/shard_map/ppermute | solution.py:57
  593.5 6.2 convolution_convert_fusion.2
  601.3 14.1 %collective-permute-done.71.refs_4_ = bf16[1024,256]{1,0:T(8,128)(2,1)S(1)} collective-permute-done((bf16[1024,256]{1,0:T(8,128)(2,1)S(1)}, bf16[1024,256]{1,0:T(8,128)(2,1)S(1)}, u32[]{:S(2)}, u32[]{:S(2)}) %collective-permute-start.71) | collective-permute-done | bytes 524320 | tf_op jit(solution)/shard_map/ppermute | solution.py:48
  616.8 7.0 collective-permute-done.73.refs_6_
  626.7 7.5 gather_matmul.2
  636.5 8.8 attend_back.2.x_ref
  658.4 11.0 %collective-permute-done.80 = bf16[1040,256]{1,0:T(8,128)(2,1)S(1)} collective-permute-done((bf16[1040,256]{1,0:T(8,128)(2,1)S(1)}, bf16[1040,256]{1,0:T(8,128)(2,1)S(1)}, u32[]{:S(2)}, u32[]{:S(2)}) %collective-permute-start.80) | collective-permute-done | bytes 532512 | tf_op jit(solution)/shard_map/ppermute | solution.py:48
  687.0 16.1 %collective-permute-done.77 = bf16[1040,256]{1,0:T(8,128)(2,1)S(1)} collective-permute-done((bf16[1040,256]{1,0:T(8,128)(2,1)}, bf16[1040,256]{1,0:T(8,128)(2,1)S(1)}, u32[]{:S(2)}, u32[]{:S(2)}) %collective-permute-start.77) | collective-permute-done | bytes 532512 | tf_op jit(solution)/shard_map/ppermute | solution.py:48
  705.5 16.8 %collective-permute-done.82.refs_3_ = bf16[512,1024]{1,0:T(8,128)(2,1)} collective-permute-done((bf16[512,1024]{1,0:T(8,128)(2,1)}, bf16[512,1024]{1,0:T(8,128)(2,1)}, u32[]{:S(2)}, u32[]{:S(2)}) %collective-permute-start.82) | collective-permute-done | bytes 1048608 | tf_op jit(solution)/shard_map/ppermute | solution.py:708
  726.6 14.0 %collective-permute-done.86.refs_4_ = bf16[1024,256]{1,0:T(8,128)(2,1)S(1)} collective-permute-done((bf16[1024,256]{1,0:T(8,128)(2,1)S(1)}, bf16[1024,256]{1,0:T(8,128)(2,1)S(1)}, u32[]{:S(2)}, u32[]{:S(2)}) %collective-permute-start.86) | collective-permute-done | bytes 524320 | tf_op jit(solution)/shard_map/ppermute | solution.py:48
  745.0 6.5 collective-permute-done.88.refs_6_
  755.7 13.6 %hidden_back.3 = (bf16[1024,2048]{1,0:T(8,128)(2,1)}, bf16[1024,1024]{1,0:T(8,128)(2,1)}, f32[8,8,128]{2,1,0:T(8,128)}, f32[8,1024]{1,0:T(8,128)}) custom-call(s32[8]{0:T(128)} %copy-done.138, s32[1]{0:T(128)} %bitcast.9.core_ref, bf16[1024,256]{1,0:T(8,128)(2,1)} %copy-done.80, bf16[1024,256]{1,0:T(8,128)(2,1)} %copy-done.121, ...), custom_call_target="tpu_custom_call" | custom-call | flops 1073741824 | bytes 4194304 | tf_op jit(solution)/shard_map/hidden_back/pallas_call | solution.py:258
  784.8 11.0 %collective-permute-done.99 = bf16[1040,256]{1,0:T(8,128)(2,1)S(1)} collective-permute-done((bf16[1040,256]{1,0:T(8,128)(2,1)S(1)}, bf16[1040,256]{1,0:T(8,128)(2,1)S(1)}, u32[]{:S(2)}, u32[]{:S(2)}) %collective-permute-start.99) | collective-permute-done | bytes 532512 | tf_op jit(solution)/shard_map/ppermute | solution.py:48
  797.7 6.3 convolution_convert_fusion.1
  823.8 14.4 %collective-permute-done.98 = bf16[1040,256]{1,0:T(8,128)(2,1)S(1)} collective-permute-done((bf16[1040,256]{1,0:T(8,128)(2,1)S(1)}, bf16[1040,256]{1,0:T(8,128)(2,1)S(1)}, u32[]{:S(2)}, u32[]{:S(2)}) %collective-permute-start.98) | collective-permute-done | bytes 532512 | tf_op jit(solution)/shard_map/ppermute | solution.py:48
  838.2 6.4 collective-permute-done.100
  849.5 9.5 convolution_convert_fusion
  861.6 23.6 %collective-permute-done.105.refs_4_ = bf16[1024,256]{1,0:T(8,128)(2,1)S(1)} collective-permute-done((bf16[1024,256]{1,0:T(8,128)(2,1)S(1)}, bf16[1024,256]{1,0:T(8,128)(2,1)S(1)}, u32[]{:S(2)}, u32[]{:S(2)}) %collective-permute-start.105) | collective-permute-done | bytes 524320 | tf_op jit(solution)/shard_map/ppermute | solution.py:48
  886.3 12.0 %collective-permute-done.107.refs_6_ = bf16[1024,256]{1,0:T(8,128)(2,1)S(1)} collective-permute-done((bf16[1024,256]{1,0:T(8,128)(2,1)S(1)}, bf16[1024,256]{1,0:T(8,128)(2,1)S(1)}, u32[]{:S(2)}, u32[]{:S(2)}) %collective-permute-start.107) | collective-permute-done | bytes 524320 | tf_op jit(solution)/shard_map/ppermute | solution.py:48
  901.3 7.0 gather_matmul.3
  910.6 8.8 attend_back.3.x_ref
  945.0 19.2 %collective-permute-done.113 = f32[1024,256]{1,0:T(8,128)S(1)} collective-permute-done((f32[1024,256]{1,0:T(8,128)}, f32[1024,256]{1,0:T(8,128)S(1)}, u32[]{:S(2)}, u32[]{:S(2)}) %collective-permute-start.113) | collective-permute-done | bytes 1048608 | tf_op jit(solution)/shard_map/ppermute | solution.py:57
  968.6 11.4 %collective-permute-done.114.refs_3_ = bf16[512,1024]{1,0:T(8,128)(2,1)S(1)} collective-permute-done((bf16[512,1024]{1,0:T(8,128)(2,1)}, bf16[512,1024]{1,0:T(8,128)(2,1)S(1)}, u32[]{:S(2)}, u32[]{:S(2)}) %collective-permute-start.114) | collective-permute-done | bytes 1048608 | tf_op jit(solution)/shard_map/ppermute | solution.py:708
  1004.0 6.6 collective-permute-done.120
  1015.6 5.9 collective-permute-start.122
  1024.0 5.9 collective-permute-done.117
  1029.8 7.7 collective-permute-done.121
  1045.1 5.7 collective-permute-start.123
  1073.3 7.1 collective-permute-done.127.refs_1_
  (786 shorter events, 383.1 us)
Async XLA Ops:
  7.2 114.5 %all-gather.7.cloned.1.call-start = ((), (), s32[]{:S(2)}) async-start(), calls=%async_computation.6 | async-start | bytes 9437184 | tf_op jit(solution)/shard_map/all_gather | solution.py:696
  33.2 198.1 %all-gather.9.cloned.1.call-start = ((), (), s32[]{:S(2)}) async-start(), calls=%async_computation.7 | async-start | bytes 9437184 | tf_op jit(solution)/shard_map/all_gather | solution.py:696
  33.9 219.3 %all-gather.11.cloned.1.call-start = ((), (), s32[]{:S(2)}) async-start(), calls=%async_computation.8 | async-start | bytes 9437184 | tf_op jit(solution)/shard_map/all_gather | solution.py:696
  34.6 323.0 %all-gather.13.cloned.1.call-start = ((), (), s32[]{:S(2)}) async-start(), calls=%async_computation.9 | async-start | bytes 9437184 | tf_op jit(solution)/shard_map/all_gather | solution.py:696
  37.2 435.2 %all-gather.15.cloned.1.call-start = ((), (), s32[]{:S(2)}) async-start(), calls=%async_computation.10 | async-start | bytes 9437184 | tf_op jit(solution)/shard_map/all_gather | solution.py:696
  40.5 453.3 %all-gather.17.cloned.1.call-start = ((), (), s32[]{:S(2)}) async-start(), calls=%async_computation.11 | async-start | bytes 9437184 | tf_op jit(solution)/shard_map/all_gather | solution.py:696
  48.5 22.8 %collective-permute-start.6 = (bf16[1120,256]{1,0:T(8,128)(2,1)S(1)}, bf16[1120,256]{1,0:T(8,128)(2,1)S(1)}, u32[]{:S(2)}, u32[]{:S(2)}) collective-permute-start(bf16[1120,256]{1,0:T(8,128)(2,1)S(1)} %copy-done.76), channel_id=1, source_target_pairs={{0,4},{2,6},{4,0},{6,2},{1,5},{3,7},{5,1},{7,3},{8,12},{10,14},{12... | collective-permute-start | bytes 1720328 | tf_op jit(solution)/shard_map/ppermute | solution.py:48
  50.9 22.0 %collective-permute-start.4 = (bf16[1120,256]{1,0:T(8,128)(2,1)S(1)}, bf16[1120,256]{1,0:T(8,128)(2,1)S(1)}, u32[]{:S(2)}, u32[]{:S(2)}) collective-permute-start(bf16[1120,256]{1,0:T(8,128)(2,1)S(1)} %copy-done.76), channel_id=1, source_target_pairs={{0,2},{2,0},{4,6},{6,4},{1,3},{3,1},{5,7},{7,5},{8,10},{10,8},{12,... | collective-permute-start | bytes 1720328 | tf_op jit(solution)/shard_map/ppermute | solution.py:48
  52.2 20.7 %collective-permute-start.3 = (bf16[1120,256]{1,0:T(8,128)(2,1)S(1)}, bf16[1120,256]{1,0:T(8,128)(2,1)S(1)}, u32[]{:S(2)}, u32[]{:S(2)}) collective-permute-start(bf16[1120,256]{1,0:T(8,128)(2,1)S(1)} %copy-done.76), channel_id=1, source_target_pairs={{0,8},{8,0},{1,9},{9,1},{2,10},{10,2},{3,11},{11,3},{4,12},{12,4},... | collective-permute-start | bytes 1720328 | tf_op jit(solution)/shard_map/ppermute | solution.py:52
  52.2 33.0 %collective-permute-start.1 = (f32[1024,256]{1,0:T(8,128)S(1)}, f32[1024,256]{1,0:T(8,128)S(1)}, u32[]{:S(2)}, u32[]{:S(2)}) collective-permute-start(f32[1024,256]{1,0:T(8,128)S(1)} %copy-done.66), channel_id=1, source_target_pairs={{1,8},{8,1},{3,10},{10,3},{5,12},{12,5},{7,14},{14,7},{17,24},{24,... | collective-permute-start | bytes 3145736 | tf_op jit(solution)/shard_map/ppermute | solution.py:57
  71.3 20.8 %collective-permute-start.8 = (bf16[1120,256]{1,0:T(8,128)(2,1)S(1)}, bf16[1120,256]{1,0:T(8,128)(2,1)S(1)}, u32[]{:S(2)}, u32[]{:S(2)}) collective-permute-start(bf16[1120,256]{1,0:T(8,128)(2,1)S(1)} %collective-permute-done.6.refs_4_), channel_id=1, source_target_pairs={{0,2},{2,0},{4,6},{6,4},{1,3},{3,1},{5,7},{7,5},{8,10},{10,8},{12,... | collective-permute-start | bytes 1720328 | tf_op jit(solution)/shard_map/ppermute | solution.py:48
  72.4 20.0 %collective-permute-start.7 = (bf16[1120,256]{1,0:T(8,128)(2,1)S(1)}, bf16[1120,256]{1,0:T(8,128)(2,1)S(1)}, u32[]{:S(2)}, u32[]{:S(2)}) collective-permute-start(bf16[1120,256]{1,0:T(8,128)(2,1)S(1)} %collective-permute-done.6.refs_4_), channel_id=1, source_target_pairs={{0,8},{8,0},{1,9},{9,1},{2,10},{10,2},{3,11},{11,3},{4,12},{12,4},... | collective-permute-start | bytes 1720328 | tf_op jit(solution)/shard_map/ppermute | solution.py:52
  86.3 19.0 %collective-permute-start.14 = (bf16[1024,256]{1,0:T(8,128)(2,1)S(1)}, bf16[1024,256]{1,0:T(8,128)(2,1)}, u32[]{:S(2)}, u32[]{:S(2)}) collective-permute-start(bf16[1024,256]{1,0:T(8,128)(2,1)S(1)} %broadcast_select_fusion.5.refs_0_), channel_id=1, source_target_pairs={{0,4},{2,6},{4,0},{6,2},{1,5},{3,7},{5,1},{7,3},{8,12},{10,14},{12... | collective-permute-start | bytes 1572872 | tf_op jit(solution)/shard_map/ppermute | solution.py:48
  88.5 23.1 %collective-permute-start.12 = (bf16[1024,256]{1,0:T(8,128)(2,1)S(1)}, bf16[1024,256]{1,0:T(8,128)(2,1)}, u32[]{:S(2)}, u32[]{:S(2)}) collective-permute-start(bf16[1024,256]{1,0:T(8,128)(2,1)S(1)} %broadcast_select_fusion.5.refs_0_), channel_id=1, source_target_pairs={{0,2},{2,0},{4,6},{6,4},{1,3},{3,1},{5,7},{7,5},{8,10},{10,8},{12,... | collective-permute-start | bytes 1572872 | tf_op jit(solution)/shard_map/ppermute | solution.py:48
  89.7 46.9 %collective-permute-start.11 = (bf16[1024,256]{1,0:T(8,128)(2,1)S(1)}, bf16[1024,256]{1,0:T(8,128)(2,1)}, u32[]{:S(2)}, u32[]{:S(2)}) collective-permute-start(bf16[1024,256]{1,0:T(8,128)(2,1)S(1)} %broadcast_select_fusion.5.refs_0_), channel_id=1, source_target_pairs={{0,8},{8,0},{1,9},{9,1},{2,10},{10,2},{3,11},{11,3},{4,12},{12,4},... | collective-permute-start | bytes 1572872 | tf_op jit(solution)/shard_map/ppermute | solution.py:52
  92.2 19.4 %collective-permute-start.9 = (bf16[1120,256]{1,0:T(8,128)(2,1)S(1)}, bf16[1120,256]{1,0:T(8,128)(2,1)S(1)}, u32[]{:S(2)}, u32[]{:S(2)}) collective-permute-start(bf16[1120,256]{1,0:T(8,128)(2,1)S(1)} %collective-permute-done.8.refs_6_), channel_id=1, source_target_pairs={{0,8},{8,0},{1,9},{9,1},{2,10},{10,2},{3,11},{11,3},{4,12},{12,4},... | collective-permute-start | bytes 1720328 | tf_op jit(solution)/shard_map/ppermute | solution.py:52
  105.3 31.3 %collective-permute-start.15 = (bf16[1024,256]{1,0:T(8,128)(2,1)}, bf16[1024,256]{1,0:T(8,128)(2,1)}, u32[]{:S(2)}, u32[]{:S(2)}) collective-permute-start(bf16[1024,256]{1,0:T(8,128)(2,1)} %collective-permute-done.14.refs_4_), channel_id=1, source_target_pairs={{0,8},{8,0},{1,9},{9,1},{2,10},{10,2},{3,11},{11,3},{4,12},{12,4},... | collective-permute-start | bytes 1572872 | tf_op jit(solution)/shard_map/ppermute | solution.py:52
  111.6 25.0 %collective-permute-start.13 = (bf16[1024,256]{1,0:T(8,128)(2,1)}, bf16[1024,256]{1,0:T(8,128)(2,1)}, u32[]{:S(2)}, u32[]{:S(2)}) collective-permute-start(bf16[1024,256]{1,0:T(8,128)(2,1)} %collective-permute-done.12.refs_2_), channel_id=1, source_target_pairs={{0,8},{8,0},{1,9},{9,1},{2,10},{10,2},{3,11},{11,3},{4,12},{12,4},... | collective-permute-start | bytes 1572872 | tf_op jit(solution)/shard_map/ppermute | solution.py:52
  156.1 32.9 %collective-permute-start.20 = (bf16[1040,256]{1,0:T(8,128)(2,1)S(1)}, bf16[1040,256]{1,0:T(8,128)(2,1)S(1)}, u32[]{:S(2)}, u32[]{:S(2)}) collective-permute-start(bf16[1040,256]{1,0:T(8,128)(2,1)S(1)} %add_convert_fusion.31), channel_id=1, source_target_pairs={{0,2},{2,0},{4,6},{6,4},{1,3},{3,1},{5,7},{7,5},{8,10},{10,8},{12,... | collective-permute-start | bytes 1597448 | tf_op jit(solution)/shard_map/ppermute | solution.py:48
  167.6 21.6 %collective-permute-start.24 = (bf16[1040,256]{1,0:T(8,128)(2,1)S(1)}, bf16[1040,256]{1,0:T(8,128)(2,1)S(1)}, u32[]{:S(2)}, u32[]{:S(2)}) collective-permute-start(bf16[1040,256]{1,0:T(8,128)(2,1)S(1)} %add_convert_fusion.28), channel_id=1, source_target_pairs={{0,4},{2,6},{4,0},{6,2},{1,5},{3,7},{5,1},{7,3},{8,12},{10,14},{12... | collective-permute-start | bytes 1597448 | tf_op jit(solution)/shard_map/ppermute | solution.py:48
  193.7 25.4 %collective-permute-start.26 = (bf16[1040,256]{1,0:T(8,128)(2,1)S(1)}, bf16[1040,256]{1,0:T(8,128)(2,1)S(1)}, u32[]{:S(2)}, u32[]{:S(2)}) collective-permute-start(bf16[1040,256]{1,0:T(8,128)(2,1)S(1)} %fusion.23.refs_0_), channel_id=1, source_target_pairs={{0,2},{2,0},{4,6},{6,4},{1,3},{3,1},{5,7},{7,5},{8,10},{10,8},{12,... | collective-permute-start | bytes 1597448 | tf_op jit(solution)/shard_map/ppermute | solution.py:48
  207.9 18.2 %collective-permute-start.30 = (bf16[1040,256]{1,0:T(8,128)(2,1)S(1)}, bf16[1040,256]{1,0:T(8,128)(2,1)}, u32[]{:S(2)}, u32[]{:S(2)}) collective-permute-start(bf16[1040,256]{1,0:T(8,128)(2,1)S(1)} %collective-permute-done.28.refs_4_), channel_id=1, source_target_pairs={{0,2},{2,0},{4,6},{6,4},{1,3},{3,1},{5,7},{7,5},{8,10},{10,8},{12,... | collective-permute-start | bytes 1597448 | tf_op jit(solution)/shard_map/ppermute | solution.py:48
  267.6 359.0 %reduce-scatter.7.cloned.1.call-start = ((), (), s32[]{:S(2)}) async-start(), calls=%async_computation.12 | async-start | bytes 5242880 | tf_op jit(solution)/shard_map/reduce_scatter | solution.py:704
  270.8 19.8 %collective-permute-start.32 = (bf16[1040,256]{1,0:T(8,128)(2,1)S(1)}, bf16[1040,256]{1,0:T(8,128)(2,1)S(1)}, u32[]{:S(2)}, u32[]{:S(2)}) collective-permute-start(bf16[1040,256]{1,0:T(8,128)(2,1)S(1)} %get-tuple-element.269), channel_id=1, source_target_pairs={{0,8},{8,0},{1,9},{9,1},{2,10},{10,2},{3,11},{11,3},{4,12},{12,4},... | collective-permute-start | bytes 1597448 | tf_op jit(solution)/shard_map/ppermute | solution.py:52
  271.4 33.5 %collective-permute-start.34 = (bf16[1040,256]{1,0:T(8,128)(2,1)S(1)}, bf16[1040,256]{1,0:T(8,128)(2,1)S(1)}, u32[]{:S(2)}, u32[]{:S(2)}) collective-permute-start(bf16[1040,256]{1,0:T(8,128)(2,1)S(1)} %add_convert_fusion.27), channel_id=1, source_target_pairs={{0,2},{2,0},{4,6},{6,4},{1,3},{3,1},{5,7},{7,5},{8,10},{10,8},{12,... | collective-permute-start | bytes 1597448 | tf_op jit(solution)/shard_map/ppermute | solution.py:48
  283.5 21.5 %collective-permute-start.38 = (bf16[1040,256]{1,0:T(8,128)(2,1)S(1)}, bf16[1040,256]{1,0:T(8,128)(2,1)S(1)}, u32[]{:S(2)}, u32[]{:S(2)}) collective-permute-start(bf16[1040,256]{1,0:T(8,128)(2,1)S(1)} %add_convert_fusion.24), channel_id=1, source_target_pairs={{0,4},{2,6},{4,0},{6,2},{1,5},{3,7},{5,1},{7,3},{8,12},{10,14},{12... | collective-permute-start | bytes 1597448 | tf_op jit(solution)/shard_map/ppermute | solution.py:48
  309.5 37.8 %collective-permute-start.40 = (bf16[1040,256]{1,0:T(8,128)(2,1)S(1)}, bf16[1040,256]{1,0:T(8,128)(2,1)S(1)}, u32[]{:S(2)}, u32[]{:S(2)}) collective-permute-start(bf16[1040,256]{1,0:T(8,128)(2,1)S(1)} %fusion.24.refs_0_), channel_id=1, source_target_pairs={{0,2},{2,0},{4,6},{6,4},{1,3},{3,1},{5,7},{7,5},{8,10},{10,8},{12,... | collective-permute-start | bytes 1597448 | tf_op jit(solution)/shard_map/ppermute | solution.py:48
  323.5 24.3 %collective-permute-start.44 = (bf16[1040,256]{1,0:T(8,128)(2,1)S(1)}, bf16[1040,256]{1,0:T(8,128)(2,1)S(1)}, u32[]{:S(2)}, u32[]{:S(2)}) collective-permute-start(bf16[1040,256]{1,0:T(8,128)(2,1)S(1)} %collective-permute-done.42.refs_4_), channel_id=1, source_target_pairs={{0,2},{2,0},{4,6},{6,4},{1,3},{3,1},{5,7},{7,5},{8,10},{10,8},{12,... | collective-permute-start | bytes 1597448 | tf_op jit(solution)/shard_map/ppermute | solution.py:48
  333.1 21.5 %collective-permute-start.39 = (bf16[1040,256]{1,0:T(8,128)(2,1)S(1)}, bf16[1040,256]{1,0:T(8,128)(2,1)S(1)}, u32[]{:S(2)}, u32[]{:S(2)}) collective-permute-start(bf16[1040,256]{1,0:T(8,128)(2,1)S(1)} %fusion.24.refs_0_), channel_id=1, source_target_pairs={{0,8},{8,0},{1,9},{9,1},{2,10},{10,2},{3,11},{11,3},{4,12},{12,4},... | collective-permute-start | bytes 1597448 | tf_op jit(solution)/shard_map/ppermute | solution.py:52
  390.7 18.3 %collective-permute-start.46 = (bf16[1040,256]{1,0:T(8,128)(2,1)S(1)}, bf16[1040,256]{1,0:T(8,128)(2,1)S(1)}, u32[]{:S(2)}, u32[]{:S(2)}) collective-permute-start(bf16[1040,256]{1,0:T(8,128)(2,1)S(1)} %get-tuple-element.287), channel_id=1, source_target_pairs={{0,8},{8,0},{1,9},{9,1},{2,10},{10,2},{3,11},{11,3},{4,12},{12,4},... | collective-permute-start | bytes 1597448 | tf_op jit(solution)/shard_map/ppermute | solution.py:52
  391.5 32.8 %collective-permute-start.48 = (bf16[1040,256]{1,0:T(8,128)(2,1)S(1)}, bf16[1040,256]{1,0:T(8,128)(2,1)S(1)}, u32[]{:S(2)}, u32[]{:S(2)}) collective-permute-start(bf16[1040,256]{1,0:T(8,128)(2,1)S(1)} %add_convert_fusion.23), channel_id=1, source_target_pairs={{0,2},{2,0},{4,6},{6,4},{1,3},{3,1},{5,7},{7,5},{8,10},{10,8},{12,... | collective-permute-start | bytes 1597448 | tf_op jit(solution)/shard_map/ppermute | solution.py:48
  403.1 21.6 %collective-permute-start.52 = (bf16[1040,256]{1,0:T(8,128)(2,1)S(1)}, bf16[1040,256]{1,0:T(8,128)(2,1)S(1)}, u32[]{:S(2)}, u32[]{:S(2)}) collective-permute-start(bf16[1040,256]{1,0:T(8,128)(2,1)S(1)} %add_convert_fusion.20), channel_id=1, source_target_pairs={{0,4},{2,6},{4,0},{6,2},{1,5},{3,7},{5,1},{7,3},{8,12},{10,14},{12... | collective-permute-start | bytes 1597448 | tf_op jit(solution)/shard_map/ppermute | solution.py:48
  429.1 35.4 %collective-permute-start.54 = (bf16[1040,256]{1,0:T(8,128)(2,1)S(1)}, bf16[1040,256]{1,0:T(8,128)(2,1)S(1)}, u32[]{:S(2)}, u32[]{:S(2)}) collective-permute-start(bf16[1040,256]{1,0:T(8,128)(2,1)S(1)} %fusion.25.refs_0_), channel_id=1, source_target_pairs={{0,2},{2,0},{4,6},{6,4},{1,3},{3,1},{5,7},{7,5},{8,10},{10,8},{12,... | collective-permute-start | bytes 1597448 | tf_op jit(solution)/shard_map/ppermute | solution.py:48
  441.3 23.7 %collective-permute-start.58 = (bf16[1040,256]{1,0:T(8,128)(2,1)S(1)}, bf16[1040,256]{1,0:T(8,128)(2,1)S(1)}, u32[]{:S(2)}, u32[]{:S(2)}) collective-permute-start(bf16[1040,256]{1,0:T(8,128)(2,1)S(1)} %collective-permute-done.56.refs_4_), channel_id=1, source_target_pairs={{0,2},{2,0},{4,6},{6,4},{1,3},{3,1},{5,7},{7,5},{8,10},{10,8},{12,... | collective-permute-start | bytes 1597448 | tf_op jit(solution)/shard_map/ppermute | solution.py:48
  450.7 21.8 %collective-permute-start.53 = (bf16[1040,256]{1,0:T(8,128)(2,1)S(1)}, bf16[1040,256]{1,0:T(8,128)(2,1)}, u32[]{:S(2)}, u32[]{:S(2)}) collective-permute-start(bf16[1040,256]{1,0:T(8,128)(2,1)S(1)} %fusion.25.refs_0_), channel_id=1, source_target_pairs={{0,8},{8,0},{1,9},{9,1},{2,10},{10,2},{3,11},{11,3},{4,12},{12,4},... | collective-permute-start | bytes 1597448 | tf_op jit(solution)/shard_map/ppermute | solution.py:52
  544.8 160.6 %reduce-scatter.9.cloned.1.call-start = ((), (), s32[]{:S(2)}) async-start(), calls=%async_computation.13 | async-start | bytes 5242880 | tf_op jit(solution)/shard_map/reduce_scatter | solution.py:704
  544.9 24.5 %collective-permute-start.63 = (bf16[1040,256]{1,0:T(8,128)(2,1)}, bf16[1040,256]{1,0:T(8,128)(2,1)S(1)}, u32[]{:S(2)}, u32[]{:S(2)}) collective-permute-start(bf16[1040,256]{1,0:T(8,128)(2,1)} %add_convert_fusion.19), channel_id=1, source_target_pairs={{0,2},{2,0},{4,6},{6,4},{1,3},{3,1},{5,7},{7,5},{8,10},{10,8},{12,... | collective-permute-start | bytes 1597448 | tf_op jit(solution)/shard_map/ppermute | solution.py:48
  546.1 23.3 %collective-permute-start.67 = (bf16[1040,256]{1,0:T(8,128)(2,1)}, bf16[1040,256]{1,0:T(8,128)(2,1)S(1)}, u32[]{:S(2)}, u32[]{:S(2)}) collective-permute-start(bf16[1040,256]{1,0:T(8,128)(2,1)} %add_convert_fusion.16), channel_id=1, source_target_pairs={{0,4},{2,6},{4,0},{6,2},{1,5},{3,7},{5,1},{7,3},{8,12},{10,14},{12... | collective-permute-start | bytes 1597448 | tf_op jit(solution)/shard_map/ppermute | solution.py:48
  552.4 38.9 %collective-permute-start.60 = (f32[1024,256]{1,0:T(8,128)}, f32[1024,256]{1,0:T(8,128)S(1)}, u32[]{:S(2)}, u32[]{:S(2)}) collective-permute-start(f32[1024,256]{1,0:T(8,128)} %get-tuple-element.304), channel_id=1, source_target_pairs={{1,8},{8,1},{3,10},{10,3},{5,12},{12,5},{7,14},{14,7},{17,24},{24,... | collective-permute-start | bytes 3145736 | tf_op jit(solution)/shard_map/ppermute | solution.py:57
  599.7 247.1 %reduce-scatter.11.cloned.1.call-start = ((), (), s32[]{:S(2)}) async-start(), calls=%async_computation.14 | async-start | bytes 5242880 | tf_op jit(solution)/shard_map/reduce_scatter | solution.py:704
  678.9 222.4 %reduce-scatter.13.cloned.1.call-start = ((), (), s32[]{:S(2)}) async-start(), calls=%async_computation.15 | async-start | bytes 5242880 | tf_op jit(solution)/shard_map/reduce_scatter | solution.py:704
  679.0 24.2 %collective-permute-start.77 = (bf16[1040,256]{1,0:T(8,128)(2,1)}, bf16[1040,256]{1,0:T(8,128)(2,1)S(1)}, u32[]{:S(2)}, u32[]{:S(2)}) collective-permute-start(bf16[1040,256]{1,0:T(8,128)(2,1)} %add_convert_fusion.15), channel_id=1, source_target_pairs={{0,2},{2,0},{4,6},{6,4},{1,3},{3,1},{5,7},{7,5},{8,10},{10,8},{12,... | collective-permute-start | bytes 1597448 | tf_op jit(solution)/shard_map/ppermute | solution.py:48
  679.8 23.3 %collective-permute-start.81 = (bf16[1040,256]{1,0:T(8,128)(2,1)}, bf16[1040,256]{1,0:T(8,128)(2,1)S(1)}, u32[]{:S(2)}, u32[]{:S(2)}) collective-permute-start(bf16[1040,256]{1,0:T(8,128)(2,1)} %add_convert_fusion.12), channel_id=1, source_target_pairs={{0,4},{2,6},{4,0},{6,2},{1,5},{3,7},{5,1},{7,3},{8,12},{10,14},{12... | collective-permute-start | bytes 1597448 | tf_op jit(solution)/shard_map/ppermute | solution.py:48
  683.4 39.0 %collective-permute-start.82 = (bf16[512,1024]{1,0:T(8,128)(2,1)}, bf16[512,1024]{1,0:T(8,128)(2,1)}, u32[]{:S(2)}, u32[]{:S(2)}) collective-permute-start(bf16[512,1024]{1,0:T(8,128)(2,1)} %reduce-scatter.7.cloned.1.call-done.refs_2_), channel_id=1, source_target_pairs={{1,8},{8,1},{3,10},{10,3},{5,12},{12,5},{7,14},{14,7},{17,24},{24,... | collective-permute-start | bytes 3145736 | tf_op jit(solution)/shard_map/ppermute | solution.py:708
  726.5 18.5 %collective-permute-start.84 = (bf16[1024,256]{1,0:T(8,128)(2,1)S(1)}, bf16[1024,256]{1,0:T(8,128)(2,1)S(1)}, u32[]{:S(2)}, u32[]{:S(2)}) collective-permute-start(bf16[1024,256]{1,0:T(8,128)(2,1)S(1)} %convert_element_type.839.refs_0_), channel_id=1, source_target_pairs={{0,2},{2,0},{4,6},{6,4},{1,3},{3,1},{5,7},{7,5},{8,10},{10,8},{12,... | collective-permute-start | bytes 1572872 | tf_op jit(solution)/shard_map/ppermute | solution.py:48
  804.0 246.8 %reduce-scatter.17.cloned.1.call-start = ((), (), s32[]{:S(2)}) async-start(), calls=%async_computation.17 | async-start | bytes 5242880 | tf_op jit(solution)/shard_map/reduce_scatter | solution.py:704
  814.2 31.7 %collective-permute-start.101 = (bf16[512,1024]{1,0:T(8,128)(2,1)S(1)}, bf16[512,1024]{1,0:T(8,128)(2,1)S(1)}, u32[]{:S(2)}, u32[]{:S(2)}) collective-permute-start(bf16[512,1024]{1,0:T(8,128)(2,1)S(1)} %copy-done.33), channel_id=1, source_target_pairs={{1,8},{8,1},{3,10},{10,3},{5,12},{12,5},{7,14},{14,7},{17,24},{24,... | collective-permute-start | bytes 3145736 | tf_op jit(solution)/shard_map/ppermute | solution.py:708
  816.1 22.1 %collective-permute-start.98 = (bf16[1040,256]{1,0:T(8,128)(2,1)S(1)}, bf16[1040,256]{1,0:T(8,128)(2,1)S(1)}, u32[]{:S(2)}, u32[]{:S(2)}) collective-permute-start(bf16[1040,256]{1,0:T(8,128)(2,1)S(1)} %copy-done.112), channel_id=1, source_target_pairs={{0,2},{2,0},{4,6},{6,4},{1,3},{3,1},{5,7},{7,5},{8,10},{10,8},{12,... | collective-permute-start | bytes 1597448 | tf_op jit(solution)/shard_map/ppermute | solution.py:48
  818.2 26.4 %collective-permute-start.100 = (bf16[1040,256]{1,0:T(8,128)(2,1)S(1)}, bf16[1040,256]{1,0:T(8,128)(2,1)S(1)}, u32[]{:S(2)}, u32[]{:S(2)}) collective-permute-start(bf16[1040,256]{1,0:T(8,128)(2,1)S(1)} %copy-done.113), channel_id=1, source_target_pairs={{0,4},{2,6},{4,0},{6,2},{1,5},{3,7},{5,1},{7,3},{8,12},{10,14},{12... | collective-permute-start | bytes 1597448 | tf_op jit(solution)/shard_map/ppermute | solution.py:48
  859.0 193.8 %reduce-scatter.15.cloned.1.call-start = ((), (), s32[]{:S(2)}) async-start(), calls=%async_computation.16 | async-start | bytes 5242880 | tf_op jit(solution)/shard_map/reduce_scatter | solution.py:704
  859.3 25.9 %collective-permute-start.105 = (bf16[1024,256]{1,0:T(8,128)(2,1)S(1)}, bf16[1024,256]{1,0:T(8,128)(2,1)S(1)}, u32[]{:S(2)}, u32[]{:S(2)}) collective-permute-start(bf16[1024,256]{1,0:T(8,128)(2,1)S(1)} %convert_element_type.868.refs_0_), channel_id=1, source_target_pairs={{0,4},{2,6},{4,0},{6,2},{1,5},{3,7},{5,1},{7,3},{8,12},{10,14},{12... | collective-permute-start | bytes 1572872 | tf_op jit(solution)/shard_map/ppermute | solution.py:48
  860.4 25.4 %collective-permute-start.103 = (bf16[1024,256]{1,0:T(8,128)(2,1)S(1)}, bf16[1024,256]{1,0:T(8,128)(2,1)S(1)}, u32[]{:S(2)}, u32[]{:S(2)}) collective-permute-start(bf16[1024,256]{1,0:T(8,128)(2,1)S(1)} %convert_element_type.868.refs_0_), channel_id=1, source_target_pairs={{0,2},{2,0},{4,6},{6,4},{1,3},{3,1},{5,7},{7,5},{8,10},{10,8},{12,... | collective-permute-start | bytes 1572872 | tf_op jit(solution)/shard_map/ppermute | solution.py:48
  928.3 35.9 %collective-permute-start.113 = (f32[1024,256]{1,0:T(8,128)}, f32[1024,256]{1,0:T(8,128)S(1)}, u32[]{:S(2)}, u32[]{:S(2)}) collective-permute-start(f32[1024,256]{1,0:T(8,128)} %copy-done.68), channel_id=1, source_target_pairs={{1,8},{8,1},{3,10},{10,3},{5,12},{12,5},{7,14},{14,7},{17,24},{24,... | collective-permute-start | bytes 3145736 | tf_op jit(solution)/shard_map/ppermute | solution.py:57
  932.7 47.3 %collective-permute-start.114 = (bf16[512,1024]{1,0:T(8,128)(2,1)}, bf16[512,1024]{1,0:T(8,128)(2,1)S(1)}, u32[]{:S(2)}, u32[]{:S(2)}) collective-permute-start(bf16[512,1024]{1,0:T(8,128)(2,1)} %reduce-scatter.11.cloned.1.call-done.refs_2_), channel_id=1, source_target_pairs={{1,8},{8,1},{3,10},{10,3},{5,12},{12,5},{7,14},{14,7},{17,24},{24,... | collective-permute-start | bytes 3145736 | tf_op jit(solution)/shard_map/ppermute | solution.py:708
  935.1 30.2 %collective-permute-start.109 = (bf16[1040,256]{1,0:T(8,128)(2,1)}, bf16[1040,256]{1,0:T(8,128)(2,1)S(1)}, u32[]{:S(2)}, u32[]{:S(2)}) collective-permute-start(bf16[1040,256]{1,0:T(8,128)(2,1)} %add_convert_fusion.8), channel_id=1, source_target_pairs={{0,2},{2,0},{4,6},{6,4},{1,3},{3,1},{5,7},{7,5},{8,10},{10,8},{12,... | collective-permute-start | bytes 1597448 | tf_op jit(solution)/shard_map/ppermute | solution.py:48
  943.1 24.3 %collective-permute-start.111 = (bf16[1040,256]{1,0:T(8,128)(2,1)S(1)}, bf16[1040,256]{1,0:T(8,128)(2,1)S(1)}, u32[]{:S(2)}, u32[]{:S(2)}) collective-permute-start(bf16[1040,256]{1,0:T(8,128)(2,1)S(1)} %add_convert_fusion.4), channel_id=1, source_target_pairs={{0,4},{2,6},{4,0},{6,2},{1,5},{3,7},{5,1},{7,3},{8,12},{10,14},{12... | collective-permute-start | bytes 1597448 | tf_op jit(solution)/shard_map/ppermute | solution.py:48
  998.0 23.5 %collective-permute-start.112 = (f32[1024,256]{1,0:T(8,128)}, f32[1024,256]{1,0:T(8,128)}, u32[]{:S(2)}, u32[]{:S(2)}) collective-permute-start(f32[1024,256]{1,0:T(8,128)} %fusion.11), channel_id=1, source_target_pairs={{1,8},{8,1},{3,10},{10,3},{5,12},{12,5},{7,14},{14,7},{17,24},{24,... | collective-permute-start | bytes 3145736 | tf_op jit(solution)/shard_map/ppermute | solution.py:57
  1001.6 22.4 %collective-permute-start.115 = (bf16[1040,256]{1,0:T(8,128)(2,1)S(1)}, bf16[1040,256]{1,0:T(8,128)(2,1)}, u32[]{:S(2)}, u32[]{:S(2)}) collective-permute-start(bf16[1040,256]{1,0:T(8,128)(2,1)S(1)} %copy-done.54), channel_id=1, source_target_pairs={{0,8},{8,0},{1,9},{9,1},{2,10},{10,2},{3,11},{11,3},{4,12},{12,4},... | collective-permute-start | bytes 1597448 | tf_op jit(solution)/shard_map/ppermute | solution.py:52
  1002.7 27.1 %collective-permute-start.117 = (bf16[1040,256]{1,0:T(8,128)(2,1)}, bf16[1040,256]{1,0:T(8,128)(2,1)}, u32[]{:S(2)}, u32[]{:S(2)}) collective-permute-start(bf16[1040,256]{1,0:T(8,128)(2,1)} %add_convert_fusion.3), channel_id=1, source_target_pairs={{0,2},{2,0},{4,6},{6,4},{1,3},{3,1},{5,7},{7,5},{8,10},{10,8},{12,... | collective-permute-start | bytes 1597448 | tf_op jit(solution)/shard_map/ppermute | solution.py:48
  1012.7 24.8 %collective-permute-start.121 = (bf16[1040,256]{1,0:T(8,128)(2,1)}, bf16[1040,256]{1,0:T(8,128)(2,1)}, u32[]{:S(2)}, u32[]{:S(2)}) collective-permute-start(bf16[1040,256]{1,0:T(8,128)(2,1)} %add_convert_fusion), channel_id=1, source_target_pairs={{0,4},{2,6},{4,0},{6,2},{1,5},{3,7},{5,1},{7,3},{8,12},{10,14},{12... | collective-permute-start | bytes 1597448 | tf_op jit(solution)/shard_map/ppermute | solution.py:48
  1015.6 23.7 %collective-permute-start.122 = (bf16[512,1024]{1,0:T(8,128)(2,1)S(1)}, bf16[512,1024]{1,0:T(8,128)(2,1)S(1)}, u32[]{:S(2)}, u32[]{:S(2)}) collective-permute-start(bf16[512,1024]{1,0:T(8,128)(2,1)S(1)} %copy-done.38), channel_id=1, source_target_pairs={{1,8},{8,1},{3,10},{10,3},{5,12},{12,5},{7,14},{14,7},{17,24},{24,... | collective-permute-start | bytes 3145736 | tf_op jit(solution)/shard_map/ppermute | solution.py:708
  1045.1 17.3 %collective-permute-start.123 = (bf16[1024,256]{1,0:T(8,128)(2,1)}, bf16[1024,256]{1,0:T(8,128)(2,1)}, u32[]{:S(2)}, u32[]{:S(2)}) collective-permute-start(bf16[1024,256]{1,0:T(8,128)(2,1)} %get-tuple-element.497), channel_id=1, source_target_pairs={{1,8},{8,1},{3,10},{10,3},{5,12},{12,5},{7,14},{14,7},{17,24},{24,... | collective-permute-start | bytes 1572872 | tf_op jit(solution)/shard_map/ppermute | solution.py:57
  1050.8 18.4 %collective-permute-start.128 = (bf16[512,1024]{1,0:T(8,128)(2,1)}, bf16[512,1024]{1,0:T(8,128)(2,1)}, u32[]{:S(2)}, u32[]{:S(2)}) collective-permute-start(bf16[512,1024]{1,0:T(8,128)(2,1)} %reduce-scatter.17.cloned.1.call-done.refs_0_), channel_id=1, source_target_pairs={{1,8},{8,1},{3,10},{10,3},{5,12},{12,5},{7,14},{14,7},{17,24},{24,... | collective-permute-start | bytes 3145736 | tf_op jit(solution)/shard_map/ppermute | solution.py:708
  1052.8 27.5 %collective-permute-start.127 = (bf16[512,1024]{1,0:T(8,128)(2,1)}, bf16[512,1024]{1,0:T(8,128)(2,1)S(1)}, u32[]{:S(2)}, u32[]{:S(2)}) collective-permute-start(bf16[512,1024]{1,0:T(8,128)(2,1)} %reduce-scatter.15.cloned.1.call-done.refs_0_), channel_id=1, source_target_pairs={{1,8},{8,1},{3,10},{10,3},{5,12},{12,5},{7,14},{14,7},{17,24},{24,... | collective-permute-start | bytes 3145736 | tf_op jit(solution)/shard_map/ppermute | solution.py:708
  (234 other events, 2177.7 us)
Sparse Core Ops, SparseCore 0:
  33.3 62.9 all-gather.6
  98.7 56.3 all-gather.8
  156.9 54.0 all-gather.10
  212.8 54.7 all-gather.12
  269.3 54.1 all-gather.14
  325.3 54.3 all-gather.16
  545.0 64.1 reduce-scatter.6
  612.4 52.6 reduce-scatter.8
  679.0 61.4 reduce-scatter.10
  804.1 61.4 reduce-scatter.12
  868.5 52.6 reduce-scatter.16
  928.3 62.8 reduce-scatter.14
